TPU v7x, 512 devices: a whole 4x8x8 slice. The times are simulated.
512 devices in a mesh: pp: 16 (over z, core), ep: 32 (over x, y).
Axes of the slice: x: 4, y: 8, z: 8, core: 2. Of those that a mesh axis runs over, the one named last changes fastest.
Arguments:
- tokens: bfloat16 [16, 4096, 3584], P('pp', 'ep'), may hold values from -6 to 6
- cotangent: bfloat16 [16, 4096, 3584], P('pp', 'ep'), may hold values from -6 to 6
- expert_slot: int32 [16, 4096], P('pp', 'ep'), may hold values from 0 to 2, as said below
- gate_fixed: int32 [16, 4096], P('pp', 'ep'), may hold values from 256 to 4095
- w_gate: bfloat16 [16, 2048, 3584], P('pp', 'ep')
- w_up: bfloat16 [16, 2048, 3584], P('pp', 'ep')
- w_down: bfloat16 [16, 2048, 3584], P('pp', 'ep')
Outputs:
- input_grad: bfloat16 [16, 4096, 3584], P('pp', 'ep')
- grad_gate: bfloat16 [16, 2048, 1792], P('pp', 'ep')
- grad_up: bfloat16 [16, 2048, 1792], P('pp', 'ep')
- grad_down: bfloat16 [16, 2048, 1792], P('pp', 'ep')
Inputs may be any that keep to these rules, and one draw needn't show every extreme that they name: `expert_slot`: 2 means the token uses none of the window's experts. In every block of 128 consecutive tokens of one device at most 16 tokens name one expert, and in each copy's microbatch one expert is named by exactly 16 tokens of every block. `gate_fixed`: the gate weight is this value divided by 4096.
All inputs are finite; a program needn't handle non-finite values.
Results may differ from a plain program's by a relative error of at most 0.0065.
Values may be sent and summed in bfloat16 or wider, within the bound.
No kernel may reach another device: no remote copies, remote signals or barrier semaphores. Data moves between devices by JAX's collectives and lax.ppermute only.
A program may use at most 128 MiB of HBM per device.

v0:
```python
import jax
import jax.numpy as jnp
from jax import lax
from jax.sharding import PartitionSpec as P

E_WIN = 2
CAP = 16


def swapped(x, axis, stride):
    return lax.ppermute(x, axis, [(i, i ^ 1 << stride) for i in range(lax.axis_size(axis))])


def slot_numbers(block_ids):
    onehot = (block_ids[:, None] == jnp.arange(E_WIN, dtype=jnp.int32)[None, :]).astype(jnp.int32)
    rank_in = jnp.sum(jnp.cumsum(onehot, axis=0) * onehot, axis=1) - 1
    return jnp.where(block_ids < E_WIN, block_ids * CAP + rank_in, -1)


def silu_grad(pre_value):
    sigmoid_value = jax.nn.sigmoid(pre_value)
    return sigmoid_value * (1.0 + pre_value * (1.0 - sigmoid_value))


def shards(tokens, cotangent, expert_slot, gate_fixed, w_gate, w_up, w_down):
    block_x = tokens[0]
    block_cot = cotangent[0]
    slot_ids = expert_slot[0]
    gate_ints = gate_fixed[0]
    slice_g = w_gate[0]
    slice_u = w_up[0]
    slice_d = w_down[0]
    width = block_x.shape[1]
    ep_count = lax.axis_size("ep")
    members = ep_count // E_WIN
    contract_rows = (((1,), (1,)), ((), ()))
    contract_first = (((0,), (0,)), ((), ()))
    gate_value = gate_ints.astype(jnp.float32) / 4096.0
    scaled = (gate_value[:, None] * block_cot.astype(jnp.float32)).astype(jnp.bfloat16)
    select = slot_numbers(slot_ids)[None, :] == jnp.arange(E_WIN * CAP, dtype=jnp.int32)[:, None]
    select_bf = select.astype(jnp.bfloat16)
    packed_x = (
        jnp.dot(select_bf, block_x, preferred_element_type=jnp.float32)
        .astype(jnp.bfloat16)
        .reshape(E_WIN, CAP, width)
    )
    packed_c = (
        jnp.dot(select_bf, scaled, preferred_element_type=jnp.float32)
        .astype(jnp.bfloat16)
        .reshape(E_WIN, CAP, width)
    )
    rows_x, rows_c = (
        lax.all_to_all(
            jnp.repeat(packed_x, members, axis=0), "ep", split_axis=0, concat_axis=0, tiled=True
        ),
        lax.all_to_all(
            jnp.repeat(packed_c, members, axis=0), "ep", split_axis=0, concat_axis=0, tiled=True
        ),
    )
    rows_x = rows_x.reshape(ep_count * CAP, width)
    rows_c = rows_c.reshape(ep_count * CAP, width)
    gate_pre = lax.dot_general(rows_x, slice_g, contract_rows, preferred_element_type=jnp.float32)
    up_pre = lax.dot_general(rows_x, slice_u, contract_rows, preferred_element_type=jnp.float32)
    activated = jax.nn.silu(gate_pre)
    hidden = (activated * up_pre).astype(jnp.bfloat16)
    hidden_cot = lax.dot_general(rows_c, slice_d, contract_rows, preferred_element_type=jnp.float32)
    grad_down = lax.dot_general(
        hidden, rows_c, contract_first, preferred_element_type=jnp.float32
    ).astype(jnp.bfloat16)
    pp_count = lax.axis_size("pp")
    half_width = width // 2
    pp_index = lax.axis_index("pp")
    upper_side = (pp_index >= pp_count // 2).astype(jnp.int32)
    keep_at = upper_side * half_width
    send_at = (1 - upper_side) * half_width
    levels = pp_count.bit_length() - 1
    gate_cot = (hidden_cot * up_pre * silu_grad(gate_pre)).astype(jnp.bfloat16)
    up_cot = (hidden_cot * activated).astype(jnp.bfloat16)
    partial_cot = jnp.dot(gate_cot, slice_g, preferred_element_type=jnp.float32)
    partial_cot = (
        partial_cot + jnp.dot(up_cot, slice_u, preferred_element_type=jnp.float32)
    ).astype(jnp.bfloat16)
    returned = lax.all_to_all(
        partial_cot.reshape(ep_count, CAP, width), "ep", split_axis=0, concat_axis=0, tiled=True
    )
    grad_gate = lax.dot_general(
        gate_cot, rows_x, contract_first, preferred_element_type=jnp.float32
    ).astype(jnp.bfloat16)
    grad_up = lax.dot_general(
        up_cot, rows_x, contract_first, preferred_element_type=jnp.float32
    ).astype(jnp.bfloat16)
    summed = jnp.sum(
        returned.astype(jnp.float32).reshape(E_WIN, members, CAP, width), axis=1
    ).reshape(E_WIN * CAP, width)
    branch = lax.dot_general(
        select.astype(jnp.float32), summed, contract_first, precision=lax.Precision.HIGHEST
    )
    input_grad = (block_cot.astype(jnp.float32) + branch).astype(jnp.bfloat16)[None]
    stacked = jnp.stack(
        [
            lax.dynamic_slice_in_dim(grad_gate, send_at, half_width, 1),
            lax.dynamic_slice_in_dim(grad_up, send_at, half_width, 1),
            lax.dynamic_slice_in_dim(grad_down, send_at, half_width, 1),
        ]
    )
    for bit_level in range(levels):
        stacked = swapped(stacked, "pp", bit_level)
    own_grads = (grad_gate, grad_up, grad_down)
    results = []
    for index_grad in range(3):
        kept = lax.dynamic_slice_in_dim(own_grads[index_grad], keep_at, half_width, 1)
        pair_total = (kept.astype(jnp.float32) + stacked[index_grad].astype(jnp.float32)).astype(
            jnp.bfloat16
        )
        results.append(pair_total[None])
    return (input_grad, results[0], results[1], results[2])


def solution(mesh):
    return jax.shard_map(
        shards,
        mesh=mesh,
        in_specs=(
            P("pp", "ep", None),
            P("pp", "ep", None),
            P("pp", "ep"),
            P("pp", "ep"),
            P("pp", "ep", None),
            P("pp", "ep", None),
            P("pp", "ep", None),
        ),
        out_specs=(
            P("pp", "ep", None),
            P("pp", "ep", None),
            P("pp", "ep", None),
            P("pp", "ep", None),
        ),
        check_vma=False,
    )
```

profile of v0, /device:TPU:1, one launch (start us, length us, event | category | flops | bytes accessed | tf_op | source)
XLA Modules:
  0.0 321.1 jit_solution(4679074994580080596)
XLA Ops:
  0.6 0.0 copy-start
  0.6 0.8 fusion.23
  1.5 0.2 reduce_window_sum.11
  1.6 0.8 select_reduce_fusion
  2.5 0.7 fusion.28
  3.1 0.0 copy-done
  3.1 0.2 convolution_convert_fusion.3
  3.4 2.2 broadcast_in_dim.25
  5.6 0.0 copy-start.4
  5.6 0.0 copy-start.1
  5.6 10.7 %all-to-all-start.1 = ((bf16[32,16,3584]{2,1,0:T(8,128)(2,1)}), bf16[32,16,3584]{2,1,0:T(8,128)(2,1)}, u32[]{:S(2)}, u32[]{:S(2)}) async-start(bf16[32,16,3584]{2,1,0:T(8,128)(2,1)} %bitcast.86), calls=%async_computation.1 | async-start | bytes 7340032 | tf_op jit(solution)/shard_map/all_to_all | solution.py:53
  16.4 0.0 copy-done.4
  16.4 0.0 copy-done.1
  16.4 0.3 convolution_convert_fusion.4
  16.8 81.2 %all-to-all-done.1 = bf16[32,16,3584]{2,1,0:T(8,128)(2,1)} async-done(((bf16[32,16,3584]{2,1,0:T(8,128)(2,1)}), bf16[32,16,3584]{2,1,0:T(8,128)(2,1)}, u32[]{:S(2)}, u32[]{:S(2)}) %all-to-all-start.1) | async-done | bytes 3670048 | tf_op jit(solution)/shard_map/all_to_all | solution.py:53
  97.9 2.2 broadcast_in_dim.24
  100.2 0.0 copy-start.2
  100.2 9.4 %all-to-all-start = ((bf16[32,16,3584]{2,1,0:T(8,128)(2,1)}), bf16[32,16,3584]{2,1,0:T(8,128)(2,1)}, u32[]{:S(2)}, u32[]{:S(2)}) async-start(bf16[32,16,3584]{2,1,0:T(8,128)(2,1)} %bitcast.87), calls=%async_computation | async-start | bytes 7340032 | tf_op jit(solution)/shard_map/all_to_all | solution.py:56
  109.6 0.0 copy-start.3
  109.6 0.0 copy-done.2
  109.6 3.3 %fusion.12 = f32[512,64]{0,1:T(8,128)S(1)} fusion(bf16[512,3584]{1,0:T(8,128)(2,1)} %bitcast.13, bf16[1,64,3584]{2,1,0:T(8,128)(2,1)S(1)} %copy-done.2), kind=kOutput, calls=%fused_computation.24 | convolution fusion | flops 234881024 | bytes 4259840 | tf_op jit(solution)/shard_map/dot_general | solution.py:62
  112.9 0.0 copy-done.3
  112.9 3.2 %fusion.15 = f32[512,64]{0,1:T(8,128)S(1)} fusion(bf16[512,3584]{1,0:T(8,128)(2,1)} %bitcast.13, bf16[1,64,3584]{2,1,0:T(8,128)(2,1)S(1)} %copy-done.3), kind=kOutput, calls=%fused_computation.27 | convolution fusion | flops 234881024 | bytes 4259840 | tf_op jit(solution)/shard_map/dot_general | solution.py:63
  116.1 74.9 %all-to-all-done = bf16[32,16,3584]{2,1,0:T(8,128)(2,1)} async-done(((bf16[32,16,3584]{2,1,0:T(8,128)(2,1)}), bf16[32,16,3584]{2,1,0:T(8,128)(2,1)}, u32[]{:S(2)}, u32[]{:S(2)}) %all-to-all-start) | async-done | bytes 3670048 | tf_op jit(solution)/shard_map/all_to_all | solution.py:56
  191.1 3.3 %multiply_convert_fusion.1 = (bf16[512,64]{0,1:T(8,128)(2,1)S(1)}, bf16[512,64]{0,1:T(8,128)(2,1)S(1)}) fusion(f32[512,64]{0,1:T(8,128)S(1)} %fusion.12, f32[512,64]{0,1:T(8,128)S(1)} %fusion.15, bf16[512,3584]{1,0:T(8,128)(2,1)} %bitcast.8, bf16[1,64,3584]{2,1,0:T(8,128)(2,1)} %param.13), kind=kOutput, calls=%fused_computation.41 | convolution fusion | flops 235307008 | bytes 4521984 | tf_op jit(solution)/shard_map/dot_general | solution.py:66
  194.4 1.1 fusion.10
  195.6 3.1 add_convert_fusion
  198.6 9.1 %all-to-all-start.2 = ((bf16[32,16,3584]{2,1,0:T(8,128)(2,1)}), bf16[32,16,3584]{2,1,0:T(8,128)(2,1)}, u32[]{:S(2)}, u32[]{:S(2)}) async-start(bf16[32,16,3584]{2,1,0:T(8,128)(2,1)} %bitcast.85), calls=%async_computation.2 | async-start | bytes 7340032 | tf_op jit(solution)/shard_map/all_to_all | solution.py:83
  207.8 2.8 convolution_convert_fusion
  210.6 2.8 convolution_convert_fusion.1
  213.4 2.8 convolution_convert_fusion.2
  216.2 0.1 pad_maximum_fusion
  216.3 2.8 collective-permute-start
  219.1 1.7 collective-permute-done
  220.9 4.4 %collective-permute-start.1 = (bf16[3,64,1792]{2,1,0:T(8,128)(2,1)S(1)}, bf16[3,64,1792]{2,1,0:T(8,128)(2,1)S(1)}, u32[]{:S(2)}, u32[]{:S(2)}) collective-permute-start(bf16[3,64,1792]{2,1,0:T(8,128)(2,1)S(1)} %collective-permute-done), channel_id=1, source_target_pairs={{0,64},{32,96},{64,0},{96,32},{128,192},{160,224},{192,128},{224,1... | collective-permute-start | bytes 2064392 | tf_op jit(solution)/shard_map/ppermute | solution.py:11
  225.2 15.6 %collective-permute-done.1 = bf16[3,64,1792]{2,1,0:T(8,128)(2,1)S(1)} collective-permute-done((bf16[3,64,1792]{2,1,0:T(8,128)(2,1)S(1)}, bf16[3,64,1792]{2,1,0:T(8,128)(2,1)S(1)}, u32[]{:S(2)}, u32[]{:S(2)}) %collective-permute-start.1) | collective-permute-done | bytes 688160 | tf_op jit(solution)/shard_map/ppermute | solution.py:11
  240.8 5.3 %collective-permute-start.2 = (bf16[3,64,1792]{2,1,0:T(8,128)(2,1)S(1)}, bf16[3,64,1792]{2,1,0:T(8,128)(2,1)}, u32[]{:S(2)}, u32[]{:S(2)}) collective-permute-start(bf16[3,64,1792]{2,1,0:T(8,128)(2,1)S(1)} %collective-permute-done.1), channel_id=1, source_target_pairs={{0,128},{32,160},{64,192},{96,224},{128,0},{160,32},{192,64},{224,... | collective-permute-start | bytes 2064392 | tf_op jit(solution)/shard_map/ppermute | solution.py:11
  246.1 29.8 %collective-permute-done.2 = bf16[3,64,1792]{2,1,0:T(8,128)(2,1)} collective-permute-done((bf16[3,64,1792]{2,1,0:T(8,128)(2,1)S(1)}, bf16[3,64,1792]{2,1,0:T(8,128)(2,1)}, u32[]{:S(2)}, u32[]{:S(2)}) %collective-permute-start.2) | collective-permute-done | bytes 688160 | tf_op jit(solution)/shard_map/ppermute | solution.py:11
  275.9 8.9 %collective-permute-start.3 = (bf16[3,64,1792]{2,1,0:T(8,128)(2,1)}, bf16[3,64,1792]{2,1,0:T(8,128)(2,1)}, u32[]{:S(2)}, u32[]{:S(2)}) collective-permute-start(bf16[3,64,1792]{2,1,0:T(8,128)(2,1)} %collective-permute-done.2), channel_id=1, source_target_pairs={{0,256},{32,288},{64,320},{96,352},{128,384},{160,416},{192,448},{... | collective-permute-start | bytes 2064392 | tf_op jit(solution)/shard_map/ppermute | solution.py:11
  284.8 29.8 %collective-permute-done.3 = bf16[3,64,1792]{2,1,0:T(8,128)(2,1)} collective-permute-done((bf16[3,64,1792]{2,1,0:T(8,128)(2,1)}, bf16[3,64,1792]{2,1,0:T(8,128)(2,1)}, u32[]{:S(2)}, u32[]{:S(2)}) %collective-permute-start.3) | collective-permute-done | bytes 688160 | tf_op jit(solution)/shard_map/ppermute | solution.py:11
  314.6 2.1 fusion.21
  316.6 0.0 all-to-all-done.2
  316.6 2.6 convert_reduce_fusion
  319.2 1.9 fusion.1
  (3 shorter events, 0.1 us)
Async XLA Ops:
  0.6 2.5 copy-start
  5.6 10.8 %copy-start.4 = (s32[1,128]{1,0:T(1,128)S(1)}, s32[1,128]{1,0:T(1,128)}, u32[]{:S(2)}) copy-start(s32[1,128]{1,0:T(1,128)} %param.10) | copy-start | bytes 1540
  5.6 10.8 %copy-start.1 = (bf16[1,128,3584]{2,1,0:T(8,128)(2,1)S(1)}, bf16[1,128,3584]{2,1,0:T(8,128)(2,1)}, u32[]{:S(2)}) copy-start(bf16[1,128,3584]{2,1,0:T(8,128)(2,1)} %param.8) | copy-start | bytes 2752516
  5.6 92.3 %all-to-all-start.1 = ((bf16[32,16,3584]{2,1,0:T(8,128)(2,1)}), bf16[32,16,3584]{2,1,0:T(8,128)(2,1)}, u32[]{:S(2)}, u32[]{:S(2)}) async-start(bf16[32,16,3584]{2,1,0:T(8,128)(2,1)} %bitcast.86), calls=%async_computation.1 | async-start | bytes 7340032 | tf_op jit(solution)/shard_map/all_to_all | solution.py:53
  100.2 9.4 %copy-start.2 = (bf16[1,64,3584]{2,1,0:T(8,128)(2,1)S(1)}, bf16[1,64,3584]{2,1,0:T(8,128)(2,1)}, u32[]{:S(2)}) copy-start(bf16[1,64,3584]{2,1,0:T(8,128)(2,1)} %param.11) | copy-start | bytes 1376260
  100.2 90.9 %all-to-all-start = ((bf16[32,16,3584]{2,1,0:T(8,128)(2,1)}), bf16[32,16,3584]{2,1,0:T(8,128)(2,1)}, u32[]{:S(2)}, u32[]{:S(2)}) async-start(bf16[32,16,3584]{2,1,0:T(8,128)(2,1)} %bitcast.87), calls=%async_computation | async-start | bytes 7340032 | tf_op jit(solution)/shard_map/all_to_all | solution.py:56
  109.6 3.3 %copy-start.3 = (bf16[1,64,3584]{2,1,0:T(8,128)(2,1)S(1)}, bf16[1,64,3584]{2,1,0:T(8,128)(2,1)}, u32[]{:S(2)}) copy-start(bf16[1,64,3584]{2,1,0:T(8,128)(2,1)} %param.12) | copy-start | bytes 1376260
  198.6 118.0 %all-to-all-start.2 = ((bf16[32,16,3584]{2,1,0:T(8,128)(2,1)}), bf16[32,16,3584]{2,1,0:T(8,128)(2,1)}, u32[]{:S(2)}, u32[]{:S(2)}) async-start(bf16[32,16,3584]{2,1,0:T(8,128)(2,1)} %bitcast.85), calls=%async_computation.2 | async-start | bytes 7340032 | tf_op jit(solution)/shard_map/all_to_all | solution.py:83
  216.3 4.6 %collective-permute-start = (bf16[3,64,1792]{2,1,0:T(8,128)(2,1)S(1)}, bf16[3,64,1792]{2,1,0:T(8,128)(2,1)S(1)}, u32[]{:S(2)}, u32[]{:S(2)}) collective-permute-start(bf16[3,64,1792]{2,1,0:T(8,128)(2,1)S(1)} %pad_maximum_fusion), channel_id=1, source_target_pairs={{0,32},{32,0},{64,96},{96,64},{128,160},{160,128},{192,224},{224,1... | collective-permute-start | bytes 2064392 | tf_op jit(solution)/shard_map/ppermute | solution.py:11
  220.9 20.0 %collective-permute-start.1 = (bf16[3,64,1792]{2,1,0:T(8,128)(2,1)S(1)}, bf16[3,64,1792]{2,1,0:T(8,128)(2,1)S(1)}, u32[]{:S(2)}, u32[]{:S(2)}) collective-permute-start(bf16[3,64,1792]{2,1,0:T(8,128)(2,1)S(1)} %collective-permute-done), channel_id=1, source_target_pairs={{0,64},{32,96},{64,0},{96,32},{128,192},{160,224},{192,128},{224,1... | collective-permute-start | bytes 2064392 | tf_op jit(solution)/shard_map/ppermute | solution.py:11
  240.8 35.1 %collective-permute-start.2 = (bf16[3,64,1792]{2,1,0:T(8,128)(2,1)S(1)}, bf16[3,64,1792]{2,1,0:T(8,128)(2,1)}, u32[]{:S(2)}, u32[]{:S(2)}) collective-permute-start(bf16[3,64,1792]{2,1,0:T(8,128)(2,1)S(1)} %collective-permute-done.1), channel_id=1, source_target_pairs={{0,128},{32,160},{64,192},{96,224},{128,0},{160,32},{192,64},{224,... | collective-permute-start | bytes 2064392 | tf_op jit(solution)/shard_map/ppermute | solution.py:11
  275.9 38.7 %collective-permute-start.3 = (bf16[3,64,1792]{2,1,0:T(8,128)(2,1)}, bf16[3,64,1792]{2,1,0:T(8,128)(2,1)}, u32[]{:S(2)}, u32[]{:S(2)}) collective-permute-start(bf16[3,64,1792]{2,1,0:T(8,128)(2,1)} %collective-permute-done.2), channel_id=1, source_target_pairs={{0,256},{32,288},{64,320},{96,352},{128,384},{160,416},{192,448},{... | collective-permute-start | bytes 2064392 | tf_op jit(solution)/shard_map/ppermute | solution.py:11
where the time goes:
time: 322 us; the launch traced here: 321 us
  waiting for transfers between devices  233 us (72%)
  starting transfers between devices  50.6 us (16%)
  matrix products  24.9 us (8%)
  other arithmetic  7.23 us (2%)
  local copies, waits for them, and re-layouts  4.57 us (1%)
    all_to_all x1, waiting for transfers between devices, shards(): lax.all_to_all(jnp.repeat(packed_x, members, axis=0), 'ep', split_axis=0,...  81.2 us
    ppermute x4, waiting for transfers between devices, swapped(): lax.ppermute(x, axis, [(i, i ^ 1 << stride) for i in range(lax.axis_size(...  76.9 us
    all_to_all x1, waiting for transfers between devices, shards(): lax.all_to_all(jnp.repeat(packed_c, members, axis=0), 'ep', split_axis=0,...  74.9 us
    ppermute x4, starting transfers between devices, swapped(): lax.ppermute(x, axis, [(i, i ^ 1 << stride) for i in range(lax.axis_size(...  21.3 us
    all_to_all x1, starting transfers between devices, shards(): lax.all_to_all(jnp.repeat(packed_x, members, axis=0), 'ep', split_axis=0,...  10.7 us
    all_to_all x1, starting transfers between devices, shards(): lax.all_to_all(jnp.repeat(packed_c, members, axis=0), 'ep', split_axis=0,...  9.38 us
    all_to_all x1, starting transfers between devices, shards(): lax.all_to_all(partial_cot.reshape(ep_count, CAP, width), 'ep', split_axi...  9.14 us
  transfers between devices with their start and end apart: 7, of which 6 were waited for; matrix products, arithmetic and copies ran while one was open for 5% of the time, Pallas kernels for 0%

commit v1 on v0

v1 whole, which is shorter than its diff:
```python
import jax
import jax.numpy as jnp
from jax import lax
from jax.sharding import PartitionSpec as P

E_WIN = 2
CAP = 16
NX = 4
NY = 8
BF = jnp.bfloat16
F32 = jnp.float32


def swap_x_outer(v):
    return lax.ppermute(v, "ep", [(i, (NX - 1 - i // NY) * NY + i % NY) for i in range(NX * NY)])


def swap_x_pair(v):
    return lax.ppermute(v, "ep", [(i, i ^ NY) for i in range(NX * NY)])


def shift_y(v, step):
    return lax.ppermute(
        v, "ep", [(i, i // NY * NY + (i + step) % NY) for i in range(NX * NY)]
    )


def mirror(v):
    n = lax.axis_size("pp")
    return lax.ppermute(v, "pp", [(i, n - 1 - i) for i in range(n)])


def row_selector(block_ids, own_expert):
    onehot = (block_ids[:, None] == jnp.arange(E_WIN, dtype=jnp.int32)[None, :]).astype(jnp.int32)
    rank_in = jnp.sum(jnp.cumsum(onehot, axis=0) * onehot, axis=1) - 1
    relative = block_ids ^ own_expert
    slot = jnp.where(block_ids < E_WIN, relative * CAP + rank_in, -1)
    return slot[None, :] == jnp.arange(E_WIN * CAP, dtype=jnp.int32)[:, None]


def dot(a, b, dims):
    return lax.dot_general(a, b, (dims, ((), ())), preferred_element_type=F32)


def shards(tokens, cotangent, expert_slot, gate_fixed, w_gate, w_up, w_down):
    block_x, block_cot = tokens[0], cotangent[0]
    width = block_x.shape[1]
    half = width // 2
    h_dev = w_gate.shape[1]
    own_expert = lax.axis_index("ep") // (NX * NY // E_WIN)
    upper = lax.axis_index("pp") >= lax.axis_size("pp") // 2

    select = row_selector(expert_slot[0], own_expert).astype(BF)
    gate_value = gate_fixed[0].astype(F32) / 4096.0
    scaled = (gate_value[:, None] * block_cot.astype(F32)).astype(BF)
    packed_x = dot(select, block_x, ((1,), (0,))).astype(BF)
    packed_c = dot(select, scaled, ((1,), (0,))).astype(BF)
    other = swap_x_outer(jnp.concatenate([packed_x[CAP:], packed_c[CAP:]], axis=0))
    chunk = jnp.concatenate([packed_x[:CAP], other[:CAP], packed_c[:CAP], other[CAP:]], axis=0)
    rows = 2 * CAP

    mine = jnp.concatenate([w_gate[0], w_up[0], w_down[0]], axis=0)
    theirs = swap_x_pair(mine)

    right = left = chunk
    lefts, rights = [], []
    for step in range(3):
        right = shift_y(right, 1)
        left = shift_y(left, -1)
        rights.append(right)
        lefts.append(left)
    far_x = shift_y(right[:rows], 1)
    far_c = shift_y(left[rows:], -1)
    near = [chunk]
    for r, l in zip(rights, lefts):
        near += [r, l]
    rows_x = jnp.concatenate([p[:rows] for p in near] + [far_x], axis=0)
    rows_c = jnp.concatenate([p[rows:] for p in near] + [far_c], axis=0)

    h = h_dev
    w_gu = jnp.concatenate([mine[: 2 * h], theirs[: 2 * h]], axis=0)
    w_d = jnp.concatenate([mine[2 * h :], theirs[2 * h :]], axis=0)
    pre = dot(rows_x, w_gu, ((1,), (1,)))
    gate_pre = jnp.concatenate([pre[:, :h], pre[:, 2 * h : 3 * h]], axis=1)
    up_pre = jnp.concatenate([pre[:, h : 2 * h], pre[:, 3 * h :]], axis=1)
    sig = jax.nn.sigmoid(gate_pre)
    activated = gate_pre * sig
    hidden = (activated * up_pre).astype(BF)
    hidden_cot = dot(rows_c, w_d, ((1,), (1,)))
    gate_cot = (hidden_cot * up_pre * (sig * (1.0 + gate_pre * (1.0 - sig)))).astype(BF)
    up_cot = (hidden_cot * activated).astype(BF)
    gu_cot = jnp.concatenate([gate_cot[:, :h], up_cot[:, :h], gate_cot[:, h:], up_cot[:, h:]], axis=1)
    partial = dot(gu_cot, w_gu, ((1,), (0,))).astype(BF).reshape(NY, rows, width)

    def plus(a, b):
        return (a.astype(F32) + b.astype(F32)).astype(BF)

    go_right = shift_y(partial[7][:CAP], 1)
    go_left = shift_y(partial[7][CAP:], -1)
    go_right = jnp.concatenate([plus(partial[6][:CAP], go_right), partial[6][CAP:]], axis=0)
    go_left = jnp.concatenate([partial[5][:CAP], plus(partial[5][CAP:], go_left)], axis=0)
    go_right, go_left = shift_y(go_right, 1), shift_y(go_left, -1)
    go_right, go_left = shift_y(plus(partial[4], go_right), 1), shift_y(plus(partial[3], go_left), -1)
    go_right, go_left = shift_y(plus(partial[2], go_right), 1), shift_y(plus(partial[1], go_left), -1)
    summed = (partial[0].astype(F32) + go_right.astype(F32) + go_left.astype(F32)).astype(BF)
    back = swap_x_outer(summed[CAP:])
    branch = dot(select, jnp.concatenate([summed[:CAP], back], axis=0), ((0,), (0,)))
    input_grad = (block_cot.astype(F32) + branch).astype(BF)[None]

    grad_gu = dot(gu_cot, rows_x, ((0,), (0,)))
    grad_d = dot(hidden, rows_c, ((0,), (0,)))
    grad_own = jnp.concatenate([grad_gu[: 2 * h], grad_d[:h]], axis=0).astype(BF)
    grad_their = jnp.concatenate([grad_gu[2 * h :], grad_d[h:]], axis=0).astype(BF)

    def keep_send(v):
        low, high = v[:, :half], v[:, half:]
        return jnp.where(upper, high, low), jnp.where(upper, low, high)

    keep_own, send_own = keep_send(grad_own)
    keep_their, send_their = keep_send(grad_their)
    got_send = swap_x_pair(send_their)
    got_keep = swap_x_pair(keep_their)
    got = mirror(plus(send_own, got_send))
    total = (keep_own.astype(F32) + got_keep.astype(F32) + got.astype(F32)).astype(BF)
    return (input_grad, total[None, :h], total[None, h : 2 * h], total[None, 2 * h :])


def solution(mesh):
    wide = P("pp", "ep", None)
    flat = P("pp", "ep")
    return jax.shard_map(
        shards,
        mesh=mesh,
        in_specs=(wide, wide, flat, flat, wide, wide, wide),
        out_specs=(wide, wide, wide, wide),
        check_vma=False,
    )
```

time: 322 us -> 166 us (0.52)
  waiting for transfers between devices: 233 us -> 41.5 us
  starting transfers between devices: 50.6 us -> 100 us
  matrix products: 24.9 us -> 6.26 us
  local copies, waits for them, and re-layouts: 4.57 us -> 8.95 us
    all_to_all x3 -> x0, waiting for transfers between devices: 156 us -> none  [the longest x1 81.2 us: shards(): lax.all_to_all(jnp.repeat(packed_x, members, axis=0), 'ep', split_axis=0,...]
    ppermute x4 -> x22, starting transfers between devices: 21.3 us -> 100 us  [the longest x16 56.5 us: shift_y(): lax.ppermute(v, 'ep', [(i, i // NY * NY + (i + step) % NY) for i in range...]
    ppermute x4 -> x22, waiting for transfers between devices: 76.9 us -> 41.5 us  [the longest x16 17.2 us: shift_y(): lax.ppermute(v, 'ep', [(i, i // NY * NY + (i + step) % NY) for i in range...]
    all_to_all x3 -> x0, starting transfers between devices: 29.3 us -> none  [the longest x1 10.7 us: shards(): lax.all_to_all(jnp.repeat(packed_x, members, axis=0), 'ep', split_axis=0,...]
    dot_general x11 -> x8, matrix products: 24.9 us -> 6.26 us  [dot(): return lax.dot_general(a, b, (dims, ((), ())), preferred_element_type=F32)]
    unnamed x10 -> x25, local copies, waits for them, and re-layouts: 0.03 us -> 5.38 us
    broadcast_in_dim x2 -> x1, local copies, waits for them, and re-layouts: 4.48 us -> 0.86 us  [shards(): total[None, 2 * h:]]
  transfers between devices with their start and end apart: 7 -> 22, of which waited for: 6 -> 13; matrix products, arithmetic and copies ran while one was open for 5% -> 7% of each run, Pallas kernels for 0% -> 0%
where the time goes in v1:
time: 166 us; the launch traced here: 165 us
  starting transfers between devices  100 us (60%)
  waiting for transfers between devices  41.5 us (25%)
  local copies, waits for them, and re-layouts  8.95 us (5%)
  other arithmetic  6.35 us (4%)
  matrix products  6.26 us (4%)
    ppermute x16, starting transfers between devices, shift_y(): lax.ppermute(v, 'ep', [(i, i // NY * NY + (i + step) % NY) for i in range...  56.5 us
    ppermute x1, starting transfers between devices, mirror(): return lax.ppermute(v, 'pp', [(i, n - 1 - i) for i in range(n)])  27 us
    ppermute x16, waiting for transfers between devices, shift_y(): lax.ppermute(v, 'ep', [(i, i // NY * NY + (i + step) % NY) for i in range...  17.2 us
    ppermute x1, waiting for transfers between devices, mirror(): return lax.ppermute(v, 'pp', [(i, n - 1 - i) for i in range(n)])  14.6 us
    ppermute x2, starting transfers between devices, swap_x_outer(): lax.ppermute(v, 'ep', [(i, (NX - 1 - i // NY) * NY + i % NY) for i in ran...  9.59 us
    ppermute x3, starting transfers between devices, swap_x_pair(): return lax.ppermute(v, 'ep', [(i, i ^ NY) for i in range(NX * NY)])  7.19 us
    dot_general x8, matrix products, dot(): return lax.dot_general(a, b, (dims, ((), ())), preferred_element_type=F32)  6.26 us
    ppermute x2, waiting for transfers between devices, swap_x_outer(): lax.ppermute(v, 'ep', [(i, (NX - 1 - i // NY) * NY + i % NY) for i in ran...  6.05 us
  transfers between devices with their start and end apart: 22, of which 13 were waited for; matrix products, arithmetic and copies ran while one was open for 7% of the time, Pallas kernels for 0%

profile of v1, /device:TPU:1, one launch (start us, length us, event | category | flops | bytes accessed | tf_op | source)
XLA Modules:
  0.0 164.6 jit_solution(16182269441657107675)
XLA Ops:
  0.7 0.8 fusion.18
  1.5 0.2 reduce_window_sum.11
  1.7 0.8 select_reduce_fusion
  2.5 0.7 multiply_bitcast_fusion
  3.1 0.7 fusion.22
  3.8 0.2 convolution_convert_fusion.3
  4.1 1.5 convolution_convert_fusion.4
  5.6 0.7 constant_dynamic-update-slice_fusion.7
  6.3 5.2 %collective-permute-start = (bf16[32,3584]{1,0:T(8,128)(2,1)S(1)}, bf16[32,3584]{1,0:T(8,128)(2,1)S(1)}, u32[]{:S(2)}, u32[]{:S(2)}) collective-permute-start(bf16[32,3584]{1,0:T(8,128)(2,1)S(1)} %pad_maximum_fusion.7), channel_id=1, source_target_pairs={{0,24},{1,25},{2,26},{3,27},{4,28},{5,29},{6,30},{7,31},{8,16},{9,... | collective-permute-start | bytes 688136 | tf_op jit(solution)/shard_map/ppermute | solution.py:15
  11.6 3.4 %collective-permute-done = bf16[32,3584]{1,0:T(8,128)(2,1)S(1)} collective-permute-done((bf16[32,3584]{1,0:T(8,128)(2,1)S(1)}, bf16[32,3584]{1,0:T(8,128)(2,1)S(1)}, u32[]{:S(2)}, u32[]{:S(2)}) %collective-permute-start) | collective-permute-done | bytes 229408 | tf_op jit(solution)/shard_map/ppermute | solution.py:15
  14.9 0.7 constant_dynamic-update-slice_fusion.6
  15.6 0.8 pad_maximum_fusion.6
  16.4 5.0 %collective-permute-start.1 = (bf16[64,3584]{1,0:T(8,128)(2,1)}, bf16[64,3584]{1,0:T(8,128)(2,1)}, u32[]{:S(2)}, u32[]{:S(2)}) collective-permute-start(bf16[64,3584]{1,0:T(8,128)(2,1)} %pad_maximum_fusion.6), channel_id=1, source_target_pairs={{0,1},{1,2},{2,3},{3,4},{4,5},{5,6},{6,7},{7,0},{8,9},{9,10},{10,1... | collective-permute-start | bytes 1376264 | tf_op jit(solution)/shard_map/ppermute | solution.py:23
  21.4 3.8 %collective-permute-start.2 = (bf16[64,3584]{1,0:T(8,128)(2,1)}, bf16[64,3584]{1,0:T(8,128)(2,1)S(1)}, u32[]{:S(2)}, u32[]{:S(2)}) collective-permute-start(bf16[64,3584]{1,0:T(8,128)(2,1)} %pad_maximum_fusion.6), channel_id=1, source_target_pairs={{0,7},{1,0},{2,1},{3,2},{4,3},{5,4},{6,5},{7,6},{8,15},{9,8},{10,9... | collective-permute-start | bytes 1376264 | tf_op jit(solution)/shard_map/ppermute | solution.py:23
  25.2 1.2 pad_maximum_fusion.1
  26.4 1.9 %collective-permute-start.8 = (bf16[192,3584]{1,0:T(8,128)(2,1)}, bf16[192,3584]{1,0:T(8,128)(2,1)}, u32[]{:S(2)}, u32[]{:S(2)}) collective-permute-start(bf16[192,3584]{1,0:T(8,128)(2,1)} %pad_maximum_fusion.1), channel_id=1, source_target_pairs={{0,8},{1,9},{2,10},{3,11},{4,12},{5,13},{6,14},{7,15},{8,0},{9,1},... | collective-permute-start | bytes 4128776 | tf_op jit(solution)/shard_map/ppermute | solution.py:19
  28.4 1.1 collective-permute-done.1
  29.5 3.7 %collective-permute-start.3 = (bf16[64,3584]{1,0:T(8,128)(2,1)}, bf16[64,3584]{1,0:T(8,128)(2,1)S(1)}, u32[]{:S(2)}, u32[]{:S(2)}) collective-permute-start(bf16[64,3584]{1,0:T(8,128)(2,1)} %collective-permute-done.1), channel_id=1, source_target_pairs={{0,1},{1,2},{2,3},{3,4},{4,5},{5,6},{6,7},{7,0},{8,9},{9,10},{10,1... | collective-permute-start | bytes 1376264 | tf_op jit(solution)/shard_map/ppermute | solution.py:23
  33.2 4.7 %collective-permute-start.4 = (bf16[64,3584]{1,0:T(8,128)(2,1)S(1)}, bf16[64,3584]{1,0:T(8,128)(2,1)S(1)}, u32[]{:S(2)}, u32[]{:S(2)}) collective-permute-start(bf16[64,3584]{1,0:T(8,128)(2,1)S(1)} %collective-permute-done.2), channel_id=1, source_target_pairs={{0,7},{1,0},{2,1},{3,2},{4,3},{5,4},{6,5},{7,6},{8,15},{9,8},{10,9... | collective-permute-start | bytes 1376264 | tf_op jit(solution)/shard_map/ppermute | solution.py:23
  37.9 1.8 %slice_dynamic-update-slice_fusion.4 = (bf16[256,3584]{1,0:T(8,128)(2,1)S(1)}, bf16[256,3584]{1,0:T(8,128)(2,1)}) fusion(bf16[256,3584]{1,0:T(8,128)(2,1)S(1)} %get-tuple-element.43, bf16[64,3584]{1,0:T(8,128)(2,1)} %collective-permute-done.1, bf16[256,3584]{1,0:T(8,128)(2,1)} %get-tuple-element.44), kind=kLoop, calls=%fused_computation.45 | loop fusion | bytes 917504
  39.6 0.7 slice_dynamic-update-slice_fusion.3
  40.4 2.0 %collective-permute-done.3 = bf16[64,3584]{1,0:T(8,128)(2,1)S(1)} collective-permute-done((bf16[64,3584]{1,0:T(8,128)(2,1)}, bf16[64,3584]{1,0:T(8,128)(2,1)S(1)}, u32[]{:S(2)}, u32[]{:S(2)}) %collective-permute-start.3) | collective-permute-done | bytes 458784 | tf_op jit(solution)/shard_map/ppermute | solution.py:23
  42.4 2.5 %collective-permute-start.5 = (bf16[64,3584]{1,0:T(8,128)(2,1)S(1)}, bf16[64,3584]{1,0:T(8,128)(2,1)S(1)}, u32[]{:S(2)}, u32[]{:S(2)}) collective-permute-start(bf16[64,3584]{1,0:T(8,128)(2,1)S(1)} %collective-permute-done.3), channel_id=1, source_target_pairs={{0,1},{1,2},{2,3},{3,4},{4,5},{5,6},{6,7},{7,0},{8,9},{9,10},{10,1... | collective-permute-start | bytes 1376264 | tf_op jit(solution)/shard_map/ppermute | solution.py:23
  44.9 4.7 %collective-permute-start.6 = (bf16[64,3584]{1,0:T(8,128)(2,1)S(1)}, bf16[64,3584]{1,0:T(8,128)(2,1)S(1)}, u32[]{:S(2)}, u32[]{:S(2)}) collective-permute-start(bf16[64,3584]{1,0:T(8,128)(2,1)S(1)} %collective-permute-done.4), channel_id=1, source_target_pairs={{0,7},{1,0},{2,1},{3,2},{4,3},{5,4},{6,5},{7,6},{8,15},{9,8},{10,9... | collective-permute-start | bytes 1376264 | tf_op jit(solution)/shard_map/ppermute | solution.py:23
  49.6 0.7 slice_dynamic-update-slice_fusion.2
  50.3 0.7 slice_dynamic-update-slice_fusion.1
  51.1 3.6 %collective-permute-done.8 = bf16[192,3584]{1,0:T(8,128)(2,1)} collective-permute-done((bf16[192,3584]{1,0:T(8,128)(2,1)}, bf16[192,3584]{1,0:T(8,128)(2,1)}, u32[]{:S(2)}, u32[]{:S(2)}) %collective-permute-start.8) | collective-permute-done | bytes 1376288 | tf_op jit(solution)/shard_map/ppermute | solution.py:19
  54.7 1.2 slice.262
  55.9 1.1 slice.255
  57.1 2.5 %collective-permute-start.9 = (bf16[32,3584]{1,0:T(8,128)(2,1)S(1)}, bf16[32,3584]{1,0:T(8,128)(2,1)S(1)}, u32[]{:S(2)}, u32[]{:S(2)}) collective-permute-start(bf16[32,3584]{1,0:T(8,128)(2,1)S(1)} %get-tuple-element.21), channel_id=1, source_target_pairs={{0,1},{1,2},{2,3},{3,4},{4,5},{5,6},{6,7},{7,0},{8,9},{9,10},{10,1... | collective-permute-start | bytes 688136 | tf_op jit(solution)/shard_map/ppermute | solution.py:23
  59.7 4.5 %collective-permute-start.7 = (bf16[32,3584]{1,0:T(8,128)(2,1)S(1)}, bf16[32,3584]{1,0:T(8,128)(2,1)S(1)}, u32[]{:S(2)}, u32[]{:S(2)}) collective-permute-start(bf16[32,3584]{1,0:T(8,128)(2,1)S(1)} %get-tuple-element.26), channel_id=1, source_target_pairs={{0,7},{1,0},{2,1},{3,2},{4,3},{5,4},{6,5},{7,6},{8,15},{9,8},{10,9... | collective-permute-start | bytes 688136 | tf_op jit(solution)/shard_map/ppermute | solution.py:23
  64.2 1.4 collective-permute-done.9
  65.7 0.7 fusion.11
  66.4 2.4 %collective-permute-done.7 = bf16[32,3584]{1,0:T(8,128)(2,1)S(1)} collective-permute-done((bf16[32,3584]{1,0:T(8,128)(2,1)S(1)}, bf16[32,3584]{1,0:T(8,128)(2,1)S(1)}, u32[]{:S(2)}, u32[]{:S(2)}) %collective-permute-start.7) | collective-permute-done | bytes 229408 | tf_op jit(solution)/shard_map/ppermute | solution.py:23
  68.8 0.7 multiply_convert_fusion.2
  69.6 0.6 convolution_convert_fusion
  70.2 0.7 convolution_convert_fusion.1
  70.9 0.1 fusion.30
  71.1 4.5 %collective-permute-start.10 = (bf16[16,3584]{1,0:T(8,128)(2,1)S(1)}, bf16[16,3584]{1,0:T(8,128)(2,1)S(1)}, u32[]{:S(2)}, u32[]{:S(2)}) collective-permute-start(bf16[16,3584]{1,0:T(8,128)(2,1)S(1)} %get-tuple-element.10), channel_id=1, source_target_pairs={{0,1},{1,2},{2,3},{3,4},{4,5},{5,6},{6,7},{7,0},{8,9},{9,10},{10,1... | collective-permute-start | bytes 344072 | tf_op jit(solution)/shard_map/ppermute | solution.py:23
  75.6 1.9 %collective-permute-start.14 = (bf16[16,3584]{1,0:T(8,128)(2,1)S(1)}, bf16[16,3584]{1,0:T(8,128)(2,1)S(1)}, u32[]{:S(2)}, u32[]{:S(2)}) collective-permute-start(bf16[16,3584]{1,0:T(8,128)(2,1)S(1)} %get-tuple-element.11), channel_id=1, source_target_pairs={{0,7},{1,0},{2,1},{3,2},{4,3},{5,4},{6,5},{7,6},{8,15},{9,8},{10,9... | collective-permute-start | bytes 344072 | tf_op jit(solution)/shard_map/ppermute | solution.py:23
  77.6 0.4 convolution_convert_fusion.2
  78.0 4.1 %collective-permute-done.14 = bf16[16,3584]{1,0:T(8,128)(2,1)S(1)} collective-permute-done((bf16[16,3584]{1,0:T(8,128)(2,1)S(1)}, bf16[16,3584]{1,0:T(8,128)(2,1)S(1)}, u32[]{:S(2)}, u32[]{:S(2)}) %collective-permute-start.14) | collective-permute-done | bytes 114720 | tf_op jit(solution)/shard_map/ppermute | solution.py:23
  82.2 4.6 %collective-permute-start.11 = (bf16[32,3584]{1,0:T(8,128)(2,1)S(1)}, bf16[32,3584]{1,0:T(8,128)(2,1)S(1)}, u32[]{:S(2)}, u32[]{:S(2)}) collective-permute-start(bf16[32,3584]{1,0:T(8,128)(2,1)S(1)} %pad_maximum_fusion.8), channel_id=1, source_target_pairs={{0,1},{1,2},{2,3},{3,4},{4,5},{5,6},{6,7},{7,0},{8,9},{9,10},{10,1... | collective-permute-start | bytes 688136 | tf_op jit(solution)/shard_map/ppermute | solution.py:23
  86.8 1.9 %collective-permute-start.15 = (bf16[32,3584]{1,0:T(8,128)(2,1)S(1)}, bf16[32,3584]{1,0:T(8,128)(2,1)S(1)}, u32[]{:S(2)}, u32[]{:S(2)}) collective-permute-start(bf16[32,3584]{1,0:T(8,128)(2,1)S(1)} %pad_maximum_fusion.9), channel_id=1, source_target_pairs={{0,7},{1,0},{2,1},{3,2},{4,3},{5,4},{6,5},{7,6},{8,15},{9,8},{10,9... | collective-permute-start | bytes 688136 | tf_op jit(solution)/shard_map/ppermute | solution.py:23
  88.7 1.4 collective-permute-done.11
  90.2 3.4 %collective-permute-start.12 = (bf16[32,3584]{1,0:T(8,128)(2,1)S(1)}, bf16[32,3584]{1,0:T(8,128)(2,1)S(1)}, u32[]{:S(2)}, u32[]{:S(2)}) collective-permute-start(bf16[32,3584]{1,0:T(8,128)(2,1)S(1)} %add_convert_fusion.6), channel_id=1, source_target_pairs={{0,1},{1,2},{2,3},{3,4},{4,5},{5,6},{6,7},{7,0},{8,9},{9,10},{10,1... | collective-permute-start | bytes 688136 | tf_op jit(solution)/shard_map/ppermute | solution.py:23
  93.7 0.5 collective-permute-done.15
  94.1 4.3 %collective-permute-done.12 = bf16[32,3584]{1,0:T(8,128)(2,1)S(1)} collective-permute-done((bf16[32,3584]{1,0:T(8,128)(2,1)S(1)}, bf16[32,3584]{1,0:T(8,128)(2,1)S(1)}, u32[]{:S(2)}, u32[]{:S(2)}) %collective-permute-start.12) | collective-permute-done | bytes 229408 | tf_op jit(solution)/shard_map/ppermute | solution.py:23
  98.4 0.1 add_convert_fusion.5
  98.5 2.2 %collective-permute-start.16 = (bf16[32,3584]{1,0:T(8,128)(2,1)S(1)}, bf16[32,3584]{1,0:T(8,128)(2,1)S(1)}, u32[]{:S(2)}, u32[]{:S(2)}) collective-permute-start(bf16[32,3584]{1,0:T(8,128)(2,1)S(1)} %get-tuple-element.7), channel_id=1, source_target_pairs={{0,7},{1,0},{2,1},{3,2},{4,3},{5,4},{6,5},{7,6},{8,15},{9,8},{10,9... | collective-permute-start | bytes 688136 | tf_op jit(solution)/shard_map/ppermute | solution.py:23
  100.8 0.2 broadcast_select_fusion.1
  101.0 1.9 %collective-permute-start.20 = (bf16[192,1792]{1,0:T(8,128)(2,1)S(1)}, bf16[192,1792]{1,0:T(8,128)(2,1)S(1)}, u32[]{:S(2)}, u32[]{:S(2)}) collective-permute-start(bf16[192,1792]{1,0:T(8,128)(2,1)S(1)} %get-tuple-element.15), channel_id=1, source_target_pairs={{0,8},{1,9},{2,10},{3,11},{4,12},{5,13},{6,14},{7,15},{8,0},{9,1},... | collective-permute-start | bytes 2064392 | tf_op jit(solution)/shard_map/ppermute | solution.py:19
  102.9 3.3 %collective-permute-start.19 = (bf16[192,1792]{1,0:T(8,128)(2,1)S(1)}, bf16[192,1792]{1,0:T(8,128)(2,1)S(1)}, u32[]{:S(2)}, u32[]{:S(2)}) collective-permute-start(bf16[192,1792]{1,0:T(8,128)(2,1)S(1)} %get-tuple-element.14), channel_id=1, source_target_pairs={{0,8},{1,9},{2,10},{3,11},{4,12},{5,13},{6,14},{7,15},{8,0},{9,1},... | collective-permute-start | bytes 2064392 | tf_op jit(solution)/shard_map/ppermute | solution.py:19
  106.3 3.6 %collective-permute-start.13 = (bf16[32,3584]{1,0:T(8,128)(2,1)S(1)}, bf16[32,3584]{1,0:T(8,128)(2,1)S(1)}, u32[]{:S(2)}, u32[]{:S(2)}) collective-permute-start(bf16[32,3584]{1,0:T(8,128)(2,1)S(1)} %get-tuple-element.6), channel_id=1, source_target_pairs={{0,1},{1,2},{2,3},{3,4},{4,5},{5,6},{6,7},{7,0},{8,9},{9,10},{10,1... | collective-permute-start | bytes 688136 | tf_op jit(solution)/shard_map/ppermute | solution.py:23
  110.0 2.9 %collective-permute-start.17 = (bf16[32,3584]{1,0:T(8,128)(2,1)S(1)}, bf16[32,3584]{1,0:T(8,128)(2,1)S(1)}, u32[]{:S(2)}, u32[]{:S(2)}) collective-permute-start(bf16[32,3584]{1,0:T(8,128)(2,1)S(1)} %add_convert_fusion.3), channel_id=1, source_target_pairs={{0,7},{1,0},{2,1},{3,2},{4,3},{5,4},{6,5},{7,6},{8,15},{9,8},{10,9... | collective-permute-start | bytes 688136 | tf_op jit(solution)/shard_map/ppermute | solution.py:23
  112.9 0.1 collective-permute-done.20
  113.0 0.3 add_convert_fusion.1
  113.2 27.0 %collective-permute-start.21 = (bf16[192,1792]{1,0:T(8,128)(2,1)S(1)}, bf16[192,1792]{1,0:T(8,128)(2,1)S(1)}, u32[]{:S(2)}, u32[]{:S(2)}) collective-permute-start(bf16[192,1792]{1,0:T(8,128)(2,1)S(1)} %add_convert_fusion.1), channel_id=1, source_target_pairs={{0,480},{32,448},{64,416},{96,384},{128,352},{160,320},{192,288},{... | collective-permute-start | bytes 2064392 | tf_op jit(solution)/shard_map/ppermute | solution.py:30
  140.4 4.4 %collective-permute-start.18 = (bf16[16,3584]{1,0:T(8,128)(2,1)S(1)}, bf16[16,3584]{1,0:T(8,128)(2,1)S(1)}, u32[]{:S(2)}, u32[]{:S(2)}) collective-permute-start(bf16[16,3584]{1,0:T(8,128)(2,1)S(1)} %get-tuple-element.42), channel_id=1, source_target_pairs={{0,24},{1,25},{2,26},{3,27},{4,28},{5,29},{6,30},{7,31},{8,16},{9,... | collective-permute-start | bytes 344072 | tf_op jit(solution)/shard_map/ppermute | solution.py:15
  144.8 2.7 %collective-permute-done.18 = bf16[16,3584]{1,0:T(8,128)(2,1)S(1)} collective-permute-done((bf16[16,3584]{1,0:T(8,128)(2,1)S(1)}, bf16[16,3584]{1,0:T(8,128)(2,1)S(1)}, u32[]{:S(2)}, u32[]{:S(2)}) %collective-permute-start.18) | collective-permute-done | bytes 114720 | tf_op jit(solution)/shard_map/ppermute | solution.py:15
  147.4 1.4 fusion.1
  148.8 14.6 %collective-permute-done.21 = bf16[192,1792]{1,0:T(8,128)(2,1)S(1)} collective-permute-done((bf16[192,1792]{1,0:T(8,128)(2,1)S(1)}, bf16[192,1792]{1,0:T(8,128)(2,1)S(1)}, u32[]{:S(2)}, u32[]{:S(2)}) %collective-permute-start.21) | collective-permute-done | bytes 688160 | tf_op jit(solution)/shard_map/ppermute | solution.py:30
  163.4 0.3 add_convert_fusion
  163.7 0.9 slice_bitcast_fusion
  (44 shorter events, 0.7 us)
Async XLA Ops:
  0.6 3.2 %copy-start = (bf16[1,128,3584]{2,1,0:T(8,128)(2,1)S(1)}, bf16[1,128,3584]{2,1,0:T(8,128)(2,1)}, u32[]{:S(2)}) copy-start(bf16[1,128,3584]{2,1,0:T(8,128)(2,1)} %param.7) | copy-start | bytes 2752516
  5.6 19.6 %copy-start.3 = (bf16[1,64,3584]{2,1,0:T(8,128)(2,1)S(1)}, bf16[1,64,3584]{2,1,0:T(8,128)(2,1)}, u32[]{:S(2)}) copy-start(bf16[1,64,3584]{2,1,0:T(8,128)(2,1)} %param.13) | copy-start | bytes 1376260
  5.6 19.6 %copy-start.5 = (bf16[1,64,3584]{2,1,0:T(8,128)(2,1)S(1)}, bf16[1,64,3584]{2,1,0:T(8,128)(2,1)}, u32[]{:S(2)}) copy-start(bf16[1,64,3584]{2,1,0:T(8,128)(2,1)} %param.12) | copy-start | bytes 1376260
  5.6 19.6 %copy-start.7 = (bf16[1,64,3584]{2,1,0:T(8,128)(2,1)S(1)}, bf16[1,64,3584]{2,1,0:T(8,128)(2,1)}, u32[]{:S(2)}) copy-start(bf16[1,64,3584]{2,1,0:T(8,128)(2,1)} %param.11) | copy-start | bytes 1376260
  6.3 8.6 %collective-permute-start = (bf16[32,3584]{1,0:T(8,128)(2,1)S(1)}, bf16[32,3584]{1,0:T(8,128)(2,1)S(1)}, u32[]{:S(2)}, u32[]{:S(2)}) collective-permute-start(bf16[32,3584]{1,0:T(8,128)(2,1)S(1)} %pad_maximum_fusion.7), channel_id=1, source_target_pairs={{0,24},{1,25},{2,26},{3,27},{4,28},{5,29},{6,30},{7,31},{8,16},{9,... | collective-permute-start | bytes 688136 | tf_op jit(solution)/shard_map/ppermute | solution.py:15
  16.4 13.0 %collective-permute-start.1 = (bf16[64,3584]{1,0:T(8,128)(2,1)}, bf16[64,3584]{1,0:T(8,128)(2,1)}, u32[]{:S(2)}, u32[]{:S(2)}) collective-permute-start(bf16[64,3584]{1,0:T(8,128)(2,1)} %pad_maximum_fusion.6), channel_id=1, source_target_pairs={{0,1},{1,2},{2,3},{3,4},{4,5},{5,6},{6,7},{7,0},{8,9},{9,10},{10,1... | collective-permute-start | bytes 1376264 | tf_op jit(solution)/shard_map/ppermute | solution.py:23
  21.4 11.8 %collective-permute-start.2 = (bf16[64,3584]{1,0:T(8,128)(2,1)}, bf16[64,3584]{1,0:T(8,128)(2,1)S(1)}, u32[]{:S(2)}, u32[]{:S(2)}) collective-permute-start(bf16[64,3584]{1,0:T(8,128)(2,1)} %pad_maximum_fusion.6), channel_id=1, source_target_pairs={{0,7},{1,0},{2,1},{3,2},{4,3},{5,4},{6,5},{7,6},{8,15},{9,8},{10,9... | collective-permute-start | bytes 1376264 | tf_op jit(solution)/shard_map/ppermute | solution.py:23
  26.4 28.2 %collective-permute-start.8 = (bf16[192,3584]{1,0:T(8,128)(2,1)}, bf16[192,3584]{1,0:T(8,128)(2,1)}, u32[]{:S(2)}, u32[]{:S(2)}) collective-permute-start(bf16[192,3584]{1,0:T(8,128)(2,1)} %pad_maximum_fusion.1), channel_id=1, source_target_pairs={{0,8},{1,9},{2,10},{3,11},{4,12},{5,13},{6,14},{7,15},{8,0},{9,1},... | collective-permute-start | bytes 4128776 | tf_op jit(solution)/shard_map/ppermute | solution.py:19
  29.5 12.9 %collective-permute-start.3 = (bf16[64,3584]{1,0:T(8,128)(2,1)}, bf16[64,3584]{1,0:T(8,128)(2,1)S(1)}, u32[]{:S(2)}, u32[]{:S(2)}) collective-permute-start(bf16[64,3584]{1,0:T(8,128)(2,1)} %collective-permute-done.1), channel_id=1, source_target_pairs={{0,1},{1,2},{2,3},{3,4},{4,5},{5,6},{6,7},{7,0},{8,9},{9,10},{10,1... | collective-permute-start | bytes 1376264 | tf_op jit(solution)/shard_map/ppermute | solution.py:23
  33.2 11.7 %collective-permute-start.4 = (bf16[64,3584]{1,0:T(8,128)(2,1)S(1)}, bf16[64,3584]{1,0:T(8,128)(2,1)S(1)}, u32[]{:S(2)}, u32[]{:S(2)}) collective-permute-start(bf16[64,3584]{1,0:T(8,128)(2,1)S(1)} %collective-permute-done.2), channel_id=1, source_target_pairs={{0,7},{1,0},{2,1},{3,2},{4,3},{5,4},{6,5},{7,6},{8,15},{9,8},{10,9... | collective-permute-start | bytes 1376264 | tf_op jit(solution)/shard_map/ppermute | solution.py:23
  42.4 14.7 %collective-permute-start.5 = (bf16[64,3584]{1,0:T(8,128)(2,1)S(1)}, bf16[64,3584]{1,0:T(8,128)(2,1)S(1)}, u32[]{:S(2)}, u32[]{:S(2)}) collective-permute-start(bf16[64,3584]{1,0:T(8,128)(2,1)S(1)} %collective-permute-done.3), channel_id=1, source_target_pairs={{0,1},{1,2},{2,3},{3,4},{4,5},{5,6},{6,7},{7,0},{8,9},{9,10},{10,1... | collective-permute-start | bytes 1376264 | tf_op jit(solution)/shard_map/ppermute | solution.py:23
  44.9 14.8 %collective-permute-start.6 = (bf16[64,3584]{1,0:T(8,128)(2,1)S(1)}, bf16[64,3584]{1,0:T(8,128)(2,1)S(1)}, u32[]{:S(2)}, u32[]{:S(2)}) collective-permute-start(bf16[64,3584]{1,0:T(8,128)(2,1)S(1)} %collective-permute-done.4), channel_id=1, source_target_pairs={{0,7},{1,0},{2,1},{3,2},{4,3},{5,4},{6,5},{7,6},{8,15},{9,8},{10,9... | collective-permute-start | bytes 1376264 | tf_op jit(solution)/shard_map/ppermute | solution.py:23
  51.1 6.0 %copy-start.2 = (bf16[256,3584]{1,0:T(8,128)(2,1)S(1)}, bf16[256,3584]{1,0:T(8,128)(2,1)}, u32[]{:S(2)}) copy-start(bf16[256,3584]{1,0:T(8,128)(2,1)} %get-tuple-element.28) | copy-start | bytes 5505028
  55.9 9.7 %copy-start.6 = (bf16[1,64,3584]{2,1,0:T(8,128)(2,1)S(1)}, bf16[1,64,3584]{2,1,0:T(8,128)(2,1)}, u32[]{:S(2)}) copy-start(bf16[1,64,3584]{2,1,0:T(8,128)(2,1)} %param.12) | copy-start | bytes 1376260
  55.9 9.7 %copy-start.8 = (bf16[1,64,3584]{2,1,0:T(8,128)(2,1)S(1)}, bf16[1,64,3584]{2,1,0:T(8,128)(2,1)}, u32[]{:S(2)}) copy-start(bf16[1,64,3584]{2,1,0:T(8,128)(2,1)} %param.11) | copy-start | bytes 1376260
  57.1 8.5 %collective-permute-start.9 = (bf16[32,3584]{1,0:T(8,128)(2,1)S(1)}, bf16[32,3584]{1,0:T(8,128)(2,1)S(1)}, u32[]{:S(2)}, u32[]{:S(2)}) collective-permute-start(bf16[32,3584]{1,0:T(8,128)(2,1)S(1)} %get-tuple-element.21), channel_id=1, source_target_pairs={{0,1},{1,2},{2,3},{3,4},{4,5},{5,6},{6,7},{7,0},{8,9},{9,10},{10,1... | collective-permute-start | bytes 688136 | tf_op jit(solution)/shard_map/ppermute | solution.py:23
  59.7 9.1 %collective-permute-start.7 = (bf16[32,3584]{1,0:T(8,128)(2,1)S(1)}, bf16[32,3584]{1,0:T(8,128)(2,1)S(1)}, u32[]{:S(2)}, u32[]{:S(2)}) collective-permute-start(bf16[32,3584]{1,0:T(8,128)(2,1)S(1)} %get-tuple-element.26), channel_id=1, source_target_pairs={{0,7},{1,0},{2,1},{3,2},{4,3},{5,4},{6,5},{7,6},{8,15},{9,8},{10,9... | collective-permute-start | bytes 688136 | tf_op jit(solution)/shard_map/ppermute | solution.py:23
  65.7 3.2 %copy-start.4 = (bf16[1,64,3584]{2,1,0:T(8,128)(2,1)S(1)}, bf16[1,64,3584]{2,1,0:T(8,128)(2,1)}, u32[]{:S(2)}) copy-start(bf16[1,64,3584]{2,1,0:T(8,128)(2,1)} %param.13) | copy-start | bytes 1376260
  71.1 7.0 %collective-permute-start.10 = (bf16[16,3584]{1,0:T(8,128)(2,1)S(1)}, bf16[16,3584]{1,0:T(8,128)(2,1)S(1)}, u32[]{:S(2)}, u32[]{:S(2)}) collective-permute-start(bf16[16,3584]{1,0:T(8,128)(2,1)S(1)} %get-tuple-element.10), channel_id=1, source_target_pairs={{0,1},{1,2},{2,3},{3,4},{4,5},{5,6},{6,7},{7,0},{8,9},{9,10},{10,1... | collective-permute-start | bytes 344072 | tf_op jit(solution)/shard_map/ppermute | solution.py:23
  75.6 6.5 %collective-permute-start.14 = (bf16[16,3584]{1,0:T(8,128)(2,1)S(1)}, bf16[16,3584]{1,0:T(8,128)(2,1)S(1)}, u32[]{:S(2)}, u32[]{:S(2)}) collective-permute-start(bf16[16,3584]{1,0:T(8,128)(2,1)S(1)} %get-tuple-element.11), channel_id=1, source_target_pairs={{0,7},{1,0},{2,1},{3,2},{4,3},{5,4},{6,5},{7,6},{8,15},{9,8},{10,9... | collective-permute-start | bytes 344072 | tf_op jit(solution)/shard_map/ppermute | solution.py:23
  82.2 8.0 %collective-permute-start.11 = (bf16[32,3584]{1,0:T(8,128)(2,1)S(1)}, bf16[32,3584]{1,0:T(8,128)(2,1)S(1)}, u32[]{:S(2)}, u32[]{:S(2)}) collective-permute-start(bf16[32,3584]{1,0:T(8,128)(2,1)S(1)} %pad_maximum_fusion.8), channel_id=1, source_target_pairs={{0,1},{1,2},{2,3},{3,4},{4,5},{5,6},{6,7},{7,0},{8,9},{9,10},{10,1... | collective-permute-start | bytes 688136 | tf_op jit(solution)/shard_map/ppermute | solution.py:23
  86.8 7.4 %collective-permute-start.15 = (bf16[32,3584]{1,0:T(8,128)(2,1)S(1)}, bf16[32,3584]{1,0:T(8,128)(2,1)S(1)}, u32[]{:S(2)}, u32[]{:S(2)}) collective-permute-start(bf16[32,3584]{1,0:T(8,128)(2,1)S(1)} %pad_maximum_fusion.9), channel_id=1, source_target_pairs={{0,7},{1,0},{2,1},{3,2},{4,3},{5,4},{6,5},{7,6},{8,15},{9,8},{10,9... | collective-permute-start | bytes 688136 | tf_op jit(solution)/shard_map/ppermute | solution.py:23
  90.2 8.2 %collective-permute-start.12 = (bf16[32,3584]{1,0:T(8,128)(2,1)S(1)}, bf16[32,3584]{1,0:T(8,128)(2,1)S(1)}, u32[]{:S(2)}, u32[]{:S(2)}) collective-permute-start(bf16[32,3584]{1,0:T(8,128)(2,1)S(1)} %add_convert_fusion.6), channel_id=1, source_target_pairs={{0,1},{1,2},{2,3},{3,4},{4,5},{5,6},{6,7},{7,0},{8,9},{9,10},{10,1... | collective-permute-start | bytes 688136 | tf_op jit(solution)/shard_map/ppermute | solution.py:23
  98.5 11.4 %collective-permute-start.16 = (bf16[32,3584]{1,0:T(8,128)(2,1)S(1)}, bf16[32,3584]{1,0:T(8,128)(2,1)S(1)}, u32[]{:S(2)}, u32[]{:S(2)}) collective-permute-start(bf16[32,3584]{1,0:T(8,128)(2,1)S(1)} %get-tuple-element.7), channel_id=1, source_target_pairs={{0,7},{1,0},{2,1},{3,2},{4,3},{5,4},{6,5},{7,6},{8,15},{9,8},{10,9... | collective-permute-start | bytes 688136 | tf_op jit(solution)/shard_map/ppermute | solution.py:23
  101.0 12.0 %collective-permute-start.20 = (bf16[192,1792]{1,0:T(8,128)(2,1)S(1)}, bf16[192,1792]{1,0:T(8,128)(2,1)S(1)}, u32[]{:S(2)}, u32[]{:S(2)}) collective-permute-start(bf16[192,1792]{1,0:T(8,128)(2,1)S(1)} %get-tuple-element.15), channel_id=1, source_target_pairs={{0,8},{1,9},{2,10},{3,11},{4,12},{5,13},{6,14},{7,15},{8,0},{9,1},... | collective-permute-start | bytes 2064392 | tf_op jit(solution)/shard_map/ppermute | solution.py:19
  102.9 45.9 %collective-permute-start.19 = (bf16[192,1792]{1,0:T(8,128)(2,1)S(1)}, bf16[192,1792]{1,0:T(8,128)(2,1)S(1)}, u32[]{:S(2)}, u32[]{:S(2)}) collective-permute-start(bf16[192,1792]{1,0:T(8,128)(2,1)S(1)} %get-tuple-element.14), channel_id=1, source_target_pairs={{0,8},{1,9},{2,10},{3,11},{4,12},{5,13},{6,14},{7,15},{8,0},{9,1},... | collective-permute-start | bytes 2064392 | tf_op jit(solution)/shard_map/ppermute | solution.py:19
  106.3 34.0 %collective-permute-start.13 = (bf16[32,3584]{1,0:T(8,128)(2,1)S(1)}, bf16[32,3584]{1,0:T(8,128)(2,1)S(1)}, u32[]{:S(2)}, u32[]{:S(2)}) collective-permute-start(bf16[32,3584]{1,0:T(8,128)(2,1)S(1)} %get-tuple-element.6), channel_id=1, source_target_pairs={{0,1},{1,2},{2,3},{3,4},{4,5},{5,6},{6,7},{7,0},{8,9},{9,10},{10,1... | collective-permute-start | bytes 688136 | tf_op jit(solution)/shard_map/ppermute | solution.py:23
  110.0 30.3 %collective-permute-start.17 = (bf16[32,3584]{1,0:T(8,128)(2,1)S(1)}, bf16[32,3584]{1,0:T(8,128)(2,1)S(1)}, u32[]{:S(2)}, u32[]{:S(2)}) collective-permute-start(bf16[32,3584]{1,0:T(8,128)(2,1)S(1)} %add_convert_fusion.3), channel_id=1, source_target_pairs={{0,7},{1,0},{2,1},{3,2},{4,3},{5,4},{6,5},{7,6},{8,15},{9,8},{10,9... | collective-permute-start | bytes 688136 | tf_op jit(solution)/shard_map/ppermute | solution.py:23
  113.0 34.5 %copy-start.1 = (bf16[1,128,3584]{2,1,0:T(8,128)(2,1)S(1)}, bf16[1,128,3584]{2,1,0:T(8,128)(2,1)}, u32[]{:S(2)}) copy-start(bf16[1,128,3584]{2,1,0:T(8,128)(2,1)} %param.8) | copy-start | bytes 2752516
  113.2 50.2 %collective-permute-start.21 = (bf16[192,1792]{1,0:T(8,128)(2,1)S(1)}, bf16[192,1792]{1,0:T(8,128)(2,1)S(1)}, u32[]{:S(2)}, u32[]{:S(2)}) collective-permute-start(bf16[192,1792]{1,0:T(8,128)(2,1)S(1)} %add_convert_fusion.1), channel_id=1, source_target_pairs={{0,480},{32,448},{64,416},{96,384},{128,352},{160,320},{192,288},{... | collective-permute-start | bytes 2064392 | tf_op jit(solution)/shard_map/ppermute | solution.py:30
  140.4 7.0 %collective-permute-start.18 = (bf16[16,3584]{1,0:T(8,128)(2,1)S(1)}, bf16[16,3584]{1,0:T(8,128)(2,1)S(1)}, u32[]{:S(2)}, u32[]{:S(2)}) collective-permute-start(bf16[16,3584]{1,0:T(8,128)(2,1)S(1)} %get-tuple-element.42), channel_id=1, source_target_pairs={{0,24},{1,25},{2,26},{3,27},{4,28},{5,29},{6,30},{7,31},{8,16},{9,... | collective-permute-start | bytes 344072 | tf_op jit(solution)/shard_map/ppermute | solution.py:15

commit v2 on v1

v2 whole, which is shorter than its diff:
```python
import jax
import jax.numpy as jnp
from jax import lax
from jax.experimental import pallas as pl
from jax.experimental.pallas import tpu as pltpu
from jax.sharding import PartitionSpec as P

E_WIN = 2
CAP = 16
NX = 4
NY = 8
BF = jnp.bfloat16
F32 = jnp.float32


def swap_x_outer(v):
    return lax.ppermute(v, "ep", [(i, (NX - 1 - i // NY) * NY + i % NY) for i in range(NX * NY)])


def swap_x_pair(v):
    return lax.ppermute(v, "ep", [(i, i ^ NY) for i in range(NX * NY)])


def shift_y(v, step):
    return lax.ppermute(
        v, "ep", [(i, i // NY * NY + (i + step) % NY) for i in range(NX * NY)]
    )


def mirror(v):
    n = lax.axis_size("pp")
    return lax.ppermute(v, "pp", [(i, n - 1 - i) for i in range(n)])


def dot(a, b, dims):
    return lax.dot_general(a, b, (dims, ((), ())), preferred_element_type=F32)


def plus(a, b):
    return (a.astype(F32) + b.astype(F32)).astype(BF)


def after(v, *others):
    return lax.optimization_barrier((v, *others))[0]


def pack_kernel(
    expert_ref, slot_hbm, gate_hbm, x_hbm, c_hbm, own_ref, other_ref, select_ref,
    slot_ref, gate_ref, x_ref, c_ref, sems,
):
    pairs = ((slot_hbm, slot_ref), (gate_hbm, gate_ref), (x_hbm, x_ref), (c_hbm, c_ref))
    copies = [pltpu.make_async_copy(src, dst, sems.at[i]) for i, (src, dst) in enumerate(pairs)]
    for copy in copies:
        copy.start()
    copies[0].wait()
    copies[1].wait()
    slots = slot_ref[...]
    n = slots.shape[1]
    expert = expert_ref[0]
    earlier = lax.broadcasted_iota(jnp.int32, (n, n), 0) < lax.broadcasted_iota(jnp.int32, (n, n), 1)
    earlier = jnp.where(earlier, 1.0, 0.0).astype(BF)
    want = lax.broadcasted_iota(jnp.int32, (CAP, n), 0).astype(F32)

    def pick(which):
        named = jnp.where(slots == which, 1.0, 0.0)
        named = jnp.broadcast_to(named, (CAP, n))
        rank = jnp.dot(named.astype(BF), earlier, preferred_element_type=F32)
        return jnp.where(rank == want, named, 0.0)

    select = jnp.concatenate([pick(expert), pick(1 - expert)], axis=0)
    gate = jnp.sum(select * (gate_ref[...].astype(F32) / 4096.0), axis=1, keepdims=True)
    select = select.astype(BF)
    select_ref[...] = select
    copies[2].wait()
    picked = jnp.dot(select, x_ref[...], preferred_element_type=F32).astype(BF)
    own_ref[:CAP] = picked[:CAP]
    other_ref[:CAP] = picked[CAP:]
    copies[3].wait()
    picked = (gate * jnp.dot(select, c_ref[...], preferred_element_type=F32)).astype(BF)
    own_ref[CAP:] = picked[:CAP]
    other_ref[CAP:] = picked[CAP:]


def pack(expert, slots, gates, block_x, block_cot):
    width = block_x.shape[1]
    vmem = pl.BlockSpec(memory_space=pltpu.VMEM)
    hbm = pl.BlockSpec(memory_space=pltpu.HBM)
    operands = (slots, gates, block_x, block_cot)
    return pl.pallas_call(
        pack_kernel,
        out_shape=(
            jax.ShapeDtypeStruct((2 * CAP, width), BF),
            jax.ShapeDtypeStruct((2 * CAP, width), BF),
            jax.ShapeDtypeStruct((E_WIN * CAP, block_x.shape[0]), BF),
        ),
        in_specs=[pl.BlockSpec(memory_space=pltpu.SMEM)] + [hbm] * 4,
        out_specs=(vmem, vmem, vmem),
        scratch_shapes=[pltpu.VMEM(v.shape, v.dtype) for v in operands]
        + [pltpu.SemaphoreType.DMA((4,))],
        compiler_params=pltpu.CompilerParams(vmem_limit_bytes=16 * 1024 * 1024),
    )(expert, *operands)


def shards(tokens, cotangent, expert_slot, gate_fixed, w_gate, w_up, w_down):
    block_x, block_cot = tokens[0], cotangent[0]
    width = block_x.shape[1]
    half = width // 2
    h = w_gate.shape[1]
    own_expert = lax.axis_index("ep") // (NX * NY // E_WIN)
    upper = lax.axis_index("pp") >= lax.axis_size("pp") // 2

    own, other, select = pack(
        own_expert.reshape(1).astype(jnp.int32), expert_slot, gate_fixed, block_x, block_cot
    )
    swapped = swap_x_outer(other)
    mine = jnp.concatenate([w_gate[0], w_up[0], w_down[0]], axis=0)
    theirs = swap_x_pair(mine)
    swapped = after(swapped, mine)
    chunk = jnp.concatenate([own, swapped], axis=0)

    right = left = chunk
    rights, lefts = [], []
    for step in range(4):
        if step == WEIGHT_STEP:
            right = after(right, theirs)
        if step == 3 and HALVES:
            right = shift_y(right[: 2 * CAP], 1)
            left = shift_y(left[2 * CAP :], -1)
            rights.append(jnp.concatenate([right, left], axis=0))
            break
        right = shift_y(right, 1)
        rights.append(right)
        if step < 3:
            left = shift_y(left, -1)
            lefts.append(left)
    near = [chunk] + lefts + rights[::-1]
    parts = [p.reshape(2, 2, CAP, width) for p in near]
    rows_x = jnp.concatenate([p[:, 0].reshape(2 * CAP, width) for p in parts], axis=0)
    rows_c = jnp.concatenate([p[:, 1].reshape(2 * CAP, width) for p in parts], axis=0)

    w_gu = jnp.concatenate([mine[: 2 * h], theirs[: 2 * h]], axis=0)
    w_d = jnp.concatenate([mine[2 * h :], theirs[2 * h :]], axis=0)
    pre = dot(rows_x, w_gu, ((1,), (1,)))
    gate_pre = jnp.concatenate([pre[:, :h], pre[:, 2 * h : 3 * h]], axis=1)
    up_pre = jnp.concatenate([pre[:, h : 2 * h], pre[:, 3 * h :]], axis=1)
    sig = jax.nn.sigmoid(gate_pre)
    activated = gate_pre * sig
    hidden = (activated * up_pre).astype(BF)
    hidden_cot = dot(rows_c, w_d, ((1,), (1,)))
    gate_cot = (hidden_cot * up_pre * (sig * (1.0 + gate_pre * (1.0 - sig)))).astype(BF)
    up_cot = (hidden_cot * activated).astype(BF)
    gu_cot = jnp.concatenate([gate_cot[:, :h], up_cot[:, :h], gate_cot[:, h:], up_cot[:, h:]], axis=1)

    def keep_send(v):
        low, high = v[:, :half], v[:, half:]
        return jnp.where(upper, high, low), jnp.where(upper, low, high)

    grad_d = dot(hidden, rows_c, ((0,), (0,))).astype(BF)
    keep_own_d, send_own_d = keep_send(grad_d[:h])
    keep_their_d, send_their_d = keep_send(grad_d[h:])
    got_send_d = swap_x_pair(send_their_d)
    grad_gu = dot(gu_cot, rows_x, ((0,), (0,))).astype(BF)
    keep_own, send_own = keep_send(grad_gu[: 2 * h])
    keep_their, send_their = keep_send(grad_gu[2 * h :])
    got_send = swap_x_pair(send_their)
    to_mirror_d = plus(send_own_d, got_send_d)
    from_mirror_d = mirror(to_mirror_d)
    to_mirror = plus(send_own, got_send)
    from_mirror = mirror(to_mirror)
    keep_their = jnp.concatenate([keep_their, keep_their_d], axis=0)
    keep_their = after(keep_their, to_mirror)
    got_keep = swap_x_pair(keep_their)

    if RS_MODE == "ring":
        partial = dot(after(gu_cot, send_their), w_gu, ((1,), (0,))).astype(BF)
        part = [partial[2 * CAP * i : 2 * CAP * (i + 1)] for i in range(NY)]
        go_right = shift_y(part[4], 1)
        go_left = shift_y(part[5], -1)
        go_right = shift_y(plus(part[3], go_right), 1)
        go_left = shift_y(plus(part[6], go_left), -1)
        go_right = plus(part[2], go_right)
        go_right = after(go_right, to_mirror)
        go_right = shift_y(go_right, 1)
        go_left = shift_y(plus(part[7], go_left), -1)
        go_right = shift_y(plus(part[1], go_right), 1)
        summed = (part[0].astype(F32) + go_right.astype(F32) + go_left.astype(F32)).astype(BF)
    else:
        y = lax.axis_index("ep") % NY
        turned = jnp.concatenate([gu_cot, gu_cot], axis=0)
        turned = lax.dynamic_slice_in_dim(turned, (NY - y) % NY * 2 * CAP, NY * 2 * CAP, 0)
        if X_FIRST:
            turned = after(turned, send_their_d if X_FIRST == 1 else send_their)
        partial = dot(turned, w_gu, ((1,), (0,))).astype(BF)
        groups = [[x * NY + k for k in range(NY)] for x in range(NX)]
        if RS_MODE == "a2a":
            got = lax.all_to_all(partial.reshape(NY, 2 * CAP, width), "ep", 0, 0, axis_index_groups=groups, tiled=True)
            summed = jnp.sum(got.astype(F32), axis=0).astype(BF)
        else:
            summed = lax.psum_scatter(partial, "ep", scatter_dimension=0, axis_index_groups=groups, tiled=True)
    back = swap_x_outer(summed[CAP:])
    branch = dot(select, jnp.concatenate([summed[:CAP], back], axis=0), ((0,), (0,)))
    input_grad = (block_cot.astype(F32) + branch).astype(BF)[None]
    if TIE_END:
        from_mirror = after(from_mirror, input_grad)

    def total(kept, near, far):
        return (kept.astype(F32) + near.astype(F32) + far.astype(F32)).astype(BF)[None]

    return (
        input_grad,
        total(keep_own[:h], got_keep[:h], from_mirror[:h]),
        total(keep_own[h:], got_keep[h : 2 * h], from_mirror[h:]),
        total(keep_own_d, got_keep[2 * h :], from_mirror_d),
    )


WEIGHT_STEP = 9
HALVES = True
RS_MODE = 'a2a'
X_FIRST = 1
TIE_END = False


def solution(mesh):
    wide = P("pp", "ep", None)
    flat = P("pp", "ep")
    return jax.shard_map(
        shards,
        mesh=mesh,
        in_specs=(wide, wide, flat, flat, wide, wide, wide),
        out_specs=(wide, wide, wide, wide),
        check_vma=False,
    )
```

time: 166 us -> 138 us (0.83)
  starting transfers between devices: 100 us -> 79.5 us
  waiting for transfers between devices: 41.5 us -> 34.2 us
  local copies, waits for them, and re-layouts: 8.95 us -> 5.51 us
  other arithmetic: 6.35 us -> 8.16 us
    ppermute x16 -> x8, starting transfers between devices: 56.5 us -> 29.2 us  [shift_y(): lax.ppermute(v, 'ep', [(i, i // NY * NY + (i + step) % NY) for i in range...]
    all_to_all x0 -> x1, starting transfers between devices: none -> 7.36 us  [shards(): lax.all_to_all(partial.reshape(NY, 2 * CAP, width), 'ep', 0, 0, axis_inde...]
    ppermute x1 -> x2, waiting for transfers between devices: 14.6 us -> 7.73 us  [mirror(): return lax.ppermute(v, 'pp', [(i, n - 1 - i) for i in range(n)])]
    ppermute x2, waiting for transfers between devices: 6.05 us -> 0.18 us  [swap_x_outer(): lax.ppermute(v, 'ep', [(i, (NX - 1 - i // NY) * NY + i % NY) for i in ran...]
    all_to_all x0 -> x1, waiting for transfers between devices: none -> 4.84 us  [shards(): lax.all_to_all(partial.reshape(NY, 2 * CAP, width), 'ep', 0, 0, axis_inde...]
    ppermute x1 -> x2, starting transfers between devices: 27 us -> 22.8 us  [mirror(): return lax.ppermute(v, 'pp', [(i, n - 1 - i) for i in range(n)])]
    ppermute x16 -> x8, waiting for transfers between devices: 17.2 us -> 21.4 us  [shift_y(): lax.ppermute(v, 'ep', [(i, i // NY * NY + (i + step) % NY) for i in range...]
    ppermute x3 -> x4, waiting for transfers between devices: 3.69 us -> 0.01 us  [swap_x_pair(): return lax.ppermute(v, 'ep', [(i, i ^ NY) for i in range(NX * NY)])]
  transfers between devices with their start and end apart: 22 -> 17, of which waited for: 13 -> 12; matrix products, arithmetic and copies ran while one was open for 7% -> 7% of each run, Pallas kernels for 0% -> 0%
where the time goes in v2:
time: 138 us; the launch traced here: 137 us
  starting transfers between devices  79.5 us (58%)
  waiting for transfers between devices  34.2 us (25%)
  other arithmetic  8.16 us (6%)
  matrix products  7.24 us (5%)
  local copies, waits for them, and re-layouts  5.51 us (4%)
    ppermute x8, starting transfers between devices, shift_y(): lax.ppermute(v, 'ep', [(i, i // NY * NY + (i + step) % NY) for i in range...  29.2 us
    ppermute x2, starting transfers between devices, mirror(): return lax.ppermute(v, 'pp', [(i, n - 1 - i) for i in range(n)])  22.8 us
    ppermute x8, waiting for transfers between devices, shift_y(): lax.ppermute(v, 'ep', [(i, i // NY * NY + (i + step) % NY) for i in range...  21.4 us
    ppermute x4, starting transfers between devices, swap_x_pair(): return lax.ppermute(v, 'ep', [(i, i ^ NY) for i in range(NX * NY)])  10.5 us
    ppermute x2, starting transfers between devices, swap_x_outer(): lax.ppermute(v, 'ep', [(i, (NX - 1 - i // NY) * NY + i % NY) for i in ran...  9.73 us
    ppermute x2, waiting for transfers between devices, mirror(): return lax.ppermute(v, 'pp', [(i, n - 1 - i) for i in range(n)])  7.73 us
    all_to_all x1, starting transfers between devices, shards(): lax.all_to_all(partial.reshape(NY, 2 * CAP, width), 'ep', 0, 0, axis_inde...  7.36 us
    dot_general x6, matrix products, dot(): return lax.dot_general(a, b, (dims, ((), ())), preferred_element_type=F32)  7.24 us
  transfers between devices with their start and end apart: 17, of which 12 were waited for; matrix products, arithmetic and copies ran while one was open for 7% of the time, Pallas kernels for 0%

profile of v2, /device:TPU:1, one launch (start us, length us, event | category | flops | bytes accessed | tf_op | source)
XLA Modules:
  0.0 137.0 jit_solution(14129362751835728204)
XLA Ops:
  0.6 0.0 copy-start
  0.7 1.2 copy-done
  1.8 1.2 copy-done.2
  3.0 0.7 copy-done.3
  3.7 0.7 copy-done.4
  4.3 1.2 shard_map.102
  5.5 5.2 %collective-permute-start = (bf16[32,3584]{1,0:T(8,128)(2,1)S(1)}, bf16[32,3584]{1,0:T(8,128)(2,1)S(1)}, u32[]{:S(2)}, u32[]{:S(2)}) collective-permute-start(bf16[32,3584]{1,0:T(8,128)(2,1)S(1)} %get-tuple-element.12), channel_id=1, source_target_pairs={{0,24},{1,25},{2,26},{3,27},{4,28},{5,29},{6,30},{7,31},{8,16},{9,... | collective-permute-start | bytes 688136 | tf_op jit(solution)/shard_map/ppermute | solution.py:17
  10.8 1.2 pad_maximum_fusion.1
  12.0 1.9 %collective-permute-start.9 = (bf16[192,3584]{1,0:T(8,128)(2,1)}, bf16[192,3584]{1,0:T(8,128)(2,1)S(1)}, u32[]{:S(2)}, u32[]{:S(2)}) collective-permute-start(bf16[192,3584]{1,0:T(8,128)(2,1)} %pad_maximum_fusion.1), channel_id=1, source_target_pairs={{0,8},{1,9},{2,10},{3,11},{4,12},{5,13},{6,14},{7,15},{8,0},{9,1},... | collective-permute-start | bytes 4128776 | tf_op jit(solution)/shard_map/ppermute | solution.py:21
  14.0 0.2 collective-permute-done
  14.2 5.0 %collective-permute-start.4 = (bf16[64,3584]{1,0:T(8,128)(2,1)S(1)}, bf16[64,3584]{1,0:T(8,128)(2,1)S(1)}, u32[]{:S(2)}, u32[]{:S(2)}) collective-permute-start(bf16[64,3584]{1,0:T(8,128)(2,1)S(1)} %constant_dynamic-update-slice_fusion), channel_id=1, source_target_pairs={{0,1},{1,2},{2,3},{3,4},{4,5},{5,6},{6,7},{7,0},{8,9},{9,10},{10,1... | collective-permute-start | bytes 1376264 | tf_op jit(solution)/shard_map/ppermute | solution.py:25
  19.2 3.8 %collective-permute-start.1 = (bf16[64,3584]{1,0:T(8,128)(2,1)S(1)}, bf16[64,3584]{1,0:T(8,128)(2,1)S(1)}, u32[]{:S(2)}, u32[]{:S(2)}) collective-permute-start(bf16[64,3584]{1,0:T(8,128)(2,1)S(1)} %constant_dynamic-update-slice_fusion), channel_id=1, source_target_pairs={{0,7},{1,0},{2,1},{3,2},{4,3},{5,4},{6,5},{7,6},{8,15},{9,8},{10,9... | collective-permute-start | bytes 1376264 | tf_op jit(solution)/shard_map/ppermute | solution.py:25
  23.1 3.8 %collective-permute-done.4 = bf16[64,3584]{1,0:T(8,128)(2,1)S(1)} collective-permute-done((bf16[64,3584]{1,0:T(8,128)(2,1)S(1)}, bf16[64,3584]{1,0:T(8,128)(2,1)S(1)}, u32[]{:S(2)}, u32[]{:S(2)}) %collective-permute-start.4) | collective-permute-done | bytes 458784 | tf_op jit(solution)/shard_map/ppermute | solution.py:25
  27.0 1.8 %collective-permute-done.1 = bf16[64,3584]{1,0:T(8,128)(2,1)S(1)} collective-permute-done((bf16[64,3584]{1,0:T(8,128)(2,1)S(1)}, bf16[64,3584]{1,0:T(8,128)(2,1)S(1)}, u32[]{:S(2)}, u32[]{:S(2)}) %collective-permute-start.1) | collective-permute-done | bytes 458784 | tf_op jit(solution)/shard_map/ppermute | solution.py:25
  28.8 5.7 %collective-permute-start.5 = (bf16[64,3584]{1,0:T(8,128)(2,1)S(1)}, bf16[64,3584]{1,0:T(8,128)(2,1)S(1)}, u32[]{:S(2)}, u32[]{:S(2)}) collective-permute-start(bf16[64,3584]{1,0:T(8,128)(2,1)S(1)} %collective-permute-done.4), channel_id=1, source_target_pairs={{0,1},{1,2},{2,3},{3,4},{4,5},{5,6},{6,7},{7,0},{8,9},{9,10},{10,1... | collective-permute-start | bytes 1376264 | tf_op jit(solution)/shard_map/ppermute | solution.py:25
  34.5 1.9 %collective-permute-start.2 = (bf16[64,3584]{1,0:T(8,128)(2,1)S(1)}, bf16[64,3584]{1,0:T(8,128)(2,1)S(1)}, u32[]{:S(2)}, u32[]{:S(2)}) collective-permute-start(bf16[64,3584]{1,0:T(8,128)(2,1)S(1)} %collective-permute-done.1), channel_id=1, source_target_pairs={{0,7},{1,0},{2,1},{3,2},{4,3},{5,4},{6,5},{7,6},{8,15},{9,8},{10,9... | collective-permute-start | bytes 1376264 | tf_op jit(solution)/shard_map/ppermute | solution.py:25
  36.5 5.1 %collective-permute-done.5 = bf16[64,3584]{1,0:T(8,128)(2,1)S(1)} collective-permute-done((bf16[64,3584]{1,0:T(8,128)(2,1)S(1)}, bf16[64,3584]{1,0:T(8,128)(2,1)S(1)}, u32[]{:S(2)}, u32[]{:S(2)}) %collective-permute-start.5) | collective-permute-done | bytes 458784 | tf_op jit(solution)/shard_map/ppermute | solution.py:25
  41.6 4.8 %collective-permute-start.6 = (bf16[64,3584]{1,0:T(8,128)(2,1)S(1)}, bf16[64,3584]{1,0:T(8,128)(2,1)S(1)}, u32[]{:S(2)}, u32[]{:S(2)}) collective-permute-start(bf16[64,3584]{1,0:T(8,128)(2,1)S(1)} %collective-permute-done.5), channel_id=1, source_target_pairs={{0,1},{1,2},{2,3},{3,4},{4,5},{5,6},{6,7},{7,0},{8,9},{9,10},{10,1... | collective-permute-start | bytes 1376264 | tf_op jit(solution)/shard_map/ppermute | solution.py:25
  46.4 0.7 collective-permute-done.2
  47.2 1.9 %collective-permute-start.3 = (bf16[64,3584]{1,0:T(8,128)(2,1)S(1)}, bf16[64,3584]{1,0:T(8,128)(2,1)S(1)}, u32[]{:S(2)}, u32[]{:S(2)}) collective-permute-start(bf16[64,3584]{1,0:T(8,128)(2,1)S(1)} %collective-permute-done.2), channel_id=1, source_target_pairs={{0,7},{1,0},{2,1},{3,2},{4,3},{5,4},{6,5},{7,6},{8,15},{9,8},{10,9... | collective-permute-start | bytes 1376264 | tf_op jit(solution)/shard_map/ppermute | solution.py:25
  49.2 0.0 collective-permute-done.9
  49.2 0.0 copy-start.6
  49.2 0.1 slice.213
  49.3 3.5 %collective-permute-done.6 = bf16[64,3584]{1,0:T(8,128)(2,1)S(1)} collective-permute-done((bf16[64,3584]{1,0:T(8,128)(2,1)S(1)}, bf16[64,3584]{1,0:T(8,128)(2,1)S(1)}, u32[]{:S(2)}, u32[]{:S(2)}) %collective-permute-start.6) | collective-permute-done | bytes 458784 | tf_op jit(solution)/shard_map/ppermute | solution.py:25
  52.8 4.1 %collective-permute-start.7 = (bf16[32,3584]{1,0:T(8,128)(2,1)S(1)}, bf16[32,3584]{1,0:T(8,128)(2,1)S(1)}, u32[]{:S(2)}, u32[]{:S(2)}) collective-permute-start(bf16[32,3584]{1,0:T(8,128)(2,1)S(1)} %slice.198), channel_id=1, source_target_pairs={{0,1},{1,2},{2,3},{3,4},{4,5},{5,6},{6,7},{7,0},{8,9},{9,10},{10,1... | collective-permute-start | bytes 688136 | tf_op jit(solution)/shard_map/ppermute | solution.py:25
  57.0 1.4 %collective-permute-done.3 = bf16[64,3584]{1,0:T(8,128)(2,1)S(1)} collective-permute-done((bf16[64,3584]{1,0:T(8,128)(2,1)S(1)}, bf16[64,3584]{1,0:T(8,128)(2,1)S(1)}, u32[]{:S(2)}, u32[]{:S(2)}) %collective-permute-start.3) | collective-permute-done | bytes 458784 | tf_op jit(solution)/shard_map/ppermute | solution.py:25
  58.4 1.9 %collective-permute-start.8 = (bf16[32,3584]{1,0:T(8,128)(2,1)S(1)}, bf16[32,3584]{1,0:T(8,128)(2,1)S(1)}, u32[]{:S(2)}, u32[]{:S(2)}) collective-permute-start(bf16[32,3584]{1,0:T(8,128)(2,1)S(1)} %slice.199), channel_id=1, source_target_pairs={{0,7},{1,0},{2,1},{3,2},{4,3},{5,4},{6,5},{7,6},{8,15},{9,8},{10,9... | collective-permute-start | bytes 688136 | tf_op jit(solution)/shard_map/ppermute | solution.py:25
  60.4 0.0 copy-start.10
  60.4 0.3 collective-permute-done.7
  60.8 4.7 %collective-permute-done.8 = bf16[32,3584]{1,0:T(8,128)(2,1)S(1)} collective-permute-done((bf16[32,3584]{1,0:T(8,128)(2,1)S(1)}, bf16[32,3584]{1,0:T(8,128)(2,1)S(1)}, u32[]{:S(2)}, u32[]{:S(2)}) %collective-permute-start.8) | collective-permute-done | bytes 229408 | tf_op jit(solution)/shard_map/ppermute | solution.py:25
  65.7 0.7 fusion.6
  66.3 0.6 copy-done.5
  67.0 0.0 slice-start
  67.0 0.4 convolution_convert_fusion.2
  67.5 0.5 slice-done
  68.0 0.7 multiply_convert_fusion.1
  68.7 0.0 copy-start.11
  68.8 0.7 broadcast_select_fusion.3
  69.5 0.7 fusion.16
  70.1 1.9 %convolution_convert_fusion.1 = bf16[256,3584]{1,0:T(8,128)(2,1)} fusion(bf16[256,256]{0,1:T(8,128)(2,1)S(1)} %fusion.16, bf16[128,3584]{1,0:T(8,128)(2,1)S(1)} %slice.213, bf16[64,3584]{1,0:T(8,128)(2,1)S(1)} %bitcast.77, bf16[64,3584]{1,0:T(8,128)(2,1)S(1)} %bitcast.80), kind=kOutput, calls=%fused_computation.1 | convolution fusion | flops 476184576 | bytes 3801088 | tf_op jit(solution)/shard_map/dot_general | solution.py:36
  72.1 0.0 copy-done.11
  72.1 7.4 %all-to-all-start = ((bf16[8,32,3584]{2,1,0:T(8,128)(2,1)}), bf16[8,32,3584]{2,1,0:T(8,128)(2,1)S(1)}, u32[]{:S(2)}, u32[]{:S(2)}) async-start(bf16[8,32,3584]{2,1,0:T(8,128)(2,1)} %bitcast.48), calls=%async_computation | async-start | bytes 3670016 | tf_op jit(solution)/shard_map/all_to_all | solution.py:196
  79.5 1.9 %collective-permute-start.14 = (bf16[64,1792]{1,0:T(8,128)(2,1)}, bf16[64,1792]{1,0:T(8,128)(2,1)S(1)}, u32[]{:S(2)}, u32[]{:S(2)}) collective-permute-start(bf16[64,1792]{1,0:T(8,128)(2,1)} %get-tuple-element.22), channel_id=1, source_target_pairs={{0,8},{1,9},{2,10},{3,11},{4,12},{5,13},{6,14},{7,15},{8,0},{9,1},... | collective-permute-start | bytes 688136 | tf_op jit(solution)/shard_map/ppermute | solution.py:21
  81.4 2.1 %convolution_convert_fusion = bf16[256,3584]{1,0:T(8,128)(2,1)S(1)} fusion(bf16[256,3584]{1,0:T(8,128)(2,1)} %copy-done.5, bf16[256,64]{0,1:T(8,128)(2,1)S(1)} %get-tuple-element.48, bf16[256,64]{0,1:T(8,128)(2,1)S(1)} %copy-done.12, bf16[256,64]{0,1:T(8,128)(2,1)S(1)} %get-tuple-element.49, bf16[256,64]{0,1:T(8,128)(2,1)S(1)} %get-tuple-element.52), kind=kOutput, calls=%fused_computation | convolution fusion | flops 471203840 | bytes 3801088 | tf_op jit(solution)/shard_map/dot_general | solution.py:36
  83.5 0.1 broadcast_select_fusion.2
  83.6 3.4 %collective-permute-start.11 = (bf16[128,1792]{1,0:T(8,128)(2,1)S(1)}, bf16[128,1792]{1,0:T(8,128)(2,1)S(1)}, u32[]{:S(2)}, u32[]{:S(2)}) collective-permute-start(bf16[128,1792]{1,0:T(8,128)(2,1)S(1)} %get-tuple-element.18), channel_id=1, source_target_pairs={{0,8},{1,9},{2,10},{3,11},{4,12},{5,13},{6,14},{7,15},{8,0},{9,1},... | collective-permute-start | bytes 1376264 | tf_op jit(solution)/shard_map/ppermute | solution.py:21
  87.0 0.9 pad_maximum_fusion.4
  87.9 0.0 collective-permute-done.14
  87.9 0.8 add_convert_fusion.2
  88.7 18.6 %collective-permute-start.15 = (bf16[64,1792]{1,0:T(8,128)(2,1)}, bf16[64,1792]{1,0:T(8,128)(2,1)}, u32[]{:S(2)}, u32[]{:S(2)}) collective-permute-start(bf16[64,1792]{1,0:T(8,128)(2,1)} %add_convert_fusion.2), channel_id=1, source_target_pairs={{0,480},{32,448},{64,416},{96,384},{128,352},{160,320},{192,288},{... | collective-permute-start | bytes 688136 | tf_op jit(solution)/shard_map/ppermute | solution.py:32
  107.3 0.0 collective-permute-done.11
  107.3 1.0 add_convert_fusion
  108.3 4.1 %collective-permute-start.13 = (bf16[128,1792]{1,0:T(8,128)(2,1)}, bf16[128,1792]{1,0:T(8,128)(2,1)}, u32[]{:S(2)}, u32[]{:S(2)}) collective-permute-start(bf16[128,1792]{1,0:T(8,128)(2,1)} %add_convert_fusion), channel_id=1, source_target_pairs={{0,480},{32,448},{64,416},{96,384},{128,352},{160,320},{192,288},{... | collective-permute-start | bytes 1376264 | tf_op jit(solution)/shard_map/ppermute | solution.py:32
  112.4 3.3 %collective-permute-start.12 = (bf16[192,1792]{1,0:T(8,128)(2,1)}, bf16[192,1792]{1,0:T(8,128)(2,1)}, u32[]{:S(2)}, u32[]{:S(2)}) collective-permute-start(bf16[192,1792]{1,0:T(8,128)(2,1)} %pad_maximum_fusion.4), channel_id=1, source_target_pairs={{0,8},{1,9},{2,10},{3,11},{4,12},{5,13},{6,14},{7,15},{8,0},{9,1},... | collective-permute-start | bytes 2064392 | tf_op jit(solution)/shard_map/ppermute | solution.py:21
  115.8 4.8 %all-to-all-done = bf16[8,32,3584]{2,1,0:T(8,128)(2,1)S(1)} async-done(((bf16[8,32,3584]{2,1,0:T(8,128)(2,1)}), bf16[8,32,3584]{2,1,0:T(8,128)(2,1)S(1)}, u32[]{:S(2)}, u32[]{:S(2)}) %all-to-all-start) | async-done | bytes 1835040 | tf_op jit(solution)/shard_map/all_to_all | solution.py:196
  120.6 0.3 reduce_sum.12
  120.9 0.0 copy-start.1
  120.9 4.5 %collective-permute-start.10 = (bf16[16,3584]{1,0:T(8,128)(2,1)S(1)}, bf16[16,3584]{1,0:T(8,128)(2,1)S(1)}, u32[]{:S(2)}, u32[]{:S(2)}) collective-permute-start(bf16[16,3584]{1,0:T(8,128)(2,1)S(1)} %get-tuple-element.47), channel_id=1, source_target_pairs={{0,24},{1,25},{2,26},{3,27},{4,28},{5,29},{6,30},{7,31},{8,16},{9,... | collective-permute-start | bytes 344072 | tf_op jit(solution)/shard_map/ppermute | solution.py:17
  125.4 0.9 collective-permute-done.15
  126.3 6.9 %collective-permute-done.13 = bf16[128,1792]{1,0:T(8,128)(2,1)} collective-permute-done((bf16[128,1792]{1,0:T(8,128)(2,1)}, bf16[128,1792]{1,0:T(8,128)(2,1)}, u32[]{:S(2)}, u32[]{:S(2)}) %collective-permute-start.13) | collective-permute-done | bytes 458784 | tf_op jit(solution)/shard_map/ppermute | solution.py:32
  133.2 0.0 collective-permute-done.12
  133.2 2.5 %fusion.8 = (bf16[1,64,1792]{2,1,0:T(8,128)(2,1)}, bf16[1,64,1792]{2,1,0:T(8,128)(2,1)}, bf16[1,64,1792]{2,1,0:T(8,128)(2,1)}) fusion(bf16[128,1792]{1,0:T(8,128)(2,1)} %collective-permute-done.13, bf16[192,1792]{1,0:T(8,128)(2,1)} %collective-permute-done.12, bf16[128,1792]{1,0:T(8,128)(2,1)S(1)} %get-tuple-element.16, ...), kind=kLoop, calls=%fused_computation.32 | loop fusion | flops 2179072 | bytes 2981889 | tf_op jit(solution)/shard_map/broadcast_in_dim | solution.py:207
  135.7 0.0 collective-permute-done.10
  135.7 1.3 fusion.1
  (47 shorter events, 0.7 us)
Async XLA Ops:
  0.6 1.2 copy-start
  1.8 1.2 copy-start.2
  3.0 0.7 copy-start.3
  3.7 0.7 copy-start.4
  4.3 6.5 %copy-start.7 = (bf16[1,64,3584]{2,1,0:T(8,128)(2,1)S(1)}, bf16[1,64,3584]{2,1,0:T(8,128)(2,1)}, u32[]{:S(2)}) copy-start(bf16[1,64,3584]{2,1,0:T(8,128)(2,1)} %param.13) | copy-start | bytes 1376260
  4.3 6.5 %copy-start.8 = (bf16[1,64,3584]{2,1,0:T(8,128)(2,1)S(1)}, bf16[1,64,3584]{2,1,0:T(8,128)(2,1)}, u32[]{:S(2)}) copy-start(bf16[1,64,3584]{2,1,0:T(8,128)(2,1)} %param.12) | copy-start | bytes 1376260
  4.3 6.5 %copy-start.9 = (bf16[1,64,3584]{2,1,0:T(8,128)(2,1)S(1)}, bf16[1,64,3584]{2,1,0:T(8,128)(2,1)}, u32[]{:S(2)}) copy-start(bf16[1,64,3584]{2,1,0:T(8,128)(2,1)} %param.11) | copy-start | bytes 1376260
  5.5 8.6 %collective-permute-start = (bf16[32,3584]{1,0:T(8,128)(2,1)S(1)}, bf16[32,3584]{1,0:T(8,128)(2,1)S(1)}, u32[]{:S(2)}, u32[]{:S(2)}) collective-permute-start(bf16[32,3584]{1,0:T(8,128)(2,1)S(1)} %get-tuple-element.12), channel_id=1, source_target_pairs={{0,24},{1,25},{2,26},{3,27},{4,28},{5,29},{6,30},{7,31},{8,16},{9,... | collective-permute-start | bytes 688136 | tf_op jit(solution)/shard_map/ppermute | solution.py:17
  12.0 37.1 %collective-permute-start.9 = (bf16[192,3584]{1,0:T(8,128)(2,1)}, bf16[192,3584]{1,0:T(8,128)(2,1)S(1)}, u32[]{:S(2)}, u32[]{:S(2)}) collective-permute-start(bf16[192,3584]{1,0:T(8,128)(2,1)} %pad_maximum_fusion.1), channel_id=1, source_target_pairs={{0,8},{1,9},{2,10},{3,11},{4,12},{5,13},{6,14},{7,15},{8,0},{9,1},... | collective-permute-start | bytes 4128776 | tf_op jit(solution)/shard_map/ppermute | solution.py:21
  14.2 12.7 %collective-permute-start.4 = (bf16[64,3584]{1,0:T(8,128)(2,1)S(1)}, bf16[64,3584]{1,0:T(8,128)(2,1)S(1)}, u32[]{:S(2)}, u32[]{:S(2)}) collective-permute-start(bf16[64,3584]{1,0:T(8,128)(2,1)S(1)} %constant_dynamic-update-slice_fusion), channel_id=1, source_target_pairs={{0,1},{1,2},{2,3},{3,4},{4,5},{5,6},{6,7},{7,0},{8,9},{9,10},{10,1... | collective-permute-start | bytes 1376264 | tf_op jit(solution)/shard_map/ppermute | solution.py:25
  19.2 9.6 %collective-permute-start.1 = (bf16[64,3584]{1,0:T(8,128)(2,1)S(1)}, bf16[64,3584]{1,0:T(8,128)(2,1)S(1)}, u32[]{:S(2)}, u32[]{:S(2)}) collective-permute-start(bf16[64,3584]{1,0:T(8,128)(2,1)S(1)} %constant_dynamic-update-slice_fusion), channel_id=1, source_target_pairs={{0,7},{1,0},{2,1},{3,2},{4,3},{5,4},{6,5},{7,6},{8,15},{9,8},{10,9... | collective-permute-start | bytes 1376264 | tf_op jit(solution)/shard_map/ppermute | solution.py:25
  28.8 12.7 %collective-permute-start.5 = (bf16[64,3584]{1,0:T(8,128)(2,1)S(1)}, bf16[64,3584]{1,0:T(8,128)(2,1)S(1)}, u32[]{:S(2)}, u32[]{:S(2)}) collective-permute-start(bf16[64,3584]{1,0:T(8,128)(2,1)S(1)} %collective-permute-done.4), channel_id=1, source_target_pairs={{0,1},{1,2},{2,3},{3,4},{4,5},{5,6},{6,7},{7,0},{8,9},{9,10},{10,1... | collective-permute-start | bytes 1376264 | tf_op jit(solution)/shard_map/ppermute | solution.py:25
  34.5 12.6 %collective-permute-start.2 = (bf16[64,3584]{1,0:T(8,128)(2,1)S(1)}, bf16[64,3584]{1,0:T(8,128)(2,1)S(1)}, u32[]{:S(2)}, u32[]{:S(2)}) collective-permute-start(bf16[64,3584]{1,0:T(8,128)(2,1)S(1)} %collective-permute-done.1), channel_id=1, source_target_pairs={{0,7},{1,0},{2,1},{3,2},{4,3},{5,4},{6,5},{7,6},{8,15},{9,8},{10,9... | collective-permute-start | bytes 1376264 | tf_op jit(solution)/shard_map/ppermute | solution.py:25
  41.6 11.2 %collective-permute-start.6 = (bf16[64,3584]{1,0:T(8,128)(2,1)S(1)}, bf16[64,3584]{1,0:T(8,128)(2,1)S(1)}, u32[]{:S(2)}, u32[]{:S(2)}) collective-permute-start(bf16[64,3584]{1,0:T(8,128)(2,1)S(1)} %collective-permute-done.5), channel_id=1, source_target_pairs={{0,1},{1,2},{2,3},{3,4},{4,5},{5,6},{6,7},{7,0},{8,9},{9,10},{10,1... | collective-permute-start | bytes 1376264 | tf_op jit(solution)/shard_map/ppermute | solution.py:25
  47.2 11.2 %collective-permute-start.3 = (bf16[64,3584]{1,0:T(8,128)(2,1)S(1)}, bf16[64,3584]{1,0:T(8,128)(2,1)S(1)}, u32[]{:S(2)}, u32[]{:S(2)}) collective-permute-start(bf16[64,3584]{1,0:T(8,128)(2,1)S(1)} %collective-permute-done.2), channel_id=1, source_target_pairs={{0,7},{1,0},{2,1},{3,2},{4,3},{5,4},{6,5},{7,6},{8,15},{9,8},{10,9... | collective-permute-start | bytes 1376264 | tf_op jit(solution)/shard_map/ppermute | solution.py:25
  49.2 7.8 %copy-start.6 = (bf16[192,3584]{1,0:T(8,128)(2,1)}, bf16[192,3584]{1,0:T(8,128)(2,1)S(1)}, u32[]{:S(2)}) copy-start(bf16[192,3584]{1,0:T(8,128)(2,1)S(1)} %collective-permute-done.9) | copy-start | bytes 4128772
  52.8 8.0 %collective-permute-start.7 = (bf16[32,3584]{1,0:T(8,128)(2,1)S(1)}, bf16[32,3584]{1,0:T(8,128)(2,1)S(1)}, u32[]{:S(2)}, u32[]{:S(2)}) collective-permute-start(bf16[32,3584]{1,0:T(8,128)(2,1)S(1)} %slice.198), channel_id=1, source_target_pairs={{0,1},{1,2},{2,3},{3,4},{4,5},{5,6},{6,7},{7,0},{8,9},{9,10},{10,1... | collective-permute-start | bytes 688136 | tf_op jit(solution)/shard_map/ppermute | solution.py:25
  58.4 7.1 %collective-permute-start.8 = (bf16[32,3584]{1,0:T(8,128)(2,1)S(1)}, bf16[32,3584]{1,0:T(8,128)(2,1)S(1)}, u32[]{:S(2)}, u32[]{:S(2)}) collective-permute-start(bf16[32,3584]{1,0:T(8,128)(2,1)S(1)} %slice.199), channel_id=1, source_target_pairs={{0,7},{1,0},{2,1},{3,2},{4,3},{5,4},{6,5},{7,6},{8,15},{9,8},{10,9... | collective-permute-start | bytes 688136 | tf_op jit(solution)/shard_map/ppermute | solution.py:25
  60.4 5.2 %copy-start.10 = (bf16[1,64,3584]{2,1,0:T(8,128)(2,1)S(1)}, bf16[1,64,3584]{2,1,0:T(8,128)(2,1)}, u32[]{:S(2)}) copy-start(bf16[1,64,3584]{2,1,0:T(8,128)(2,1)} %param.11) | copy-start | bytes 1376260
  65.6 1.2 copy-start.5
  67.0 1.0 slice-start
  68.7 3.3 %copy-start.11 = (bf16[256,64]{0,1:T(8,128)(2,1)}, bf16[256,64]{0,1:T(8,128)(2,1)S(1)}, u32[]{:S(2)}) copy-start(bf16[256,64]{0,1:T(8,128)(2,1)S(1)} %get-tuple-element.53) | copy-start | bytes 98308
  72.1 9.3 %copy-start.12 = (bf16[256,64]{0,1:T(8,128)(2,1)S(1)}, bf16[256,64]{0,1:T(8,128)(2,1)}, u32[]{:S(2)}) copy-start(bf16[256,64]{0,1:T(8,128)(2,1)} %copy-done.11) | copy-start | bytes 98308
  72.1 48.5 %all-to-all-start = ((bf16[8,32,3584]{2,1,0:T(8,128)(2,1)}), bf16[8,32,3584]{2,1,0:T(8,128)(2,1)S(1)}, u32[]{:S(2)}, u32[]{:S(2)}) async-start(bf16[8,32,3584]{2,1,0:T(8,128)(2,1)} %bitcast.48), calls=%async_computation | async-start | bytes 3670016 | tf_op jit(solution)/shard_map/all_to_all | solution.py:196
  79.5 8.5 %collective-permute-start.14 = (bf16[64,1792]{1,0:T(8,128)(2,1)}, bf16[64,1792]{1,0:T(8,128)(2,1)S(1)}, u32[]{:S(2)}, u32[]{:S(2)}) collective-permute-start(bf16[64,1792]{1,0:T(8,128)(2,1)} %get-tuple-element.22), channel_id=1, source_target_pairs={{0,8},{1,9},{2,10},{3,11},{4,12},{5,13},{6,14},{7,15},{8,0},{9,1},... | collective-permute-start | bytes 688136 | tf_op jit(solution)/shard_map/ppermute | solution.py:21
  83.6 23.7 %collective-permute-start.11 = (bf16[128,1792]{1,0:T(8,128)(2,1)S(1)}, bf16[128,1792]{1,0:T(8,128)(2,1)S(1)}, u32[]{:S(2)}, u32[]{:S(2)}) collective-permute-start(bf16[128,1792]{1,0:T(8,128)(2,1)S(1)} %get-tuple-element.18), channel_id=1, source_target_pairs={{0,8},{1,9},{2,10},{3,11},{4,12},{5,13},{6,14},{7,15},{8,0},{9,1},... | collective-permute-start | bytes 1376264 | tf_op jit(solution)/shard_map/ppermute | solution.py:21
  88.7 37.6 %collective-permute-start.15 = (bf16[64,1792]{1,0:T(8,128)(2,1)}, bf16[64,1792]{1,0:T(8,128)(2,1)}, u32[]{:S(2)}, u32[]{:S(2)}) collective-permute-start(bf16[64,1792]{1,0:T(8,128)(2,1)} %add_convert_fusion.2), channel_id=1, source_target_pairs={{0,480},{32,448},{64,416},{96,384},{128,352},{160,320},{192,288},{... | collective-permute-start | bytes 688136 | tf_op jit(solution)/shard_map/ppermute | solution.py:32
  108.3 24.9 %collective-permute-start.13 = (bf16[128,1792]{1,0:T(8,128)(2,1)}, bf16[128,1792]{1,0:T(8,128)(2,1)}, u32[]{:S(2)}, u32[]{:S(2)}) collective-permute-start(bf16[128,1792]{1,0:T(8,128)(2,1)} %add_convert_fusion), channel_id=1, source_target_pairs={{0,480},{32,448},{64,416},{96,384},{128,352},{160,320},{192,288},{... | collective-permute-start | bytes 1376264 | tf_op jit(solution)/shard_map/ppermute | solution.py:32
  112.4 20.8 %collective-permute-start.12 = (bf16[192,1792]{1,0:T(8,128)(2,1)}, bf16[192,1792]{1,0:T(8,128)(2,1)}, u32[]{:S(2)}, u32[]{:S(2)}) collective-permute-start(bf16[192,1792]{1,0:T(8,128)(2,1)} %pad_maximum_fusion.4), channel_id=1, source_target_pairs={{0,8},{1,9},{2,10},{3,11},{4,12},{5,13},{6,14},{7,15},{8,0},{9,1},... | collective-permute-start | bytes 2064392 | tf_op jit(solution)/shard_map/ppermute | solution.py:21
  120.9 14.8 %copy-start.1 = (bf16[1,128,3584]{2,1,0:T(8,128)(2,1)S(1)}, bf16[1,128,3584]{2,1,0:T(8,128)(2,1)}, u32[]{:S(2)}) copy-start(bf16[1,128,3584]{2,1,0:T(8,128)(2,1)} %param.8) | copy-start | bytes 2752516
  120.9 14.8 %collective-permute-start.10 = (bf16[16,3584]{1,0:T(8,128)(2,1)S(1)}, bf16[16,3584]{1,0:T(8,128)(2,1)S(1)}, u32[]{:S(2)}, u32[]{:S(2)}) collective-permute-start(bf16[16,3584]{1,0:T(8,128)(2,1)S(1)} %get-tuple-element.47), channel_id=1, source_target_pairs={{0,24},{1,25},{2,26},{3,27},{4,28},{5,29},{6,30},{7,31},{8,16},{9,... | collective-permute-start | bytes 344072 | tf_op jit(solution)/shard_map/ppermute | solution.py:17

commit v3 on v2

v3 whole, which is shorter than its diff:
```python
import jax
import jax.numpy as jnp
from jax import lax
from jax.experimental import pallas as pl
from jax.experimental.pallas import tpu as pltpu
from jax.sharding import PartitionSpec as P

E_WIN = 2
CAP = 16
NX = 4
NY = 8
BF = jnp.bfloat16
F32 = jnp.float32


def swap_x_outer(v):
    return lax.ppermute(v, "ep", [(i, (NX - 1 - i // NY) * NY + i % NY) for i in range(NX * NY)])


def swap_x_pair(v):
    return lax.ppermute(v, "ep", [(i, i ^ NY) for i in range(NX * NY)])


def shift_y(v, step):
    return lax.ppermute(
        v, "ep", [(i, i // NY * NY + (i + step) % NY) for i in range(NX * NY)]
    )


def mirror(v):
    n = lax.axis_size("pp")
    return lax.ppermute(v, "pp", [(i, n - 1 - i) for i in range(n)])


def dot(a, b, dims):
    return lax.dot_general(a, b, (dims, ((), ())), preferred_element_type=F32)


def plus(a, b):
    return (a.astype(F32) + b.astype(F32)).astype(BF)


def after(v, *others):
    return lax.optimization_barrier((v, *others))[0]


def pack_kernel(
    expert_ref, slot_hbm, gate_hbm, x_hbm, c_hbm, own_ref, other_ref, select_ref,
    slot_ref, gate_ref, x_ref, c_ref, sems,
):
    pairs = ((slot_hbm, slot_ref), (gate_hbm, gate_ref), (x_hbm, x_ref), (c_hbm, c_ref))
    copies = [pltpu.make_async_copy(src, dst, sems.at[i]) for i, (src, dst) in enumerate(pairs)]
    for copy in copies:
        copy.start()
    copies[0].wait()
    copies[1].wait()
    slots = slot_ref[...]
    n = slots.shape[1]
    expert = expert_ref[0]
    earlier = lax.broadcasted_iota(jnp.int32, (n, n), 0) < lax.broadcasted_iota(jnp.int32, (n, n), 1)
    earlier = jnp.where(earlier, 1.0, 0.0).astype(BF)
    want = lax.broadcasted_iota(jnp.int32, (CAP, n), 0).astype(F32)

    def pick(which):
        named = jnp.where(slots == which, 1.0, 0.0)
        named = jnp.broadcast_to(named, (CAP, n))
        rank = jnp.dot(named.astype(BF), earlier, preferred_element_type=F32)
        return jnp.where(rank == want, named, 0.0)

    mine, theirs = pick(expert), pick(1 - expert)
    first = jnp.where(expert == 0, mine, theirs)
    second = jnp.where(expert == 0, theirs, mine)
    select_ref[...] = jnp.concatenate([first, second], axis=0).astype(BF)
    select = jnp.concatenate([mine, theirs], axis=0)
    gate = jnp.sum(select * (gate_ref[...].astype(F32) / 4096.0), axis=1, keepdims=True)
    select = select.astype(BF)
    copies[2].wait()
    picked = jnp.dot(select, x_ref[...], preferred_element_type=F32).astype(BF)
    own_ref[:CAP] = picked[:CAP]
    other_ref[:CAP] = picked[CAP:]
    copies[3].wait()
    picked = (gate * jnp.dot(select, c_ref[...], preferred_element_type=F32)).astype(BF)
    own_ref[CAP:] = picked[:CAP]
    other_ref[CAP:] = picked[CAP:]


def pack(expert, slots, gates, block_x, block_cot):
    width = block_x.shape[1]
    vmem = pl.BlockSpec(memory_space=pltpu.VMEM)
    hbm = pl.BlockSpec(memory_space=pltpu.HBM)
    operands = (slots, gates, block_x, block_cot)
    return pl.pallas_call(
        pack_kernel,
        out_shape=(
            jax.ShapeDtypeStruct((2 * CAP, width), BF),
            jax.ShapeDtypeStruct((2 * CAP, width), BF),
            jax.ShapeDtypeStruct((E_WIN * CAP, block_x.shape[0]), BF),
        ),
        in_specs=[pl.BlockSpec(memory_space=pltpu.SMEM)] + [hbm] * 4,
        out_specs=(vmem, vmem, vmem),
        scratch_shapes=[pltpu.VMEM(v.shape, v.dtype) for v in operands]
        + [pltpu.SemaphoreType.DMA((4,))],
        compiler_params=pltpu.CompilerParams(vmem_limit_bytes=PACK_VMEM * 1024 * 1024),
    )(expert, *operands)


def expert_kernel(
    place_ref, x_ref, c_ref, mine_ref, theirs_ref,
    partial_ref, first_ref, second_ref, own_ref, their_keep_ref,
):
    h = mine_ref.shape[0] // 3
    rows, width = x_ref.shape
    half = width // 2
    y, expert, upper = place_ref[0], place_ref[1], place_ref[2]

    def both(k):
        return [mine_ref[k * h : (k + 1) * h], theirs_ref[k * h : (k + 1) * h]]

    w_gu = jnp.concatenate(both(0) + both(1), axis=0)
    pre = dot(x_ref[...], w_gu, ((1,), (1,)))
    gate_pre, up_pre = pre[:, : 2 * h], pre[:, 2 * h :]
    sig = 1.0 / (1.0 + jnp.exp(-gate_pre))
    activated = gate_pre * sig
    hidden = (activated * up_pre).astype(BF)
    hidden_cot = dot(c_ref[...], jnp.concatenate(both(2), axis=0), ((1,), (1,)))
    gate_cot = (hidden_cot * up_pre * (sig * (1.0 + gate_pre * (1.0 - sig)))).astype(BF)
    up_cot = (hidden_cot * activated).astype(BF)
    gu_cot = jnp.concatenate([gate_cot, up_cot], axis=1)

    to = lax.broadcasted_iota(jnp.int32, (rows, rows), 0)
    at = lax.broadcasted_iota(jnp.int32, (rows, rows), 1)
    side, block, rank = to // (NY * CAP), to // CAP % NY, to % CAP
    ring = (block - y + NY) % NY
    ring = sum(jnp.where(ring == r, ORDER.index(r), 0) for r in ORDER)
    source = ring * (2 * CAP) + jnp.where(side == expert, 0, CAP) + rank
    move = jnp.where(at == source, 1.0, 0.0).astype(BF)
    moved = dot(move, gu_cot, ((1,), (0,))).astype(BF)
    tile = half // TILES
    for k in range(2 * TILES):
        cols = slice(k * tile, (k + 1) * tile)
        partial_ref[:, cols] = dot(moved, w_gu[:, cols], ((1,), (0,))).astype(BF)

    for k in range(TILES):
        cols = slice(k * tile, (k + 1) * tile)
        for send in (True, False):
            start = (1 - upper if send else upper) * half + k * tile
            start = pl.multiple_of(start, 128)
            down = dot(hidden, c_ref[:, pl.ds(start, tile)], ((0,), (0,))).astype(BF)
            gu = dot(gu_cot, x_ref[:, pl.ds(start, tile)], ((0,), (0,))).astype(BF)
            if send:
                first_ref[:, cols] = down[h:]
                own_ref[2 * h : 3 * h, cols] = down[:h]
                second_ref[:h, cols] = gu[h : 2 * h]
                second_ref[h:, cols] = gu[3 * h :]
                own_ref[:h, cols] = gu[:h]
                own_ref[h : 2 * h, cols] = gu[2 * h : 3 * h]
            else:
                their_keep_ref[:h, cols] = gu[h : 2 * h]
                their_keep_ref[h : 2 * h, cols] = gu[3 * h :]
                their_keep_ref[2 * h :, cols] = down[h:]
                own_ref[3 * h : 4 * h, cols] = gu[:h]
                own_ref[4 * h : 5 * h, cols] = gu[2 * h : 3 * h]
                own_ref[5 * h :, cols] = down[:h]


def experts(place, rows_x, rows_c, mine, theirs):
    rows, width = rows_x.shape
    h, half = mine.shape[0] // 3, width // 2
    vmem = pl.BlockSpec(memory_space=pltpu.VMEM)
    shapes = [(rows, width), (h, half), (2 * h, half), (6 * h, half), (3 * h, half)]
    return pl.pallas_call(
        expert_kernel,
        out_shape=tuple(jax.ShapeDtypeStruct(v, BF) for v in shapes),
        in_specs=[pl.BlockSpec(memory_space=pltpu.SMEM)] + [vmem] * 4,
        out_specs=(vmem,) * len(shapes),
        compiler_params=pltpu.CompilerParams(vmem_limit_bytes=EXPERT_VMEM * 1024 * 1024),
        cost_estimate=pl.CostEstimate(flops=4 * 10**9, bytes_accessed=16 * 2**20, transcendentals=0),
    )(place, rows_x, rows_c, mine, theirs)


def add_kernel(a_ref, b_ref, out_ref):
    out_ref[...] = plus(a_ref[...], b_ref[...])


def add(a, b, at, cost):
    return pl.pallas_call(
        add_kernel,
        grid=(1,),
        out_shape=jax.ShapeDtypeStruct(b.shape, BF),
        in_specs=[pl.BlockSpec(b.shape, lambda i: (at, 0)), pl.BlockSpec(b.shape, lambda i: (0, 0))],
        out_specs=pl.BlockSpec(b.shape, lambda i: (0, 0)),
        compiler_params=pltpu.CompilerParams(vmem_limit_bytes=8 * 1024 * 1024),
        cost_estimate=pl.CostEstimate(flops=cost * 10**9, bytes_accessed=2**20, transcendentals=0),
    )(a, b)


def shards(tokens, cotangent, expert_slot, gate_fixed, w_gate, w_up, w_down):
    block_x, block_cot = tokens[0], cotangent[0]
    width = block_x.shape[1]
    half = width // 2
    h = w_gate.shape[1]
    own_expert = lax.axis_index("ep") // (NX * NY // E_WIN)
    upper = lax.axis_index("pp") >= lax.axis_size("pp") // 2

    own, other, select = pack(
        own_expert.reshape(1).astype(jnp.int32), expert_slot, gate_fixed, block_x, block_cot
    )
    swapped = swap_x_outer(other)
    mine = jnp.concatenate([w_gate[0], w_up[0], w_down[0]], axis=0)
    theirs = swap_x_pair(mine)
    swapped = after(swapped, mine)
    chunk = jnp.concatenate([own, swapped], axis=0)

    right = left = chunk
    rights, lefts = [], []
    for step in range(4):
        if step == WEIGHT_STEP:
            if WEIGHT_SIDE:
                left = after(left, theirs)
            else:
                right = after(right, theirs)
        if step == 3:
            right = shift_y(right[: RIGHT_ROWS * CAP], 1)
            left = shift_y(left[RIGHT_ROWS * CAP :], -1)
            rights.append(jnp.concatenate([right, left], axis=0))
            break
        right = shift_y(right, 1)
        rights.append(right)
        if step < 3:
            left = shift_y(left, -1)
            lefts.append(left)
    near = [chunk] + lefts + rights[::-1]
    near = [near[r] for r in ORDER]
    parts = [p.reshape(2, 2, CAP, width) for p in near]
    rows_x = jnp.concatenate([p[:, 0].reshape(2 * CAP, width) for p in parts], axis=0)
    rows_c = jnp.concatenate([p[:, 1].reshape(2 * CAP, width) for p in parts], axis=0)

    place = jnp.stack([lax.axis_index("ep") % NY, own_expert, upper.astype(jnp.int32)])
    partial, their_send_d, their_send, own, their_keep = experts(
        place.astype(jnp.int32), rows_x, rows_c, mine, theirs
    )

    got_send_d = swap_x_pair(their_send_d)
    got_send = swap_x_pair(their_send)
    from_mirror_d = mirror(add(own, got_send_d, 2, FIRST_COST))
    to_mirror = add(own, got_send, 0, SECOND_COST)
    from_mirror = mirror(to_mirror)
    if X_LAST == 1:
        their_keep = after(their_keep, to_mirror)
    if X_LAST == 2:
        their_keep = after(their_keep, from_mirror_d)
    got_keep = swap_x_pair(their_keep)

    groups = [[x * NY + k for x in pair for k in range(NY)] for pair in ((0, 3), (1, 2))]
    got = lax.all_to_all(
        partial.reshape(2 * NY, CAP, width), "ep", 0, 0, axis_index_groups=groups, tiled=True
    )
    summed = jnp.sum(got.reshape(2, NY, CAP, width).astype(F32), axis=1).astype(BF)
    branch = dot(select, summed.reshape(2 * CAP, width), ((0,), (0,)))
    input_grad = (block_cot.astype(F32) + branch).astype(BF)[None]
    own_keep = own[3 * h :]

    def total(kept, near, far):
        return (kept.astype(F32) + near.astype(F32) + far.astype(F32)).astype(BF)[None]

    return (
        input_grad,
        total(own_keep[:h], got_keep[:h], from_mirror[:h]),
        total(own_keep[h : 2 * h], got_keep[h : 2 * h], from_mirror[h:]),
        total(own_keep[2 * h :], got_keep[2 * h :], from_mirror_d),
    )


WEIGHT_STEP = 3
X_LAST = 1
TILES = 2
RIGHT_ROWS = 2
WEIGHT_SIDE = 0
ORDER = (4, 5, 3, 6, 2, 7, 1, 0)
FIRST_COST = 100
SECOND_COST = 100
EXPERT_VMEM = 16
PACK_VMEM = 60


def solution(mesh):
    wide = P("pp", "ep", None)
    flat = P("pp", "ep")
    return jax.shard_map(
        shards,
        mesh=mesh,
        in_specs=(wide, wide, flat, flat, wide, wide, wide),
        out_specs=(wide, wide, wide, wide),
        check_vma=False,
    )
```

time: 138 us -> 130 us (0.942)
  Pallas kernels: 1.21 us -> 7.37 us
  matrix products: 7.24 us -> 1.35 us
  other arithmetic: 8.16 us -> 2.96 us
  waiting for transfers between devices: 34.2 us -> 39.2 us
  starting transfers between devices: 79.5 us -> 74.7 us
  local copies, waits for them, and re-layouts: 5.51 us -> 2.46 us
    ppermute x2, waiting for transfers between devices: 7.73 us -> 17.6 us  [mirror(): return lax.ppermute(v, 'pp', [(i, n - 1 - i) for i in range(n)])]
    dot_general x6 -> x1, matrix products: 7.24 us -> 1.35 us  [dot(): return lax.dot_general(a, b, (dims, ((), ())), preferred_element_type=F32)]
    all_to_all x1, waiting for transfers between devices: 4.84 us -> 0.01 us  [shards(): lax.all_to_all(partial.reshape(2 * NY, CAP, width), 'ep', 0, 0, axis_inde...]
    pallas_call x0 -> x3, Pallas kernels: none -> 4.74 us  [the longest x1 4.57 us: experts(): pl.pallas_call(expert_kernel, out_shape=tuple((jax.ShapeDtypeStruct(v, BF...]
    ppermute x2 -> x1, starting transfers between devices: 9.73 us -> 5.35 us  [swap_x_outer(): lax.ppermute(v, 'ep', [(i, (NX - 1 - i // NY) * NY + i % NY) for i in ran...]
    unnamed x41 -> x35, local copies, waits for them, and re-layouts: 4.52 us -> 2.13 us
    convert_element_type x2 -> x0, other arithmetic: 1.73 us -> none  [plus(): return (a.astype(F32) + b.astype(F32)).astype(BF)]
    concatenate x2 -> x0, other arithmetic: 1.55 us -> none  [the longest x1 0.9 us: shards(): keep_their = jnp.concatenate([keep_their, keep_their_d], axis=0)]
  transfers between devices with their start and end apart: 17 -> 16, of which waited for: 12 -> 7; matrix products, arithmetic and copies ran while one was open for 7% -> 1% of each run, Pallas kernels for 0% -> 0%
where the time goes in v3:
time: 130 us; the launch traced here: 129 us
  starting transfers between devices  74.7 us (57%)
  waiting for transfers between devices  39.2 us (30%)
  Pallas kernels  7.37 us (6%)
  other arithmetic  2.96 us (2%)
  local copies, waits for them, and re-layouts  2.46 us (2%)
  matrix products  1.35 us (1%)
    ppermute x8, starting transfers between devices, shift_y(): lax.ppermute(v, 'ep', [(i, i // NY * NY + (i + step) % NY) for i in range...  30.5 us
    ppermute x2, starting transfers between devices, mirror(): return lax.ppermute(v, 'pp', [(i, n - 1 - i) for i in range(n)])  22.3 us
    ppermute x8, waiting for transfers between devices, shift_y(): lax.ppermute(v, 'ep', [(i, i // NY * NY + (i + step) % NY) for i in range...  20.2 us
    ppermute x2, waiting for transfers between devices, mirror(): return lax.ppermute(v, 'pp', [(i, n - 1 - i) for i in range(n)])  17.6 us
    ppermute x4, starting transfers between devices, swap_x_pair(): return lax.ppermute(v, 'ep', [(i, i ^ NY) for i in range(NX * NY)])  10.3 us
    all_to_all x1, starting transfers between devices, shards(): lax.all_to_all(partial.reshape(2 * NY, CAP, width), 'ep', 0, 0, axis_inde...  6.29 us
    ppermute x1, starting transfers between devices, swap_x_outer(): lax.ppermute(v, 'ep', [(i, (NX - 1 - i // NY) * NY + i % NY) for i in ran...  5.35 us
    pallas_call x1, Pallas kernels, experts(): pl.pallas_call(expert_kernel, out_shape=tuple((jax.ShapeDtypeStruct(v, BF...  4.57 us
  transfers between devices with their start and end apart: 16, of which 7 were waited for; matrix products, arithmetic and copies ran while one was open for 1% of the time, Pallas kernels for 0%

profile of v3, /device:TPU:1, one launch (start us, length us, event | category | flops | bytes accessed | tf_op | source)
XLA Modules:
  0.0 129.3 jit_solution(9126540720462041336)
XLA Ops:
  0.6 0.0 copy-start.5
  0.6 0.0 copy-start.6
  0.7 0.0 copy-start.7
  0.7 2.6 %shard_map.102 = (bf16[32,3584]{1,0:T(8,128)(2,1)}, bf16[32,3584]{1,0:T(8,128)(2,1)}, bf16[32,128]{1,0:T(8,128)(2,1)}) custom-call(s32[1]{0:T(128)} %bitcast.1.expert_ref, s32[1,128]{1,0:T(1,128)} %slot_hbm.1, s32[1,128]{1,0:T(1,128)} %gate_hbm.1, bf16[128,3584]{1,0:T(8,128)(2,1)} %bitcast.100, bf16[128,3584]{1,0:T(8,128)(2,1)} %bitcast.79), custom_call_target="tpu_custom_call" | custom-call | tf_op jit(solution)/shard_map/pallas_call | solution.py:92
  3.3 0.0 copy-start.8
  3.3 5.4 %collective-permute-start = (bf16[32,3584]{1,0:T(8,128)(2,1)}, bf16[32,3584]{1,0:T(8,128)(2,1)S(1)}, u32[]{:S(2)}, u32[]{:S(2)}) collective-permute-start(bf16[32,3584]{1,0:T(8,128)(2,1)} %get-tuple-element.17), channel_id=1, source_target_pairs={{0,24},{1,25},{2,26},{3,27},{4,28},{5,29},{6,30},{7,31},{8,16},{9,... | collective-permute-start | bytes 688136 | tf_op jit(solution)/shard_map/ppermute | solution.py:17
  8.7 0.0 copy-done.5
  8.7 0.0 copy-done.6
  8.7 0.0 copy-done.7
  8.7 0.1 pad_maximum_fusion.mine_ref
  8.8 1.9 %collective-permute-start.4 = (bf16[192,3584]{1,0:T(8,128)(2,1)S(1)}, bf16[192,3584]{1,0:T(8,128)(2,1)S(1)}, u32[]{:S(2)}, u32[]{:S(2)}) collective-permute-start(bf16[192,3584]{1,0:T(8,128)(2,1)S(1)} %pad_maximum_fusion.mine_ref), channel_id=1, source_target_pairs={{0,8},{1,9},{2,10},{3,11},{4,12},{5,13},{6,14},{7,15},{8,0},{9,1},... | collective-permute-start | bytes 4128776 | tf_op jit(solution)/shard_map/ppermute | solution.py:21
  10.8 0.0 copy-done.8
  10.8 0.1 pad_add_fusion.place_ref
  10.9 1.4 %collective-permute-done = bf16[32,3584]{1,0:T(8,128)(2,1)S(1)} collective-permute-done((bf16[32,3584]{1,0:T(8,128)(2,1)}, bf16[32,3584]{1,0:T(8,128)(2,1)S(1)}, u32[]{:S(2)}, u32[]{:S(2)}) %collective-permute-start) | collective-permute-done | bytes 229408 | tf_op jit(solution)/shard_map/ppermute | solution.py:17
  12.3 6.9 %collective-permute-start.6 = (bf16[64,3584]{1,0:T(8,128)(2,1)S(1)}, bf16[64,3584]{1,0:T(8,128)(2,1)S(1)}, u32[]{:S(2)}, u32[]{:S(2)}) collective-permute-start(bf16[64,3584]{1,0:T(8,128)(2,1)S(1)} %constant_dynamic-update-slice_fusion), channel_id=1, source_target_pairs={{0,7},{1,0},{2,1},{3,2},{4,3},{5,4},{6,5},{7,6},{8,15},{9,8},{10,9... | collective-permute-start | bytes 1376264 | tf_op jit(solution)/shard_map/ppermute | solution.py:25
  19.2 1.9 %collective-permute-start.1 = (bf16[64,3584]{1,0:T(8,128)(2,1)S(1)}, bf16[64,3584]{1,0:T(8,128)(2,1)S(1)}, u32[]{:S(2)}, u32[]{:S(2)}) collective-permute-start(bf16[64,3584]{1,0:T(8,128)(2,1)S(1)} %constant_dynamic-update-slice_fusion), channel_id=1, source_target_pairs={{0,1},{1,2},{2,3},{3,4},{4,5},{5,6},{6,7},{7,0},{8,9},{9,10},{10,1... | collective-permute-start | bytes 1376264 | tf_op jit(solution)/shard_map/ppermute | solution.py:25
  21.2 5.7 %collective-permute-done.6 = bf16[64,3584]{1,0:T(8,128)(2,1)S(1)} collective-permute-done((bf16[64,3584]{1,0:T(8,128)(2,1)S(1)}, bf16[64,3584]{1,0:T(8,128)(2,1)S(1)}, u32[]{:S(2)}, u32[]{:S(2)}) %collective-permute-start.6) | collective-permute-done | bytes 458784 | tf_op jit(solution)/shard_map/ppermute | solution.py:25
  26.8 5.3 %collective-permute-start.7 = (bf16[64,3584]{1,0:T(8,128)(2,1)S(1)}, bf16[64,3584]{1,0:T(8,128)(2,1)S(1)}, u32[]{:S(2)}, u32[]{:S(2)}) collective-permute-start(bf16[64,3584]{1,0:T(8,128)(2,1)S(1)} %collective-permute-done.6), channel_id=1, source_target_pairs={{0,7},{1,0},{2,1},{3,2},{4,3},{5,4},{6,5},{7,6},{8,15},{9,8},{10,9... | collective-permute-start | bytes 1376264 | tf_op jit(solution)/shard_map/ppermute | solution.py:25
  32.2 0.0 collective-permute-done.1
  32.2 1.9 %collective-permute-start.2 = (bf16[64,3584]{1,0:T(8,128)(2,1)S(1)}, bf16[64,3584]{1,0:T(8,128)(2,1)S(1)}, u32[]{:S(2)}, u32[]{:S(2)}) collective-permute-start(bf16[64,3584]{1,0:T(8,128)(2,1)S(1)} %collective-permute-done.1), channel_id=1, source_target_pairs={{0,1},{1,2},{2,3},{3,4},{4,5},{5,6},{6,7},{7,0},{8,9},{9,10},{10,1... | collective-permute-start | bytes 1376264 | tf_op jit(solution)/shard_map/ppermute | solution.py:25
  34.2 4.7 %collective-permute-done.7 = bf16[64,3584]{1,0:T(8,128)(2,1)S(1)} collective-permute-done((bf16[64,3584]{1,0:T(8,128)(2,1)S(1)}, bf16[64,3584]{1,0:T(8,128)(2,1)S(1)}, u32[]{:S(2)}, u32[]{:S(2)}) %collective-permute-start.7) | collective-permute-done | bytes 458784 | tf_op jit(solution)/shard_map/ppermute | solution.py:25
  38.9 5.3 %collective-permute-start.8 = (bf16[64,3584]{1,0:T(8,128)(2,1)S(1)}, bf16[64,3584]{1,0:T(8,128)(2,1)S(1)}, u32[]{:S(2)}, u32[]{:S(2)}) collective-permute-start(bf16[64,3584]{1,0:T(8,128)(2,1)S(1)} %collective-permute-done.7), channel_id=1, source_target_pairs={{0,7},{1,0},{2,1},{3,2},{4,3},{5,4},{6,5},{7,6},{8,15},{9,8},{10,9... | collective-permute-start | bytes 1376264 | tf_op jit(solution)/shard_map/ppermute | solution.py:25
  44.2 0.0 collective-permute-done.2
  44.2 1.9 %collective-permute-start.3 = (bf16[64,3584]{1,0:T(8,128)(2,1)S(1)}, bf16[64,3584]{1,0:T(8,128)(2,1)S(1)}, u32[]{:S(2)}, u32[]{:S(2)}) collective-permute-start(bf16[64,3584]{1,0:T(8,128)(2,1)S(1)} %collective-permute-done.2), channel_id=1, source_target_pairs={{0,1},{1,2},{2,3},{3,4},{4,5},{5,6},{6,7},{7,0},{8,9},{9,10},{10,1... | collective-permute-start | bytes 1376264 | tf_op jit(solution)/shard_map/ppermute | solution.py:25
  46.2 3.8 %collective-permute-done.8 = bf16[64,3584]{1,0:T(8,128)(2,1)S(1)} collective-permute-done((bf16[64,3584]{1,0:T(8,128)(2,1)S(1)}, bf16[64,3584]{1,0:T(8,128)(2,1)S(1)}, u32[]{:S(2)}, u32[]{:S(2)}) %collective-permute-start.8) | collective-permute-done | bytes 458784 | tf_op jit(solution)/shard_map/ppermute | solution.py:25
  50.0 5.3 %collective-permute-start.9 = (bf16[32,3584]{1,0:T(8,128)(2,1)S(1)}, bf16[32,3584]{1,0:T(8,128)(2,1)S(1)}, u32[]{:S(2)}, u32[]{:S(2)}) collective-permute-start(bf16[32,3584]{1,0:T(8,128)(2,1)S(1)} %slice.108), channel_id=1, source_target_pairs={{0,7},{1,0},{2,1},{3,2},{4,3},{5,4},{6,5},{7,6},{8,15},{9,8},{10,9... | collective-permute-start | bytes 688136 | tf_op jit(solution)/shard_map/ppermute | solution.py:25
  55.4 0.0 collective-permute-done.4.theirs_ref
  55.4 0.0 copy-start
  55.4 0.0 collective-permute-done.3
  55.4 1.9 %collective-permute-start.5 = (bf16[32,3584]{1,0:T(8,128)(2,1)S(1)}, bf16[32,3584]{1,0:T(8,128)(2,1)S(1)}, u32[]{:S(2)}, u32[]{:S(2)}) collective-permute-start(bf16[32,3584]{1,0:T(8,128)(2,1)S(1)} %slice.82), channel_id=1, source_target_pairs={{0,1},{1,2},{2,3},{3,4},{4,5},{5,6},{6,7},{7,0},{8,9},{9,10},{10,1... | collective-permute-start | bytes 688136 | tf_op jit(solution)/shard_map/ppermute | solution.py:25
  57.4 0.9 collective-permute-done.9
  58.3 5.1 %collective-permute-done.5 = bf16[32,3584]{1,0:T(8,128)(2,1)S(1)} collective-permute-done((bf16[32,3584]{1,0:T(8,128)(2,1)S(1)}, bf16[32,3584]{1,0:T(8,128)(2,1)S(1)}, u32[]{:S(2)}, u32[]{:S(2)}) %collective-permute-start.5) | collective-permute-done | bytes 229408 | tf_op jit(solution)/shard_map/ppermute | solution.py:25
  63.5 0.0 copy-done
  63.7 0.0 copy-start.1
  63.9 1.1 copy-done.1
  65.0 4.6 %shard_map.103 = (bf16[256,3584]{1,0:T(8,128)(2,1)}, bf16[64,1792]{1,0:T(8,128)(2,1)S(1)}, bf16[128,1792]{1,0:T(8,128)(2,1)}, bf16[384,1792]{1,0:T(8,128)(2,1)S(1)}, bf16[192,1792]{1,0:T(8,128)(2,1)S(1)}) custom-call(s32[3]{0:T(128)S(1)} %pad_add_fusion.place_ref, bf16[256,3584]{1,0:T(8,128)(2,1)S(1)} %get-tuple-element.45.x_ref, ...), custom_call_target="tpu_custom_call" | custom-call | flops 4000000000 | bytes 16777216 | tf_op jit(solution)/shard_map/pallas_call | solution.py:171
  69.6 0.0 copy-start.2
  69.6 0.7 copy-done.2
  70.3 3.7 %collective-permute-start.10 = (bf16[128,1792]{1,0:T(8,128)(2,1)}, bf16[128,1792]{1,0:T(8,128)(2,1)S(1)}, u32[]{:S(2)}, u32[]{:S(2)}) collective-permute-start(bf16[128,1792]{1,0:T(8,128)(2,1)} %get-tuple-element.23), channel_id=1, source_target_pairs={{0,8},{1,9},{2,10},{3,11},{4,12},{5,13},{6,14},{7,15},{8,0},{9,1},... | collective-permute-start | bytes 1376264 | tf_op jit(solution)/shard_map/ppermute | solution.py:21
  74.0 0.0 copy-start.3
  74.0 6.3 %all-to-all-start = ((bf16[16,16,3584]{2,1,0:T(8,128)(2,1)}), bf16[16,16,3584]{2,1,0:T(8,128)(2,1)}, u32[]{:S(2)}, u32[]{:S(2)}) async-start(bf16[16,16,3584]{2,1,0:T(8,128)(2,1)} %bitcast.32), calls=%async_computation | async-start | bytes 3670016 | tf_op jit(solution)/shard_map/all_to_all | solution.py:255
  80.3 0.0 copy-done.3
  80.4 2.8 %collective-permute-start.13 = (bf16[64,1792]{1,0:T(8,128)(2,1)S(1)}, bf16[64,1792]{1,0:T(8,128)(2,1)S(1)}, u32[]{:S(2)}, u32[]{:S(2)}) collective-permute-start(bf16[64,1792]{1,0:T(8,128)(2,1)S(1)} %copy-done.3), channel_id=1, source_target_pairs={{0,8},{1,9},{2,10},{3,11},{4,12},{5,13},{6,14},{7,15},{8,0},{9,1},... | collective-permute-start | bytes 688136 | tf_op jit(solution)/shard_map/ppermute | solution.py:21
  83.1 0.0 collective-permute-done.10.b_ref
  83.1 0.1 shard_map.104
  83.2 18.6 %collective-permute-start.12 = (bf16[128,1792]{1,0:T(8,128)(2,1)S(1)}, bf16[128,1792]{1,0:T(8,128)(2,1)S(1)}, u32[]{:S(2)}, u32[]{:S(2)}) collective-permute-start(bf16[128,1792]{1,0:T(8,128)(2,1)S(1)} %shard_map.104), channel_id=1, source_target_pairs={{0,480},{32,448},{64,416},{96,384},{128,352},{160,320},{192,288},{... | collective-permute-start | bytes 1376264 | tf_op jit(solution)/shard_map/ppermute | solution.py:32
  101.8 1.9 %collective-permute-start.11 = (bf16[192,1792]{1,0:T(8,128)(2,1)S(1)}, bf16[192,1792]{1,0:T(8,128)(2,1)S(1)}, u32[]{:S(2)}, u32[]{:S(2)}) collective-permute-start(bf16[192,1792]{1,0:T(8,128)(2,1)S(1)} %get-tuple-element.24), channel_id=1, source_target_pairs={{0,8},{1,9},{2,10},{3,11},{4,12},{5,13},{6,14},{7,15},{8,0},{9,1},... | collective-permute-start | bytes 2064392 | tf_op jit(solution)/shard_map/ppermute | solution.py:21
  103.8 0.0 collective-permute-done.13.b_ref
  103.8 0.1 shard_map.105
  103.8 0.0 copy-start.4
  103.8 0.0 copy-start.9
  103.9 3.7 %collective-permute-start.14 = (bf16[64,1792]{1,0:T(8,128)(2,1)S(1)}, bf16[64,1792]{1,0:T(8,128)(2,1)S(1)}, u32[]{:S(2)}, u32[]{:S(2)}) collective-permute-start(bf16[64,1792]{1,0:T(8,128)(2,1)S(1)} %shard_map.105), channel_id=1, source_target_pairs={{0,480},{32,448},{64,416},{96,384},{128,352},{160,320},{192,288},{... | collective-permute-start | bytes 688136 | tf_op jit(solution)/shard_map/ppermute | solution.py:32
  107.5 17.6 %collective-permute-done.14 = bf16[64,1792]{1,0:T(8,128)(2,1)S(1)} collective-permute-done((bf16[64,1792]{1,0:T(8,128)(2,1)S(1)}, bf16[64,1792]{1,0:T(8,128)(2,1)S(1)}, u32[]{:S(2)}, u32[]{:S(2)}) %collective-permute-start.14) | collective-permute-done | bytes 229408 | tf_op jit(solution)/shard_map/ppermute | solution.py:32
  125.1 0.0 collective-permute-done.12
  125.1 0.0 collective-permute-done.11
  125.1 1.0 fusion.3
  126.1 0.0 all-to-all-done
  126.1 1.7 %bitcast_reduce_fusion = bf16[2,16,3584]{2,1,0:T(8,128)(2,1)S(1)} fusion(bf16[16,16,3584]{2,1,0:T(8,128)(2,1)} %all-to-all-done), kind=kLoop, calls=%fused_computation.3 | loop fusion | flops 802816 | bytes 2064384 | tf_op jit(solution)/shard_map/reduce_sum | solution.py:258
  127.9 0.0 copy-done.4
  127.9 0.0 copy-done.9
  127.9 1.4 %fusion.1 = bf16[1,128,3584]{2,1,0:T(8,128)(2,1)} fusion(bf16[32,128]{1,0:T(8,128)(2,1)S(1)} %copy-done.9, bf16[32,3584]{1,0:T(8,128)(2,1)S(1)} %bitcast.101, bf16[1,128,3584]{2,1,0:T(8,128)(2,1)S(1)} %copy-done.4), kind=kOutput, calls=%fused_computation.2 | convolution fusion | flops 30736384 | bytes 2072576 | tf_op jit(solution)/shard_map/dot_general | solution.py:36
  (28 shorter events, 0.6 us)
Async XLA Ops:
  0.6 8.1 %copy-start.5 = (bf16[1,64,3584]{2,1,0:T(8,128)(2,1)S(1)}, bf16[1,64,3584]{2,1,0:T(8,128)(2,1)}, u32[]{:S(2)}) copy-start(bf16[1,64,3584]{2,1,0:T(8,128)(2,1)} %param.13) | copy-start | bytes 1376260
  0.6 8.1 %copy-start.6 = (bf16[1,64,3584]{2,1,0:T(8,128)(2,1)S(1)}, bf16[1,64,3584]{2,1,0:T(8,128)(2,1)}, u32[]{:S(2)}) copy-start(bf16[1,64,3584]{2,1,0:T(8,128)(2,1)} %param.12) | copy-start | bytes 1376260
  0.7 8.1 %copy-start.7 = (bf16[1,64,3584]{2,1,0:T(8,128)(2,1)S(1)}, bf16[1,64,3584]{2,1,0:T(8,128)(2,1)}, u32[]{:S(2)}) copy-start(bf16[1,64,3584]{2,1,0:T(8,128)(2,1)} %param.11) | copy-start | bytes 1376260
  3.3 7.4 %copy-start.8 = (bf16[32,3584]{1,0:T(8,128)(2,1)S(1)}, bf16[32,3584]{1,0:T(8,128)(2,1)}, u32[]{:S(2)}) copy-start(bf16[32,3584]{1,0:T(8,128)(2,1)} %get-tuple-element.16) | copy-start | bytes 688132
  3.3 9.0 %collective-permute-start = (bf16[32,3584]{1,0:T(8,128)(2,1)}, bf16[32,3584]{1,0:T(8,128)(2,1)S(1)}, u32[]{:S(2)}, u32[]{:S(2)}) collective-permute-start(bf16[32,3584]{1,0:T(8,128)(2,1)} %get-tuple-element.17), channel_id=1, source_target_pairs={{0,24},{1,25},{2,26},{3,27},{4,28},{5,29},{6,30},{7,31},{8,16},{9,... | collective-permute-start | bytes 688136 | tf_op jit(solution)/shard_map/ppermute | solution.py:17
  8.8 46.6 %collective-permute-start.4 = (bf16[192,3584]{1,0:T(8,128)(2,1)S(1)}, bf16[192,3584]{1,0:T(8,128)(2,1)S(1)}, u32[]{:S(2)}, u32[]{:S(2)}) collective-permute-start(bf16[192,3584]{1,0:T(8,128)(2,1)S(1)} %pad_maximum_fusion.mine_ref), channel_id=1, source_target_pairs={{0,8},{1,9},{2,10},{3,11},{4,12},{5,13},{6,14},{7,15},{8,0},{9,1},... | collective-permute-start | bytes 4128776 | tf_op jit(solution)/shard_map/ppermute | solution.py:21
  12.3 14.5 %collective-permute-start.6 = (bf16[64,3584]{1,0:T(8,128)(2,1)S(1)}, bf16[64,3584]{1,0:T(8,128)(2,1)S(1)}, u32[]{:S(2)}, u32[]{:S(2)}) collective-permute-start(bf16[64,3584]{1,0:T(8,128)(2,1)S(1)} %constant_dynamic-update-slice_fusion), channel_id=1, source_target_pairs={{0,7},{1,0},{2,1},{3,2},{4,3},{5,4},{6,5},{7,6},{8,15},{9,8},{10,9... | collective-permute-start | bytes 1376264 | tf_op jit(solution)/shard_map/ppermute | solution.py:25
  19.2 13.0 %collective-permute-start.1 = (bf16[64,3584]{1,0:T(8,128)(2,1)S(1)}, bf16[64,3584]{1,0:T(8,128)(2,1)S(1)}, u32[]{:S(2)}, u32[]{:S(2)}) collective-permute-start(bf16[64,3584]{1,0:T(8,128)(2,1)S(1)} %constant_dynamic-update-slice_fusion), channel_id=1, source_target_pairs={{0,1},{1,2},{2,3},{3,4},{4,5},{5,6},{6,7},{7,0},{8,9},{9,10},{10,1... | collective-permute-start | bytes 1376264 | tf_op jit(solution)/shard_map/ppermute | solution.py:25
  26.8 12.0 %collective-permute-start.7 = (bf16[64,3584]{1,0:T(8,128)(2,1)S(1)}, bf16[64,3584]{1,0:T(8,128)(2,1)S(1)}, u32[]{:S(2)}, u32[]{:S(2)}) collective-permute-start(bf16[64,3584]{1,0:T(8,128)(2,1)S(1)} %collective-permute-done.6), channel_id=1, source_target_pairs={{0,7},{1,0},{2,1},{3,2},{4,3},{5,4},{6,5},{7,6},{8,15},{9,8},{10,9... | collective-permute-start | bytes 1376264 | tf_op jit(solution)/shard_map/ppermute | solution.py:25
  32.2 12.0 %collective-permute-start.2 = (bf16[64,3584]{1,0:T(8,128)(2,1)S(1)}, bf16[64,3584]{1,0:T(8,128)(2,1)S(1)}, u32[]{:S(2)}, u32[]{:S(2)}) collective-permute-start(bf16[64,3584]{1,0:T(8,128)(2,1)S(1)} %collective-permute-done.1), channel_id=1, source_target_pairs={{0,1},{1,2},{2,3},{3,4},{4,5},{5,6},{6,7},{7,0},{8,9},{9,10},{10,1... | collective-permute-start | bytes 1376264 | tf_op jit(solution)/shard_map/ppermute | solution.py:25
  38.9 11.1 %collective-permute-start.8 = (bf16[64,3584]{1,0:T(8,128)(2,1)S(1)}, bf16[64,3584]{1,0:T(8,128)(2,1)S(1)}, u32[]{:S(2)}, u32[]{:S(2)}) collective-permute-start(bf16[64,3584]{1,0:T(8,128)(2,1)S(1)} %collective-permute-done.7), channel_id=1, source_target_pairs={{0,7},{1,0},{2,1},{3,2},{4,3},{5,4},{6,5},{7,6},{8,15},{9,8},{10,9... | collective-permute-start | bytes 1376264 | tf_op jit(solution)/shard_map/ppermute | solution.py:25
  44.2 11.2 %collective-permute-start.3 = (bf16[64,3584]{1,0:T(8,128)(2,1)S(1)}, bf16[64,3584]{1,0:T(8,128)(2,1)S(1)}, u32[]{:S(2)}, u32[]{:S(2)}) collective-permute-start(bf16[64,3584]{1,0:T(8,128)(2,1)S(1)} %collective-permute-done.2), channel_id=1, source_target_pairs={{0,1},{1,2},{2,3},{3,4},{4,5},{5,6},{6,7},{7,0},{8,9},{9,10},{10,1... | collective-permute-start | bytes 1376264 | tf_op jit(solution)/shard_map/ppermute | solution.py:25
  50.0 8.3 %collective-permute-start.9 = (bf16[32,3584]{1,0:T(8,128)(2,1)S(1)}, bf16[32,3584]{1,0:T(8,128)(2,1)S(1)}, u32[]{:S(2)}, u32[]{:S(2)}) collective-permute-start(bf16[32,3584]{1,0:T(8,128)(2,1)S(1)} %slice.108), channel_id=1, source_target_pairs={{0,7},{1,0},{2,1},{3,2},{4,3},{5,4},{6,5},{7,6},{8,15},{9,8},{10,9... | collective-permute-start | bytes 688136 | tf_op jit(solution)/shard_map/ppermute | solution.py:25
  55.4 8.1 %copy-start = (bf16[192,3584]{1,0:T(8,128)(2,1)}, bf16[192,3584]{1,0:T(8,128)(2,1)S(1)}, u32[]{:S(2)}) copy-start(bf16[192,3584]{1,0:T(8,128)(2,1)S(1)} %collective-permute-done.4.theirs_ref) | copy-start | bytes 4128772
  55.4 8.0 %collective-permute-start.5 = (bf16[32,3584]{1,0:T(8,128)(2,1)S(1)}, bf16[32,3584]{1,0:T(8,128)(2,1)S(1)}, u32[]{:S(2)}, u32[]{:S(2)}) collective-permute-start(bf16[32,3584]{1,0:T(8,128)(2,1)S(1)} %slice.82), channel_id=1, source_target_pairs={{0,1},{1,2},{2,3},{3,4},{4,5},{5,6},{6,7},{7,0},{8,9},{9,10},{10,1... | collective-permute-start | bytes 688136 | tf_op jit(solution)/shard_map/ppermute | solution.py:25
  63.7 1.3 %copy-start.1 = (bf16[192,3584]{1,0:T(8,128)(2,1)S(1)}, bf16[192,3584]{1,0:T(8,128)(2,1)}, u32[]{:S(2)}) copy-start(bf16[192,3584]{1,0:T(8,128)(2,1)} %copy-done) | copy-start | bytes 4128772
  69.6 0.7 copy-start.2
  70.3 12.8 %collective-permute-start.10 = (bf16[128,1792]{1,0:T(8,128)(2,1)}, bf16[128,1792]{1,0:T(8,128)(2,1)S(1)}, u32[]{:S(2)}, u32[]{:S(2)}) collective-permute-start(bf16[128,1792]{1,0:T(8,128)(2,1)} %get-tuple-element.23), channel_id=1, source_target_pairs={{0,8},{1,9},{2,10},{3,11},{4,12},{5,13},{6,14},{7,15},{8,0},{9,1},... | collective-permute-start | bytes 1376264 | tf_op jit(solution)/shard_map/ppermute | solution.py:21
  74.0 6.3 %copy-start.3 = (bf16[64,1792]{1,0:T(8,128)(2,1)S(1)}, bf16[64,1792]{1,0:T(8,128)(2,1)}, u32[]{:S(2)}) copy-start(bf16[64,1792]{1,0:T(8,128)(2,1)} %copy-done.2) | copy-start | bytes 688132
  74.0 52.1 %all-to-all-start = ((bf16[16,16,3584]{2,1,0:T(8,128)(2,1)}), bf16[16,16,3584]{2,1,0:T(8,128)(2,1)}, u32[]{:S(2)}, u32[]{:S(2)}) async-start(bf16[16,16,3584]{2,1,0:T(8,128)(2,1)} %bitcast.32), calls=%async_computation | async-start | bytes 3670016 | tf_op jit(solution)/shard_map/all_to_all | solution.py:255
  80.4 23.4 %collective-permute-start.13 = (bf16[64,1792]{1,0:T(8,128)(2,1)S(1)}, bf16[64,1792]{1,0:T(8,128)(2,1)S(1)}, u32[]{:S(2)}, u32[]{:S(2)}) collective-permute-start(bf16[64,1792]{1,0:T(8,128)(2,1)S(1)} %copy-done.3), channel_id=1, source_target_pairs={{0,8},{1,9},{2,10},{3,11},{4,12},{5,13},{6,14},{7,15},{8,0},{9,1},... | collective-permute-start | bytes 688136 | tf_op jit(solution)/shard_map/ppermute | solution.py:21
  83.2 41.9 %collective-permute-start.12 = (bf16[128,1792]{1,0:T(8,128)(2,1)S(1)}, bf16[128,1792]{1,0:T(8,128)(2,1)S(1)}, u32[]{:S(2)}, u32[]{:S(2)}) collective-permute-start(bf16[128,1792]{1,0:T(8,128)(2,1)S(1)} %shard_map.104), channel_id=1, source_target_pairs={{0,480},{32,448},{64,416},{96,384},{128,352},{160,320},{192,288},{... | collective-permute-start | bytes 1376264 | tf_op jit(solution)/shard_map/ppermute | solution.py:32
  101.8 23.3 %collective-permute-start.11 = (bf16[192,1792]{1,0:T(8,128)(2,1)S(1)}, bf16[192,1792]{1,0:T(8,128)(2,1)S(1)}, u32[]{:S(2)}, u32[]{:S(2)}) collective-permute-start(bf16[192,1792]{1,0:T(8,128)(2,1)S(1)} %get-tuple-element.24), channel_id=1, source_target_pairs={{0,8},{1,9},{2,10},{3,11},{4,12},{5,13},{6,14},{7,15},{8,0},{9,1},... | collective-permute-start | bytes 2064392 | tf_op jit(solution)/shard_map/ppermute | solution.py:21
  103.8 24.1 %copy-start.4 = (bf16[1,128,3584]{2,1,0:T(8,128)(2,1)S(1)}, bf16[1,128,3584]{2,1,0:T(8,128)(2,1)}, u32[]{:S(2)}) copy-start(bf16[1,128,3584]{2,1,0:T(8,128)(2,1)} %param.8) | copy-start | bytes 2752516
  103.8 24.0 %copy-start.9 = (bf16[32,128]{1,0:T(8,128)(2,1)S(1)}, bf16[32,128]{1,0:T(8,128)(2,1)}, u32[]{:S(2)}) copy-start(bf16[32,128]{1,0:T(8,128)(2,1)} %get-tuple-element.15) | copy-start | bytes 24580
  103.9 21.3 %collective-permute-start.14 = (bf16[64,1792]{1,0:T(8,128)(2,1)S(1)}, bf16[64,1792]{1,0:T(8,128)(2,1)S(1)}, u32[]{:S(2)}, u32[]{:S(2)}) collective-permute-start(bf16[64,1792]{1,0:T(8,128)(2,1)S(1)} %shard_map.105), channel_id=1, source_target_pairs={{0,480},{32,448},{64,416},{96,384},{128,352},{160,320},{192,288},{... | collective-permute-start | bytes 688136 | tf_op jit(solution)/shard_map/ppermute | solution.py:32

commit v4 on v3

--- a/solution.py
+++ b/solution.py
@@ -70,7 +70,7 @@
     mine, theirs = pick(expert), pick(1 - expert)
     first = jnp.where(expert == 0, mine, theirs)
     second = jnp.where(expert == 0, theirs, mine)
-    select_ref[...] = jnp.concatenate([first, second], axis=0).astype(BF)
+    select_ref[...] = jnp.concatenate([first] * NY + [second] * NY, axis=0).astype(BF)
     select = jnp.concatenate([mine, theirs], axis=0)
     gate = jnp.sum(select * (gate_ref[...].astype(F32) / 4096.0), axis=1, keepdims=True)
     select = select.astype(BF)
@@ -94,7 +94,7 @@
         out_shape=(
             jax.ShapeDtypeStruct((2 * CAP, width), BF),
             jax.ShapeDtypeStruct((2 * CAP, width), BF),
-            jax.ShapeDtypeStruct((E_WIN * CAP, block_x.shape[0]), BF),
+            jax.ShapeDtypeStruct((E_WIN * NY * CAP, block_x.shape[0]), BF),
         ),
         in_specs=[pl.BlockSpec(memory_space=pltpu.SMEM)] + [hbm] * 4,
         out_specs=(vmem, vmem, vmem),
@@ -104,78 +104,194 @@
     )(expert, *operands)
 
 
-def expert_kernel(
-    place_ref, x_ref, c_ref, mine_ref, theirs_ref,
-    partial_ref, first_ref, second_ref, own_ref, their_keep_ref,
-):
-    h = mine_ref.shape[0] // 3
-    rows, width = x_ref.shape
-    half = width // 2
-    y, expert, upper = place_ref[0], place_ref[1], place_ref[2]
-
-    def both(k):
-        return [mine_ref[k * h : (k + 1) * h], theirs_ref[k * h : (k + 1) * h]]
-
-    w_gu = jnp.concatenate(both(0) + both(1), axis=0)
-    pre = dot(x_ref[...], w_gu, ((1,), (1,)))
-    gate_pre, up_pre = pre[:, : 2 * h], pre[:, 2 * h :]
+def activations(x, c, w_gu, w_d):
+    pre = dot(x, w_gu, ((1,), (1,)))
+    units = pre.shape[1] // 2
+    gate_pre, up_pre = pre[:, :units], pre[:, units:]
     sig = 1.0 / (1.0 + jnp.exp(-gate_pre))
     activated = gate_pre * sig
     hidden = (activated * up_pre).astype(BF)
-    hidden_cot = dot(c_ref[...], jnp.concatenate(both(2), axis=0), ((1,), (1,)))
+    hidden_cot = dot(c, w_d, ((1,), (1,)))
     gate_cot = (hidden_cot * up_pre * (sig * (1.0 + gate_pre * (1.0 - sig)))).astype(BF)
     up_cot = (hidden_cot * activated).astype(BF)
-    gu_cot = jnp.concatenate([gate_cot, up_cot], axis=1)
-
-    to = lax.broadcasted_iota(jnp.int32, (rows, rows), 0)
-    at = lax.broadcasted_iota(jnp.int32, (rows, rows), 1)
+    return hidden, jnp.concatenate([gate_cot, up_cot], axis=1)
+
+
+def weights(mine_ref, theirs_ref):
+    h = mine_ref.shape[0] // 3
+    parts = [ref[k * h : (k + 1) * h] for k in range(3) for ref in (mine_ref, theirs_ref)]
+    return jnp.concatenate(parts[:4], axis=0), jnp.concatenate(parts[4:], axis=0)
+
+
+def turn(v):
+    return jnp.transpose(v.astype(F32)).astype(BF)
+
+
+def near_kernel(place_ref, x_ref, c_ref, mine_ref, theirs_ref, partial_ref, send_ref, keep_ref):
+    rows, width = x_ref.shape
+    half = width // 2
+    tile = half // TILES
+    y, expert, upper = place_ref[0], place_ref[1], place_ref[2]
+    w_gu, w_d = weights(mine_ref, theirs_ref)
+    hidden, gu_cot = activations(x_ref[...], c_ref[...], w_gu, w_d)
+
+    shape = (partial_ref.shape[0], rows)
+    to = lax.broadcasted_iota(jnp.int32, shape, 0)
+    at = lax.broadcasted_iota(jnp.int32, shape, 1)
     side, block, rank = to // (NY * CAP), to // CAP % NY, to % CAP
     ring = (block - y + NY) % NY
-    ring = sum(jnp.where(ring == r, ORDER.index(r), 0) for r in ORDER)
-    source = ring * (2 * CAP) + jnp.where(side == expert, 0, CAP) + rank
-    move = jnp.where(at == source, 1.0, 0.0).astype(BF)
+    chunk = sum(jnp.where(ring == r, ORDER.index(r), 0) for r in ORDER)
+    source = chunk * (2 * CAP) + jnp.where(side == expert, 0, CAP) + rank
+    move = jnp.where((at == source) & (ring != FAR), 1.0, 0.0).astype(BF)
     moved = dot(move, gu_cot, ((1,), (0,))).astype(BF)
-    tile = half // TILES
     for k in range(2 * TILES):
         cols = slice(k * tile, (k + 1) * tile)
         partial_ref[:, cols] = dot(moved, w_gu[:, cols], ((1,), (0,))).astype(BF)
 
+    hidden_t, gu_t = turn(hidden), turn(gu_cot)
+    units = gu_t.shape[0]
+    for out_ref, side in ((send_ref, 1 - upper), (keep_ref, upper)):
+        for k in range(TILES):
+            cols = slice(k * tile, (k + 1) * tile)
+            at_cols = pl.ds(pl.multiple_of(side * half + k * tile, 128), tile)
+            out_ref[:units, cols] = dot(gu_t, x_ref[:, at_cols], ((1,), (0,))).astype(BF)
+            out_ref[units:, cols] = dot(hidden_t, c_ref[:, at_cols], ((1,), (0,))).astype(BF)
+
+
+def pair(right_ref, left_ref, start, cols):
+    return jnp.concatenate([ref[start : start + CAP, cols] for ref in (right_ref, left_ref)], axis=0)
+
+
+def far_kernel(
+    place_ref, right_ref, left_ref, mine_any, theirs_any, send_any, partial_any,
+    partial_out, first_ref, second_ref, own_ref, hidden_ref, cot_ref,
+    mine_ref, theirs_ref, send_ref, rows_ref, sems,
+):
+    loads = ((mine_any, mine_ref), (theirs_any, theirs_ref), (send_any, send_ref))
+    loads = [pltpu.make_async_copy(src, dst, sems.at[i]) for i, (src, dst) in enumerate(loads)]
+    for copy in loads:
+        copy.start()
+    h = mine_ref.shape[0] // 3
+    half = first_ref.shape[1]
+    tile = half // TILES
+    y, expert, upper = place_ref[0], place_ref[1], place_ref[2]
+
+    loads[0].wait()
+    loads[1].wait()
+    w_gu, w_d = weights(mine_ref, theirs_ref)
+    everything = slice(0, 2 * half)
+    rows_x = pair(right_ref, left_ref, 0, everything)
+    rows_c = pair(right_ref, left_ref, CAP, everything)
+    hidden, gu_cot = activations(rows_x, rows_c, w_gu, w_d)
+    hidden_ref[...] = hidden
+    cot_ref[...] = gu_cot
+    for k in range(2 * TILES):
+        cols = slice(k * tile, (k + 1) * tile)
+        rows_ref[:, cols] = dot(gu_cot, w_gu[:, cols], ((1,), (0,))).astype(BF)
+    block = (y + FAR) % NY
+    stores = []
+    for i, side in enumerate((expert, 1 - expert)):
+        start = pl.multiple_of(side * (NY * CAP) + block * CAP, CAP)
+        stores.append(
+            pltpu.make_async_copy(
+                rows_ref.at[pl.ds(i * CAP, CAP)], partial_out.at[pl.ds(start, CAP)], sems.at[3 + i]
+            )
+        )
+        stores[-1].start()
+
+    hidden_t, gu_t = turn(hidden), turn(gu_cot)
+    loads[2].wait()
     for k in range(TILES):
         cols = slice(k * tile, (k + 1) * tile)
-        for send in (True, False):
-            start = (1 - upper if send else upper) * half + k * tile
-            start = pl.multiple_of(start, 128)
-            down = dot(hidden, c_ref[:, pl.ds(start, tile)], ((0,), (0,))).astype(BF)
-            gu = dot(gu_cot, x_ref[:, pl.ds(start, tile)], ((0,), (0,))).astype(BF)
-            if send:
-                first_ref[:, cols] = down[h:]
-                own_ref[2 * h : 3 * h, cols] = down[:h]
-                second_ref[:h, cols] = gu[h : 2 * h]
-                second_ref[h:, cols] = gu[3 * h :]
-                own_ref[:h, cols] = gu[:h]
-                own_ref[h : 2 * h, cols] = gu[2 * h : 3 * h]
-            else:
-                their_keep_ref[:h, cols] = gu[h : 2 * h]
-                their_keep_ref[h : 2 * h, cols] = gu[3 * h :]
-                their_keep_ref[2 * h :, cols] = down[h:]
-                own_ref[3 * h : 4 * h, cols] = gu[:h]
-                own_ref[4 * h : 5 * h, cols] = gu[2 * h : 3 * h]
-                own_ref[5 * h :, cols] = down[:h]
-
-
-def experts(place, rows_x, rows_c, mine, theirs):
-    rows, width = rows_x.shape
+        at_cols = pl.ds(pl.multiple_of((1 - upper) * half + k * tile, 128), tile)
+        gu = dot(gu_t, pair(right_ref, left_ref, 0, at_cols), ((1,), (0,)))
+        gu = (gu + send_ref[: 4 * h, cols].astype(F32)).astype(BF)
+        down = dot(hidden_t, pair(right_ref, left_ref, CAP, at_cols), ((1,), (0,)))
+        down = (down + send_ref[4 * h :, cols].astype(F32)).astype(BF)
+        first_ref[:, cols] = down[h:]
+        second_ref[:h, cols] = gu[h : 2 * h]
+        second_ref[h:, cols] = gu[3 * h :]
+        own_ref[:h, cols] = gu[:h]
+        own_ref[h : 2 * h, cols] = gu[2 * h : 3 * h]
+        own_ref[2 * h :, cols] = down[:h]
+    for copy in stores:
+        copy.wait()
+
+
+def keep_kernel(place_ref, right_any, left_any, hidden_ref, cot_ref, keep_any, own_ref, their_ref, right_ref, left_ref, keep_ref, sems):
+    loads = ((right_any, right_ref), (left_any, left_ref), (keep_any, keep_ref))
+    loads = [pltpu.make_async_copy(src, dst, sems.at[i]) for i, (src, dst) in enumerate(loads)]
+    for copy in loads:
+        copy.start()
+    h = own_ref.shape[0] // 3
+    half = own_ref.shape[1]
+    tile = half // TILES
+    hidden_t, gu_t = turn(hidden_ref[...]), turn(cot_ref[...])
+    for copy in loads:
+        copy.wait()
+    for k in range(TILES):
+        cols = slice(k * tile, (k + 1) * tile)
+        at_cols = pl.ds(pl.multiple_of(place_ref[2] * half + k * tile, 128), tile)
+        gu = dot(gu_t, pair(right_ref, left_ref, 0, at_cols), ((1,), (0,)))
+        gu = (gu + keep_ref[: 4 * h, cols].astype(F32)).astype(BF)
+        down = dot(hidden_t, pair(right_ref, left_ref, CAP, at_cols), ((1,), (0,)))
+        down = (down + keep_ref[4 * h :, cols].astype(F32)).astype(BF)
+        own_ref[:h, cols] = gu[:h]
+        own_ref[h : 2 * h, cols] = gu[2 * h : 3 * h]
+        own_ref[2 * h :, cols] = down[:h]
+        their_ref[:h, cols] = gu[h : 2 * h]
+        their_ref[h : 2 * h, cols] = gu[3 * h :]
+        their_ref[2 * h :, cols] = down[h:]
+
+
+def kept(place, far, hidden, cot, keep):
+    h, half = keep.shape[0] // 6, keep.shape[1]
+    vmem = pl.BlockSpec(memory_space=pltpu.VMEM)
+    anywhere = pl.BlockSpec(memory_space=pl.ANY)
+    return pl.pallas_call(
+        keep_kernel,
+        out_shape=(jax.ShapeDtypeStruct((3 * h, half), BF),) * 2,
+        in_specs=[pl.BlockSpec(memory_space=pltpu.SMEM), anywhere, anywhere, vmem, vmem, anywhere],
+        out_specs=(vmem, vmem),
+        scratch_shapes=[pltpu.VMEM(v.shape, BF) for v in (*far, keep)] + [pltpu.SemaphoreType.DMA((3,))],
+        compiler_params=pltpu.CompilerParams(vmem_limit_bytes=EXPERT_VMEM * 1024 * 1024),
+        cost_estimate=pl.CostEstimate(flops=10**9, bytes_accessed=8 * 2**20, transcendentals=0),
+    )(place, *far, hidden, cot, keep)
+
+
+def experts(place, rows_x, rows_c, far, mine, theirs):
+    width = rows_x.shape[1]
     h, half = mine.shape[0] // 3, width // 2
     vmem = pl.BlockSpec(memory_space=pltpu.VMEM)
-    shapes = [(rows, width), (h, half), (2 * h, half), (6 * h, half), (3 * h, half)]
-    return pl.pallas_call(
-        expert_kernel,
-        out_shape=tuple(jax.ShapeDtypeStruct(v, BF) for v in shapes),
-        in_specs=[pl.BlockSpec(memory_space=pltpu.SMEM)] + [vmem] * 4,
-        out_specs=(vmem,) * len(shapes),
-        compiler_params=pltpu.CompilerParams(vmem_limit_bytes=EXPERT_VMEM * 1024 * 1024),
+    smem = pl.BlockSpec(memory_space=pltpu.SMEM)
+    anywhere = pl.BlockSpec(memory_space=pl.ANY)
+    params = pltpu.CompilerParams(vmem_limit_bytes=EXPERT_VMEM * 1024 * 1024)
+
+    def arrays(*shapes):
+        return tuple(jax.ShapeDtypeStruct(v, BF) for v in shapes)
+
+    near = arrays((2 * NY * CAP, width), (6 * h, half), (6 * h, half))
+    partial, send, keep = pl.pallas_call(
+        near_kernel,
+        out_shape=near,
+        in_specs=[smem] + [vmem] * 4,
+        out_specs=(vmem,) * 3,
+        compiler_params=params,
         cost_estimate=pl.CostEstimate(flops=4 * 10**9, bytes_accessed=16 * 2**20, transcendentals=0),
     )(place, rows_x, rows_c, mine, theirs)
+    rows = near[0].shape[0] // NY
+    outs = pl.pallas_call(
+        far_kernel,
+        out_shape=near[:1] + arrays((h, half), (2 * h, half), (3 * h, half), (rows, 2 * h), (rows, 4 * h)),
+        in_specs=[smem] + [vmem] * 2 + [anywhere] * 4,
+        out_specs=(anywhere,) + (vmem,) * 5,
+        scratch_shapes=[pltpu.VMEM(v.shape, BF) for v in (mine, theirs, send)]
+        + [pltpu.VMEM((rows, width), BF), pltpu.SemaphoreType.DMA((5,))],
+        input_output_aliases={6: 0},
+        compiler_params=params,
+        cost_estimate=pl.CostEstimate(flops=2 * 10**9, bytes_accessed=8 * 2**20, transcendentals=0),
+    )(place, *far, mine, theirs, send, partial)
+    return (*outs, keep)
 
 
 def add_kernel(a_ref, b_ref, out_ref):
@@ -220,46 +336,44 @@
             else:
                 right = after(right, theirs)
         if step == 3:
-            right = shift_y(right[: RIGHT_ROWS * CAP], 1)
-            left = shift_y(left[RIGHT_ROWS * CAP :], -1)
-            rights.append(jnp.concatenate([right, left], axis=0))
+            right = shift_y(right[: 2 * CAP], 1)
+            left = shift_y(left[2 * CAP :], -1)
             break
         right = shift_y(right, 1)
         rights.append(right)
-        if step < 3:
-            left = shift_y(left, -1)
-            lefts.append(left)
-    near = [chunk] + lefts + rights[::-1]
-    near = [near[r] for r in ORDER]
-    parts = [p.reshape(2, 2, CAP, width) for p in near]
+        left = shift_y(left, -1)
+        lefts.append(left)
+    near = dict(enumerate([chunk] + lefts))
+    near.update({NY - 1 - i: v for i, v in enumerate(rights)})
+    parts = [near[r].reshape(2, 2, CAP, width) for r in ORDER]
     rows_x = jnp.concatenate([p[:, 0].reshape(2 * CAP, width) for p in parts], axis=0)
     rows_c = jnp.concatenate([p[:, 1].reshape(2 * CAP, width) for p in parts], axis=0)
 
     place = jnp.stack([lax.axis_index("ep") % NY, own_expert, upper.astype(jnp.int32)])
-    partial, their_send_d, their_send, own, their_keep = experts(
-        place.astype(jnp.int32), rows_x, rows_c, mine, theirs
+    place = place.astype(jnp.int32)
+    partial, their_send_d, their_send, own, hidden, cot, keep = experts(
+        place, rows_x, rows_c, (right, left), mine, theirs
     )
 
     got_send_d = swap_x_pair(their_send_d)
     got_send = swap_x_pair(their_send)
-    from_mirror_d = mirror(add(own, got_send_d, 2, FIRST_COST))
+    to_mirror_d = add(own, got_send_d, 2, FIRST_COST)
+    from_mirror_d = mirror(to_mirror_d)
     to_mirror = add(own, got_send, 0, SECOND_COST)
     from_mirror = mirror(to_mirror)
     if X_LAST == 1:
-        their_keep = after(their_keep, to_mirror)
+        keep = after(keep, to_mirror)
     if X_LAST == 2:
-        their_keep = after(their_keep, from_mirror_d)
+        keep = after(keep, to_mirror, to_mirror_d)
+    own_keep, their_keep = kept(place, (right, left), hidden, cot, keep)
     got_keep = swap_x_pair(their_keep)
 
     groups = [[x * NY + k for x in pair for k in range(NY)] for pair in ((0, 3), (1, 2))]
     got = lax.all_to_all(
         partial.reshape(2 * NY, CAP, width), "ep", 0, 0, axis_index_groups=groups, tiled=True
     )
-    summed = jnp.sum(got.reshape(2, NY, CAP, width).astype(F32), axis=1).astype(BF)
-    branch = dot(select, summed.reshape(2 * CAP, width), ((0,), (0,)))
+    branch = dot(select, got.reshape(2 * NY * CAP, width), ((0,), (0,)))
     input_grad = (block_cot.astype(F32) + branch).astype(BF)[None]
-    own_keep = own[3 * h :]
-
     def total(kept, near, far):
         return (kept.astype(F32) + near.astype(F32) + far.astype(F32)).astype(BF)[None]
 
@@ -274,9 +388,9 @@
 WEIGHT_STEP = 3
 X_LAST = 1
 TILES = 2
-RIGHT_ROWS = 2
 WEIGHT_SIDE = 0
-ORDER = (4, 5, 3, 6, 2, 7, 1, 0)
+FAR = NY // 2
+ORDER = (5, 3, 6, 2, 7, 1, 0)
 FIRST_COST = 100
 SECOND_COST = 100
 EXPERT_VMEM = 16

time: 130 us -> 128 us (0.985)
  waiting for transfers between devices: 39.2 us -> 34.1 us
  Pallas kernels: 7.37 us -> 12.2 us
  starting transfers between devices: 74.7 us -> 72.7 us
  other arithmetic: 2.96 us -> 1.2 us
  matrix products: 1.35 us -> 2.86 us
    ppermute x8, waiting for transfers between devices: 20.2 us -> 14.9 us  [shift_y(): lax.ppermute(v, 'ep', [(i, i // NY * NY + (i + step) % NY) for i in range...]
    pallas_call x1 -> x3, Pallas kernels: 4.57 us -> 9.36 us  [the longest x1 3.94 us: experts(): pl.pallas_call(near_kernel, out_shape=near, in_specs=[smem] + [vmem] * 4,...]
    ppermute x2, starting transfers between devices: 22.3 us -> 20.3 us  [mirror(): return lax.ppermute(v, 'pp', [(i, n - 1 - i) for i in range(n)])]
    reduce_sum x1 -> x0, other arithmetic: 1.75 us -> none  [shards(): jnp.sum(got.reshape(2, NY, CAP, width).astype(F32), axis=1).astype(BF)]
    dot_general x1, matrix products: 1.35 us -> 2.86 us  [dot(): return lax.dot_general(a, b, (dims, ((), ())), preferred_element_type=F32)]
    unnamed x35 -> x41, local copies, waits for them, and re-layouts: 2.13 us -> 2.92 us
  transfers between devices with their start and end apart: 16 -> 16, of which waited for: 7 -> 6; matrix products, arithmetic and copies ran while one was open for 1% -> 1% of each run, Pallas kernels for 0% -> 5%
where the time goes in v4:
time: 128 us; the launch traced here: 127 us
  starting transfers between devices  72.7 us (57%)
  waiting for transfers between devices  34.1 us (27%)
  Pallas kernels  12.2 us (10%)
  local copies, waits for them, and re-layouts  3.23 us (3%)
  matrix products  2.86 us (2%)
    ppermute x8, starting transfers between devices, shift_y(): lax.ppermute(v, 'ep', [(i, i // NY * NY + (i + step) % NY) for i in range...  30.5 us
    ppermute x2, starting transfers between devices, mirror(): return lax.ppermute(v, 'pp', [(i, n - 1 - i) for i in range(n)])  20.3 us
    ppermute x2, waiting for transfers between devices, mirror(): return lax.ppermute(v, 'pp', [(i, n - 1 - i) for i in range(n)])  17.8 us
    ppermute x8, waiting for transfers between devices, shift_y(): lax.ppermute(v, 'ep', [(i, i // NY * NY + (i + step) % NY) for i in range...  14.9 us
    ppermute x4, starting transfers between devices, swap_x_pair(): return lax.ppermute(v, 'ep', [(i, i ^ NY) for i in range(NX * NY)])  10.3 us
    all_to_all x1, starting transfers between devices, shards(): lax.all_to_all(partial.reshape(2 * NY, CAP, width), 'ep', 0, 0, axis_inde...  6.29 us
    ppermute x1, starting transfers between devices, swap_x_outer(): lax.ppermute(v, 'ep', [(i, (NX - 1 - i // NY) * NY + i % NY) for i in ran...  5.35 us
    pallas_call x1, Pallas kernels, experts(): pl.pallas_call(near_kernel, out_shape=near, in_specs=[smem] + [vmem] * 4,...  3.94 us
  transfers between devices with their start and end apart: 16, of which 6 were waited for; matrix products, arithmetic and copies ran while one was open for 1% of the time, Pallas kernels for 5%

profile of v4, /device:TPU:1, one launch (start us, length us, event | category | flops | bytes accessed | tf_op | source)
XLA Modules:
  0.0 127.5 jit_solution(6245386515941580128)
XLA Ops:
  0.6 0.0 copy-start.9
  0.6 0.0 copy-start.10
  0.7 0.0 copy-start.11
  0.7 2.6 %shard_map.102 = (bf16[32,3584]{1,0:T(8,128)(2,1)}, bf16[32,3584]{1,0:T(8,128)(2,1)}, bf16[256,128]{1,0:T(8,128)(2,1)}) custom-call(s32[1]{0:T(128)} %bitcast.1.expert_ref, s32[1,128]{1,0:T(1,128)} %slot_hbm.1, s32[1,128]{1,0:T(1,128)} %gate_hbm.1, bf16[128,3584]{1,0:T(8,128)(2,1)} %bitcast.60, bf16[128,3584]{1,0:T(8,128)(2,1)} %bitcast.42), custom_call_target="tpu_custom_call" | custom-call | tf_op jit(solution)/shard_map/pallas_call | solution.py:92
  3.3 0.0 copy-start.12
  3.3 5.4 %collective-permute-start = (bf16[32,3584]{1,0:T(8,128)(2,1)}, bf16[32,3584]{1,0:T(8,128)(2,1)S(1)}, u32[]{:S(2)}, u32[]{:S(2)}) collective-permute-start(bf16[32,3584]{1,0:T(8,128)(2,1)} %get-tuple-element.23), channel_id=1, source_target_pairs={{0,24},{1,25},{2,26},{3,27},{4,28},{5,29},{6,30},{7,31},{8,16},{9,... | collective-permute-start | bytes 688136 | tf_op jit(solution)/shard_map/ppermute | solution.py:17
  8.7 0.0 copy-done.9
  8.7 0.0 copy-done.10
  8.7 0.0 copy-done.11
  8.7 0.1 pad_maximum_fusion.mine_ref.mine_any
  8.8 1.9 %collective-permute-start.4 = (bf16[192,3584]{1,0:T(8,128)(2,1)S(1)}, bf16[192,3584]{1,0:T(8,128)(2,1)S(1)}, u32[]{:S(2)}, u32[]{:S(2)}) collective-permute-start(bf16[192,3584]{1,0:T(8,128)(2,1)S(1)} %pad_maximum_fusion.mine_ref.mine_any), channel_id=1, source_target_pairs={{0,8},{1,9},{2,10},{3,11},{4,12},{5,13},{6,14},{7,15},{8,0},{9,1},... | collective-permute-start | bytes 4128776 | tf_op jit(solution)/shard_map/ppermute | solution.py:21
  10.8 0.0 copy-done.12
  10.8 0.1 pad_add_fusion.place_ref
  10.9 1.4 %collective-permute-done = bf16[32,3584]{1,0:T(8,128)(2,1)S(1)} collective-permute-done((bf16[32,3584]{1,0:T(8,128)(2,1)}, bf16[32,3584]{1,0:T(8,128)(2,1)S(1)}, u32[]{:S(2)}, u32[]{:S(2)}) %collective-permute-start) | collective-permute-done | bytes 229408 | tf_op jit(solution)/shard_map/ppermute | solution.py:17
  12.3 6.9 %collective-permute-start.6 = (bf16[64,3584]{1,0:T(8,128)(2,1)S(1)}, bf16[64,3584]{1,0:T(8,128)(2,1)S(1)}, u32[]{:S(2)}, u32[]{:S(2)}) collective-permute-start(bf16[64,3584]{1,0:T(8,128)(2,1)S(1)} %constant_dynamic-update-slice_fusion), channel_id=1, source_target_pairs={{0,7},{1,0},{2,1},{3,2},{4,3},{5,4},{6,5},{7,6},{8,15},{9,8},{10,9... | collective-permute-start | bytes 1376264 | tf_op jit(solution)/shard_map/ppermute | solution.py:25
  19.2 1.9 %collective-permute-start.1 = (bf16[64,3584]{1,0:T(8,128)(2,1)S(1)}, bf16[64,3584]{1,0:T(8,128)(2,1)S(1)}, u32[]{:S(2)}, u32[]{:S(2)}) collective-permute-start(bf16[64,3584]{1,0:T(8,128)(2,1)S(1)} %constant_dynamic-update-slice_fusion), channel_id=1, source_target_pairs={{0,1},{1,2},{2,3},{3,4},{4,5},{5,6},{6,7},{7,0},{8,9},{9,10},{10,1... | collective-permute-start | bytes 1376264 | tf_op jit(solution)/shard_map/ppermute | solution.py:25
  21.2 5.7 %collective-permute-done.6 = bf16[64,3584]{1,0:T(8,128)(2,1)S(1)} collective-permute-done((bf16[64,3584]{1,0:T(8,128)(2,1)S(1)}, bf16[64,3584]{1,0:T(8,128)(2,1)S(1)}, u32[]{:S(2)}, u32[]{:S(2)}) %collective-permute-start.6) | collective-permute-done | bytes 458784 | tf_op jit(solution)/shard_map/ppermute | solution.py:25
  26.9 5.3 %collective-permute-start.7 = (bf16[64,3584]{1,0:T(8,128)(2,1)S(1)}, bf16[64,3584]{1,0:T(8,128)(2,1)S(1)}, u32[]{:S(2)}, u32[]{:S(2)}) collective-permute-start(bf16[64,3584]{1,0:T(8,128)(2,1)S(1)} %collective-permute-done.6), channel_id=1, source_target_pairs={{0,7},{1,0},{2,1},{3,2},{4,3},{5,4},{6,5},{7,6},{8,15},{9,8},{10,9... | collective-permute-start | bytes 1376264 | tf_op jit(solution)/shard_map/ppermute | solution.py:25
  32.2 0.0 collective-permute-done.1
  32.2 1.9 %collective-permute-start.2 = (bf16[64,3584]{1,0:T(8,128)(2,1)S(1)}, bf16[64,3584]{1,0:T(8,128)(2,1)S(1)}, u32[]{:S(2)}, u32[]{:S(2)}) collective-permute-start(bf16[64,3584]{1,0:T(8,128)(2,1)S(1)} %collective-permute-done.1), channel_id=1, source_target_pairs={{0,1},{1,2},{2,3},{3,4},{4,5},{5,6},{6,7},{7,0},{8,9},{9,10},{10,1... | collective-permute-start | bytes 1376264 | tf_op jit(solution)/shard_map/ppermute | solution.py:25
  34.2 4.7 %collective-permute-done.7 = bf16[64,3584]{1,0:T(8,128)(2,1)S(1)} collective-permute-done((bf16[64,3584]{1,0:T(8,128)(2,1)S(1)}, bf16[64,3584]{1,0:T(8,128)(2,1)S(1)}, u32[]{:S(2)}, u32[]{:S(2)}) %collective-permute-start.7) | collective-permute-done | bytes 458784 | tf_op jit(solution)/shard_map/ppermute | solution.py:25
  38.9 5.3 %collective-permute-start.8 = (bf16[64,3584]{1,0:T(8,128)(2,1)S(1)}, bf16[64,3584]{1,0:T(8,128)(2,1)S(1)}, u32[]{:S(2)}, u32[]{:S(2)}) collective-permute-start(bf16[64,3584]{1,0:T(8,128)(2,1)S(1)} %collective-permute-done.7), channel_id=1, source_target_pairs={{0,7},{1,0},{2,1},{3,2},{4,3},{5,4},{6,5},{7,6},{8,15},{9,8},{10,9... | collective-permute-start | bytes 1376264 | tf_op jit(solution)/shard_map/ppermute | solution.py:25
  44.3 0.0 collective-permute-done.2
  44.3 1.9 %collective-permute-start.3 = (bf16[64,3584]{1,0:T(8,128)(2,1)S(1)}, bf16[64,3584]{1,0:T(8,128)(2,1)S(1)}, u32[]{:S(2)}, u32[]{:S(2)}) collective-permute-start(bf16[64,3584]{1,0:T(8,128)(2,1)S(1)} %collective-permute-done.2), channel_id=1, source_target_pairs={{0,1},{1,2},{2,3},{3,4},{4,5},{5,6},{6,7},{7,0},{8,9},{9,10},{10,1... | collective-permute-start | bytes 1376264 | tf_op jit(solution)/shard_map/ppermute | solution.py:25
  46.3 3.8 %collective-permute-done.8 = bf16[64,3584]{1,0:T(8,128)(2,1)S(1)} collective-permute-done((bf16[64,3584]{1,0:T(8,128)(2,1)S(1)}, bf16[64,3584]{1,0:T(8,128)(2,1)S(1)}, u32[]{:S(2)}, u32[]{:S(2)}) %collective-permute-start.8) | collective-permute-done | bytes 458784 | tf_op jit(solution)/shard_map/ppermute | solution.py:25
  50.1 5.3 %collective-permute-start.9 = (bf16[32,3584]{1,0:T(8,128)(2,1)S(1)}, bf16[32,3584]{1,0:T(8,128)(2,1)S(1)}, u32[]{:S(2)}, u32[]{:S(2)}) collective-permute-start(bf16[32,3584]{1,0:T(8,128)(2,1)S(1)} %slice.96), channel_id=1, source_target_pairs={{0,7},{1,0},{2,1},{3,2},{4,3},{5,4},{6,5},{7,6},{8,15},{9,8},{10,9... | collective-permute-start | bytes 688136 | tf_op jit(solution)/shard_map/ppermute | solution.py:25
  55.4 0.0 collective-permute-done.3
  55.5 0.0 collective-permute-done.4.theirs_ref.theirs_any
  55.6 1.9 %collective-permute-start.5 = (bf16[32,3584]{1,0:T(8,128)(2,1)S(1)}, bf16[32,3584]{1,0:T(8,128)(2,1)S(1)}, u32[]{:S(2)}, u32[]{:S(2)}) collective-permute-start(bf16[32,3584]{1,0:T(8,128)(2,1)S(1)} %slice.72), channel_id=1, source_target_pairs={{0,1},{1,2},{2,3},{3,4},{4,5},{5,6},{6,7},{7,0},{8,9},{9,10},{10,1... | collective-permute-start | bytes 688136 | tf_op jit(solution)/shard_map/ppermute | solution.py:25
  57.8 3.9 %shard_map.103 = (bf16[256,3584]{1,0:T(8,128)(2,1)}, bf16[384,1792]{1,0:T(8,128)(2,1)S(1)}, bf16[384,1792]{1,0:T(8,128)(2,1)S(1)}) custom-call(s32[3]{0:T(128)S(1)} %pad_add_fusion.place_ref, bf16[224,3584]{1,0:T(8,128)(2,1)S(1)} %get-tuple-element.55.x_ref, bf16[224,3584]{1,0:T(8,128)(2,1)S(1)} %get-tuple-element.56.c_ref, ...), custom_call_target="tpu_custom_call" | custom-call | flops 4000000000 | bytes 16777216 | tf_op jit(solution)/shard_map/pallas_call | solution.py:274
  61.7 1.1 copy-done.6
  62.8 0.0 collective-permute-done.9.left_ref.left_any
  62.8 0.7 collective-permute-done.5.right_ref.right_any
  63.5 3.5 %shard_map.104 = (bf16[256,3584]{1,0:T(8,128)(2,1)}, bf16[64,1792]{1,0:T(8,128)(2,1)S(1)}, bf16[128,1792]{1,0:T(8,128)(2,1)S(1)}, bf16[192,1792]{1,0:T(8,128)(2,...) custom-call(s32[3]{0:T(128)S(1)} %pad_add_fusion.place_ref, ...), custom_call_target="tpu_custom_call", output_to_operand_aliasing={{0}: (6, {})} | custom-call | flops 2000000000 | bytes 8388608 | tf_op jit(solution)/shard_map/pallas_call | solution.py:283
  67.1 0.0 copy-done
  67.1 0.0 copy-start.2
  67.1 0.7 copy-done.2
  67.8 0.8 copy-done.4
  68.6 3.7 %collective-permute-start.10 = (bf16[128,1792]{1,0:T(8,128)(2,1)S(1)}, bf16[128,1792]{1,0:T(8,128)(2,1)S(1)}, u32[]{:S(2)}, u32[]{:S(2)}) collective-permute-start(bf16[128,1792]{1,0:T(8,128)(2,1)S(1)} %get-tuple-element.33), channel_id=1, source_target_pairs={{0,8},{1,9},{2,10},{3,11},{4,12},{5,13},{6,14},{7,15},{8,0},{9,1},... | collective-permute-start | bytes 1376264 | tf_op jit(solution)/shard_map/ppermute | solution.py:21
  72.3 0.0 copy-start.3
  72.3 0.0 copy-start.5
  72.3 6.3 %all-to-all-start = ((bf16[16,16,3584]{2,1,0:T(8,128)(2,1)}), bf16[16,16,3584]{2,1,0:T(8,128)(2,1)}, u32[]{:S(2)}, u32[]{:S(2)}) async-start(bf16[16,16,3584]{2,1,0:T(8,128)(2,1)} %bitcast.29), calls=%async_computation | async-start | bytes 3670016 | tf_op jit(solution)/shard_map/all_to_all | solution.py:372
  78.6 0.0 copy-done.3
  78.6 2.8 %collective-permute-start.13 = (bf16[64,1792]{1,0:T(8,128)(2,1)S(1)}, bf16[64,1792]{1,0:T(8,128)(2,1)S(1)}, u32[]{:S(2)}, u32[]{:S(2)}) collective-permute-start(bf16[64,1792]{1,0:T(8,128)(2,1)S(1)} %copy-done.3), channel_id=1, source_target_pairs={{0,8},{1,9},{2,10},{3,11},{4,12},{5,13},{6,14},{7,15},{8,0},{9,1},... | collective-permute-start | bytes 688136 | tf_op jit(solution)/shard_map/ppermute | solution.py:21
  81.4 0.0 collective-permute-done.10.b_ref
  81.4 0.0 copy-done.5
  81.4 0.0 copy-start.1
  81.4 0.0 copy-start.7
  81.4 0.1 shard_map.105
  81.5 18.2 %collective-permute-start.12 = (bf16[128,1792]{1,0:T(8,128)(2,1)S(1)}, bf16[128,1792]{1,0:T(8,128)(2,1)S(1)}, u32[]{:S(2)}, u32[]{:S(2)}) collective-permute-start(bf16[128,1792]{1,0:T(8,128)(2,1)S(1)} %shard_map.105), channel_id=1, source_target_pairs={{0,480},{32,448},{64,416},{96,384},{128,352},{160,320},{192,288},{... | collective-permute-start | bytes 1376264 | tf_op jit(solution)/shard_map/ppermute | solution.py:32
  99.8 1.9 %shard_map.106 = (bf16[192,1792]{1,0:T(8,128)(2,1)S(1)}, bf16[192,1792]{1,0:T(8,128)(2,1)S(1)}) custom-call(s32[3]{0:T(128)S(1)} %pad_add_fusion.place_ref, bf16[32,3584]{1,0:T(8,128)(2,1)S(1)} %copy-done.1, bf16[32,3584]{1,0:T(8,128)(2,1)S(1)} %collective-permute-done.9.left_ref.left_any, bf16[32,128]{1,0:T(8,128)(2,1)S(1)} %get-tuple-element.29.hidden_ref, ...), custom_call_target="tpu_custom_call" | custom-call | flops 1000000000 | bytes 8388608 | tf_op jit(solution)/shard_map/pallas_call | solution.py:251
  101.7 1.9 %collective-permute-start.11 = (bf16[192,1792]{1,0:T(8,128)(2,1)S(1)}, bf16[192,1792]{1,0:T(8,128)(2,1)S(1)}, u32[]{:S(2)}, u32[]{:S(2)}) collective-permute-start(bf16[192,1792]{1,0:T(8,128)(2,1)S(1)} %get-tuple-element.36), channel_id=1, source_target_pairs={{0,8},{1,9},{2,10},{3,11},{4,12},{5,13},{6,14},{7,15},{8,0},{9,1},... | collective-permute-start | bytes 2064392 | tf_op jit(solution)/shard_map/ppermute | solution.py:21
  103.6 0.0 collective-permute-done.13.b_ref
  103.6 0.1 shard_map.107
  103.7 0.0 copy-start.8
  103.7 0.0 copy-start.13
  103.7 2.1 %collective-permute-start.14 = (bf16[64,1792]{1,0:T(8,128)(2,1)S(1)}, bf16[64,1792]{1,0:T(8,128)(2,1)S(1)}, u32[]{:S(2)}, u32[]{:S(2)}) collective-permute-start(bf16[64,1792]{1,0:T(8,128)(2,1)S(1)} %shard_map.107), channel_id=1, source_target_pairs={{0,480},{32,448},{64,416},{96,384},{128,352},{160,320},{192,288},{... | collective-permute-start | bytes 688136 | tf_op jit(solution)/shard_map/ppermute | solution.py:32
  105.8 17.8 %collective-permute-done.14 = bf16[64,1792]{1,0:T(8,128)(2,1)S(1)} collective-permute-done((bf16[64,1792]{1,0:T(8,128)(2,1)S(1)}, bf16[64,1792]{1,0:T(8,128)(2,1)S(1)}, u32[]{:S(2)}, u32[]{:S(2)}) %collective-permute-start.14) | collective-permute-done | bytes 229408 | tf_op jit(solution)/shard_map/ppermute | solution.py:32
  123.5 0.0 collective-permute-done.12
  123.5 0.0 collective-permute-done.11
  123.5 1.0 fusion.3
  124.6 0.0 all-to-all-done
  124.6 0.0 copy-done.8
  124.6 2.9 %fusion.1 = bf16[1,128,3584]{2,1,0:T(8,128)(2,1)} fusion(bf16[256,128]{1,0:T(8,128)(2,1)S(1)} %copy-done.13, bf16[256,3584]{1,0:T(8,128)(2,1)} %bitcast.30, bf16[1,128,3584]{2,1,0:T(8,128)(2,1)S(1)} %copy-done.8), kind=kOutput, calls=%fused_computation.2 | convolution fusion | flops 236257280 | bytes 3735552 | tf_op jit(solution)/shard_map/dot_general | solution.py:36
  (30 shorter events, 0.5 us)
Async XLA Ops:
  0.6 8.1 %copy-start.9 = (bf16[1,64,3584]{2,1,0:T(8,128)(2,1)S(1)}, bf16[1,64,3584]{2,1,0:T(8,128)(2,1)}, u32[]{:S(2)}) copy-start(bf16[1,64,3584]{2,1,0:T(8,128)(2,1)} %param.13) | copy-start | bytes 1376260
  0.6 8.1 %copy-start.10 = (bf16[1,64,3584]{2,1,0:T(8,128)(2,1)S(1)}, bf16[1,64,3584]{2,1,0:T(8,128)(2,1)}, u32[]{:S(2)}) copy-start(bf16[1,64,3584]{2,1,0:T(8,128)(2,1)} %param.12) | copy-start | bytes 1376260
  0.7 8.1 %copy-start.11 = (bf16[1,64,3584]{2,1,0:T(8,128)(2,1)S(1)}, bf16[1,64,3584]{2,1,0:T(8,128)(2,1)}, u32[]{:S(2)}) copy-start(bf16[1,64,3584]{2,1,0:T(8,128)(2,1)} %param.11) | copy-start | bytes 1376260
  3.3 7.4 %copy-start.12 = (bf16[32,3584]{1,0:T(8,128)(2,1)S(1)}, bf16[32,3584]{1,0:T(8,128)(2,1)}, u32[]{:S(2)}) copy-start(bf16[32,3584]{1,0:T(8,128)(2,1)} %get-tuple-element.22) | copy-start | bytes 688132
  3.3 9.0 %collective-permute-start = (bf16[32,3584]{1,0:T(8,128)(2,1)}, bf16[32,3584]{1,0:T(8,128)(2,1)S(1)}, u32[]{:S(2)}, u32[]{:S(2)}) collective-permute-start(bf16[32,3584]{1,0:T(8,128)(2,1)} %get-tuple-element.23), channel_id=1, source_target_pairs={{0,24},{1,25},{2,26},{3,27},{4,28},{5,29},{6,30},{7,31},{8,16},{9,... | collective-permute-start | bytes 688136 | tf_op jit(solution)/shard_map/ppermute | solution.py:17
  8.8 46.7 %collective-permute-start.4 = (bf16[192,3584]{1,0:T(8,128)(2,1)S(1)}, bf16[192,3584]{1,0:T(8,128)(2,1)S(1)}, u32[]{:S(2)}, u32[]{:S(2)}) collective-permute-start(bf16[192,3584]{1,0:T(8,128)(2,1)S(1)} %pad_maximum_fusion.mine_ref.mine_any), channel_id=1, source_target_pairs={{0,8},{1,9},{2,10},{3,11},{4,12},{5,13},{6,14},{7,15},{8,0},{9,1},... | collective-permute-start | bytes 4128776 | tf_op jit(solution)/shard_map/ppermute | solution.py:21
  12.3 14.5 %collective-permute-start.6 = (bf16[64,3584]{1,0:T(8,128)(2,1)S(1)}, bf16[64,3584]{1,0:T(8,128)(2,1)S(1)}, u32[]{:S(2)}, u32[]{:S(2)}) collective-permute-start(bf16[64,3584]{1,0:T(8,128)(2,1)S(1)} %constant_dynamic-update-slice_fusion), channel_id=1, source_target_pairs={{0,7},{1,0},{2,1},{3,2},{4,3},{5,4},{6,5},{7,6},{8,15},{9,8},{10,9... | collective-permute-start | bytes 1376264 | tf_op jit(solution)/shard_map/ppermute | solution.py:25
  19.2 13.0 %collective-permute-start.1 = (bf16[64,3584]{1,0:T(8,128)(2,1)S(1)}, bf16[64,3584]{1,0:T(8,128)(2,1)S(1)}, u32[]{:S(2)}, u32[]{:S(2)}) collective-permute-start(bf16[64,3584]{1,0:T(8,128)(2,1)S(1)} %constant_dynamic-update-slice_fusion), channel_id=1, source_target_pairs={{0,1},{1,2},{2,3},{3,4},{4,5},{5,6},{6,7},{7,0},{8,9},{9,10},{10,1... | collective-permute-start | bytes 1376264 | tf_op jit(solution)/shard_map/ppermute | solution.py:25
  26.9 12.0 %collective-permute-start.7 = (bf16[64,3584]{1,0:T(8,128)(2,1)S(1)}, bf16[64,3584]{1,0:T(8,128)(2,1)S(1)}, u32[]{:S(2)}, u32[]{:S(2)}) collective-permute-start(bf16[64,3584]{1,0:T(8,128)(2,1)S(1)} %collective-permute-done.6), channel_id=1, source_target_pairs={{0,7},{1,0},{2,1},{3,2},{4,3},{5,4},{6,5},{7,6},{8,15},{9,8},{10,9... | collective-permute-start | bytes 1376264 | tf_op jit(solution)/shard_map/ppermute | solution.py:25
  32.2 12.0 %collective-permute-start.2 = (bf16[64,3584]{1,0:T(8,128)(2,1)S(1)}, bf16[64,3584]{1,0:T(8,128)(2,1)S(1)}, u32[]{:S(2)}, u32[]{:S(2)}) collective-permute-start(bf16[64,3584]{1,0:T(8,128)(2,1)S(1)} %collective-permute-done.1), channel_id=1, source_target_pairs={{0,1},{1,2},{2,3},{3,4},{4,5},{5,6},{6,7},{7,0},{8,9},{9,10},{10,1... | collective-permute-start | bytes 1376264 | tf_op jit(solution)/shard_map/ppermute | solution.py:25
  38.9 11.1 %collective-permute-start.8 = (bf16[64,3584]{1,0:T(8,128)(2,1)S(1)}, bf16[64,3584]{1,0:T(8,128)(2,1)S(1)}, u32[]{:S(2)}, u32[]{:S(2)}) collective-permute-start(bf16[64,3584]{1,0:T(8,128)(2,1)S(1)} %collective-permute-done.7), channel_id=1, source_target_pairs={{0,7},{1,0},{2,1},{3,2},{4,3},{5,4},{6,5},{7,6},{8,15},{9,8},{10,9... | collective-permute-start | bytes 1376264 | tf_op jit(solution)/shard_map/ppermute | solution.py:25
  44.3 11.1 %collective-permute-start.3 = (bf16[64,3584]{1,0:T(8,128)(2,1)S(1)}, bf16[64,3584]{1,0:T(8,128)(2,1)S(1)}, u32[]{:S(2)}, u32[]{:S(2)}) collective-permute-start(bf16[64,3584]{1,0:T(8,128)(2,1)S(1)} %collective-permute-done.2), channel_id=1, source_target_pairs={{0,1},{1,2},{2,3},{3,4},{4,5},{5,6},{6,7},{7,0},{8,9},{9,10},{10,1... | collective-permute-start | bytes 1376264 | tf_op jit(solution)/shard_map/ppermute | solution.py:25
  50.1 12.8 %collective-permute-start.9 = (bf16[32,3584]{1,0:T(8,128)(2,1)S(1)}, bf16[32,3584]{1,0:T(8,128)(2,1)S(1)}, u32[]{:S(2)}, u32[]{:S(2)}) collective-permute-start(bf16[32,3584]{1,0:T(8,128)(2,1)S(1)} %slice.96), channel_id=1, source_target_pairs={{0,7},{1,0},{2,1},{3,2},{4,3},{5,4},{6,5},{7,6},{8,15},{9,8},{10,9... | collective-permute-start | bytes 688136 | tf_op jit(solution)/shard_map/ppermute | solution.py:25
  55.6 8.0 %collective-permute-start.5 = (bf16[32,3584]{1,0:T(8,128)(2,1)S(1)}, bf16[32,3584]{1,0:T(8,128)(2,1)S(1)}, u32[]{:S(2)}, u32[]{:S(2)}) collective-permute-start(bf16[32,3584]{1,0:T(8,128)(2,1)S(1)} %slice.72), channel_id=1, source_target_pairs={{0,1},{1,2},{2,3},{3,4},{4,5},{5,6},{6,7},{7,0},{8,9},{9,10},{10,1... | collective-permute-start | bytes 688136 | tf_op jit(solution)/shard_map/ppermute | solution.py:25
  61.7 1.1 copy-start.6
  63.5 3.5 %copy-start = (bf16[32,3584]{1,0:T(8,128)(2,1)}, bf16[32,3584]{1,0:T(8,128)(2,1)S(1)}, u32[]{:S(2)}) copy-start(bf16[32,3584]{1,0:T(8,128)(2,1)S(1)} %collective-permute-done.5.right_ref.right_any) | copy-start | bytes 688132
  67.1 0.7 copy-start.2
  67.8 0.8 copy-start.4
  68.6 12.8 %collective-permute-start.10 = (bf16[128,1792]{1,0:T(8,128)(2,1)S(1)}, bf16[128,1792]{1,0:T(8,128)(2,1)S(1)}, u32[]{:S(2)}, u32[]{:S(2)}) collective-permute-start(bf16[128,1792]{1,0:T(8,128)(2,1)S(1)} %get-tuple-element.33), channel_id=1, source_target_pairs={{0,8},{1,9},{2,10},{3,11},{4,12},{5,13},{6,14},{7,15},{8,0},{9,1},... | collective-permute-start | bytes 1376264 | tf_op jit(solution)/shard_map/ppermute | solution.py:21
  72.3 6.3 %copy-start.3 = (bf16[64,1792]{1,0:T(8,128)(2,1)S(1)}, bf16[64,1792]{1,0:T(8,128)(2,1)}, u32[]{:S(2)}) copy-start(bf16[64,1792]{1,0:T(8,128)(2,1)} %copy-done.2) | copy-start | bytes 688132
  72.3 9.1 %copy-start.5 = (bf16[192,1792]{1,0:T(8,128)(2,1)S(1)}, bf16[192,1792]{1,0:T(8,128)(2,1)}, u32[]{:S(2)}) copy-start(bf16[192,1792]{1,0:T(8,128)(2,1)} %copy-done.4) | copy-start | bytes 2064388
  72.3 52.3 %all-to-all-start = ((bf16[16,16,3584]{2,1,0:T(8,128)(2,1)}), bf16[16,16,3584]{2,1,0:T(8,128)(2,1)}, u32[]{:S(2)}, u32[]{:S(2)}) async-start(bf16[16,16,3584]{2,1,0:T(8,128)(2,1)} %bitcast.29), calls=%async_computation | async-start | bytes 3670016 | tf_op jit(solution)/shard_map/all_to_all | solution.py:372
  78.6 25.0 %collective-permute-start.13 = (bf16[64,1792]{1,0:T(8,128)(2,1)S(1)}, bf16[64,1792]{1,0:T(8,128)(2,1)S(1)}, u32[]{:S(2)}, u32[]{:S(2)}) collective-permute-start(bf16[64,1792]{1,0:T(8,128)(2,1)S(1)} %copy-done.3), channel_id=1, source_target_pairs={{0,8},{1,9},{2,10},{3,11},{4,12},{5,13},{6,14},{7,15},{8,0},{9,1},... | collective-permute-start | bytes 688136 | tf_op jit(solution)/shard_map/ppermute | solution.py:21
  81.4 18.4 %copy-start.1 = (bf16[32,3584]{1,0:T(8,128)(2,1)S(1)}, bf16[32,3584]{1,0:T(8,128)(2,1)}, u32[]{:S(2)}) copy-start(bf16[32,3584]{1,0:T(8,128)(2,1)} %copy-done) | copy-start | bytes 688132
  81.4 18.3 %copy-start.7 = (bf16[384,1792]{1,0:T(8,128)(2,1)S(1)}, bf16[384,1792]{1,0:T(8,128)(2,1)}, u32[]{:S(2)}) copy-start(bf16[384,1792]{1,0:T(8,128)(2,1)} %copy-done.6) | copy-start | bytes 4128772
  81.5 42.0 %collective-permute-start.12 = (bf16[128,1792]{1,0:T(8,128)(2,1)S(1)}, bf16[128,1792]{1,0:T(8,128)(2,1)S(1)}, u32[]{:S(2)}, u32[]{:S(2)}) collective-permute-start(bf16[128,1792]{1,0:T(8,128)(2,1)S(1)} %shard_map.105), channel_id=1, source_target_pairs={{0,480},{32,448},{64,416},{96,384},{128,352},{160,320},{192,288},{... | collective-permute-start | bytes 1376264 | tf_op jit(solution)/shard_map/ppermute | solution.py:32
  101.7 21.9 %collective-permute-start.11 = (bf16[192,1792]{1,0:T(8,128)(2,1)S(1)}, bf16[192,1792]{1,0:T(8,128)(2,1)S(1)}, u32[]{:S(2)}, u32[]{:S(2)}) collective-permute-start(bf16[192,1792]{1,0:T(8,128)(2,1)S(1)} %get-tuple-element.36), channel_id=1, source_target_pairs={{0,8},{1,9},{2,10},{3,11},{4,12},{5,13},{6,14},{7,15},{8,0},{9,1},... | collective-permute-start | bytes 2064392 | tf_op jit(solution)/shard_map/ppermute | solution.py:21
  103.7 20.9 %copy-start.8 = (bf16[1,128,3584]{2,1,0:T(8,128)(2,1)S(1)}, bf16[1,128,3584]{2,1,0:T(8,128)(2,1)}, u32[]{:S(2)}) copy-start(bf16[1,128,3584]{2,1,0:T(8,128)(2,1)} %param.8) | copy-start | bytes 2752516
  103.7 20.9 %copy-start.13 = (bf16[256,128]{1,0:T(8,128)(2,1)S(1)}, bf16[256,128]{1,0:T(8,128)(2,1)}, u32[]{:S(2)}) copy-start(bf16[256,128]{1,0:T(8,128)(2,1)} %get-tuple-element.21) | copy-start | bytes 196612
  103.7 19.8 %collective-permute-start.14 = (bf16[64,1792]{1,0:T(8,128)(2,1)S(1)}, bf16[64,1792]{1,0:T(8,128)(2,1)S(1)}, u32[]{:S(2)}, u32[]{:S(2)}) collective-permute-start(bf16[64,1792]{1,0:T(8,128)(2,1)S(1)} %shard_map.107), channel_id=1, source_target_pairs={{0,480},{32,448},{64,416},{96,384},{128,352},{160,320},{192,288},{... | collective-permute-start | bytes 688136 | tf_op jit(solution)/shard_map/ppermute | solution.py:32

commit v5 on v4

--- a/solution.py
+++ b/solution.py
@@ -163,28 +163,24 @@
 
 
 def far_kernel(
-    place_ref, right_ref, left_ref, mine_any, theirs_any, send_any, partial_any,
-    partial_out, first_ref, second_ref, own_ref, hidden_ref, cot_ref,
-    mine_ref, theirs_ref, send_ref, rows_ref, sems,
+    place_ref, right_ref, left_ref, mine_ref, theirs_ref, send_any, partial_any,
+    partial_out, first_ref, second_ref, own_ref,
+    send_ref, rows_ref, sems,
 ):
-    loads = ((mine_any, mine_ref), (theirs_any, theirs_ref), (send_any, send_ref))
-    loads = [pltpu.make_async_copy(src, dst, sems.at[i]) for i, (src, dst) in enumerate(loads)]
-    for copy in loads:
-        copy.start()
+    load = pltpu.make_async_copy(send_any, send_ref, sems.at[0])
+    load.start()
     h = mine_ref.shape[0] // 3
     half = first_ref.shape[1]
     tile = half // TILES
     y, expert, upper = place_ref[0], place_ref[1], place_ref[2]
 
-    loads[0].wait()
-    loads[1].wait()
     w_gu, w_d = weights(mine_ref, theirs_ref)
     everything = slice(0, 2 * half)
     rows_x = pair(right_ref, left_ref, 0, everything)
     rows_c = pair(right_ref, left_ref, CAP, everything)
     hidden, gu_cot = activations(rows_x, rows_c, w_gu, w_d)
-    hidden_ref[...] = hidden
-    cot_ref[...] = gu_cot
+    own_ref[3 * h :, : 2 * h] = hidden
+    own_ref[3 * h :, 2 * h : 6 * h] = gu_cot
     for k in range(2 * TILES):
         cols = slice(k * tile, (k + 1) * tile)
         rows_ref[:, cols] = dot(gu_cot, w_gu[:, cols], ((1,), (0,))).astype(BF)
@@ -200,7 +196,7 @@
         stores[-1].start()
 
     hidden_t, gu_t = turn(hidden), turn(gu_cot)
-    loads[2].wait()
+    load.wait()
     for k in range(TILES):
         cols = slice(k * tile, (k + 1) * tile)
         at_cols = pl.ds(pl.multiple_of((1 - upper) * half + k * tile, 128), tile)
@@ -213,22 +209,26 @@
         second_ref[h:, cols] = gu[3 * h :]
         own_ref[:h, cols] = gu[:h]
         own_ref[h : 2 * h, cols] = gu[2 * h : 3 * h]
-        own_ref[2 * h :, cols] = down[:h]
+        own_ref[2 * h : 3 * h, cols] = down[:h]
     for copy in stores:
         copy.wait()
 
 
-def keep_kernel(place_ref, right_any, left_any, hidden_ref, cot_ref, keep_any, own_ref, their_ref, right_ref, left_ref, keep_ref, sems):
-    loads = ((right_any, right_ref), (left_any, left_ref), (keep_any, keep_ref))
+def keep_kernel(
+    place_ref, right_any, left_any, keep_any, sent_any, own_ref, their_ref, right_ref, left_ref, keep_ref, cot_ref, sems
+):
+    rows, units = cot_ref.shape
+    sent = sent_any.at[pl.ds(units // 2, rows), pl.ds(0, units)]
+    loads = ((right_any, right_ref), (left_any, left_ref), (keep_any, keep_ref), (sent, cot_ref))
     loads = [pltpu.make_async_copy(src, dst, sems.at[i]) for i, (src, dst) in enumerate(loads)]
     for copy in loads:
         copy.start()
     h = own_ref.shape[0] // 3
     half = own_ref.shape[1]
     tile = half // TILES
-    hidden_t, gu_t = turn(hidden_ref[...]), turn(cot_ref[...])
     for copy in loads:
         copy.wait()
+    hidden_t, gu_t = turn(cot_ref[:, : 2 * h]), turn(cot_ref[:, 2 * h :])
     for k in range(TILES):
         cols = slice(k * tile, (k + 1) * tile)
         at_cols = pl.ds(pl.multiple_of(place_ref[2] * half + k * tile, 128), tile)
@@ -238,25 +238,26 @@
         down = (down + keep_ref[4 * h :, cols].astype(F32)).astype(BF)
         own_ref[:h, cols] = gu[:h]
         own_ref[h : 2 * h, cols] = gu[2 * h : 3 * h]
-        own_ref[2 * h :, cols] = down[:h]
+        own_ref[2 * h : 3 * h, cols] = down[:h]
         their_ref[:h, cols] = gu[h : 2 * h]
         their_ref[h : 2 * h, cols] = gu[3 * h :]
         their_ref[2 * h :, cols] = down[h:]
 
 
-def kept(place, far, hidden, cot, keep):
+def kept(place, far, keep, sent):
     h, half = keep.shape[0] // 6, keep.shape[1]
     vmem = pl.BlockSpec(memory_space=pltpu.VMEM)
     anywhere = pl.BlockSpec(memory_space=pl.ANY)
     return pl.pallas_call(
         keep_kernel,
         out_shape=(jax.ShapeDtypeStruct((3 * h, half), BF),) * 2,
-        in_specs=[pl.BlockSpec(memory_space=pltpu.SMEM), anywhere, anywhere, vmem, vmem, anywhere],
+        in_specs=[pl.BlockSpec(memory_space=pltpu.SMEM)] + [anywhere] * 4,
         out_specs=(vmem, vmem),
-        scratch_shapes=[pltpu.VMEM(v.shape, BF) for v in (*far, keep)] + [pltpu.SemaphoreType.DMA((3,))],
+        scratch_shapes=[pltpu.VMEM(v.shape, BF) for v in (*far, keep)]
+        + [pltpu.VMEM((far[0].shape[0], 6 * h), BF), pltpu.SemaphoreType.DMA((4,))],
         compiler_params=pltpu.CompilerParams(vmem_limit_bytes=EXPERT_VMEM * 1024 * 1024),
         cost_estimate=pl.CostEstimate(flops=10**9, bytes_accessed=8 * 2**20, transcendentals=0),
-    )(place, *far, hidden, cot, keep)
+    )(place, *far, keep, sent)
 
 
 def experts(place, rows_x, rows_c, far, mine, theirs):
@@ -282,16 +283,56 @@
     rows = near[0].shape[0] // NY
     outs = pl.pallas_call(
         far_kernel,
-        out_shape=near[:1] + arrays((h, half), (2 * h, half), (3 * h, half), (rows, 2 * h), (rows, 4 * h)),
-        in_specs=[smem] + [vmem] * 2 + [anywhere] * 4,
-        out_specs=(anywhere,) + (vmem,) * 5,
-        scratch_shapes=[pltpu.VMEM(v.shape, BF) for v in (mine, theirs, send)]
-        + [pltpu.VMEM((rows, width), BF), pltpu.SemaphoreType.DMA((5,))],
+        out_shape=near[:1] + arrays((h, half), (2 * h, half), (3 * h + rows, half)),
+        in_specs=[smem] + [vmem] * 4 + [anywhere] * 2,
+        out_specs=(anywhere,) + (vmem,) * 3,
+        scratch_shapes=[pltpu.VMEM(send.shape, BF), pltpu.VMEM((rows, width), BF), pltpu.SemaphoreType.DMA((5,))],
         input_output_aliases={6: 0},
         compiler_params=params,
         cost_estimate=pl.CostEstimate(flops=2 * 10**9, bytes_accessed=8 * 2**20, transcendentals=0),
     )(place, *far, mine, theirs, send, partial)
     return (*outs, keep)
+
+
+def unpack_kernel(got_any, select_ref, cot_ref, out_any, got_ref, out_ref, sems):
+    tile = got_ref.shape[1] // UNPACK_STEPS
+    blocks = [pl.ds(k * tile, tile) for k in range(UNPACK_STEPS)]
+    loads = [
+        pltpu.make_async_copy(got_any.at[:, cols], got_ref.at[:, cols], sems.at[0, k])
+        for k, cols in enumerate(blocks)
+    ]
+    stores = [
+        pltpu.make_async_copy(out_ref.at[:, cols], out_any.at[:, cols], sems.at[1, k])
+        for k, cols in enumerate(blocks)
+    ]
+    for copy in loads:
+        copy.start()
+    places = turn(select_ref[...])
+    for cols, load, store in zip(blocks, loads, stores):
+        load.wait()
+        branch = dot(places, got_ref[:, cols], ((1,), (0,)))
+        out_ref[:, cols] = (cot_ref[:, cols].astype(F32) + branch).astype(BF)
+        store.start()
+    for copy in stores:
+        copy.wait()
+
+
+def unpack(got, select, block_cot):
+    vmem = pl.BlockSpec(memory_space=pltpu.VMEM)
+    anywhere = pl.BlockSpec(memory_space=pl.ANY)
+    return pl.pallas_call(
+        unpack_kernel,
+        out_shape=jax.ShapeDtypeStruct(block_cot.shape, BF),
+        in_specs=[anywhere, vmem, vmem],
+        out_specs=anywhere,
+        scratch_shapes=[
+            pltpu.VMEM(got.shape, BF),
+            pltpu.VMEM(block_cot.shape, BF),
+            pltpu.SemaphoreType.DMA((2, UNPACK_STEPS)),
+        ],
+        compiler_params=pltpu.CompilerParams(vmem_limit_bytes=16 * 1024 * 1024),
+        cost_estimate=pl.CostEstimate(flops=10**9, bytes_accessed=4 * 2**20, transcendentals=0),
+    )(got, select, block_cot)
 
 
 def add_kernel(a_ref, b_ref, out_ref):
@@ -351,7 +392,7 @@
 
     place = jnp.stack([lax.axis_index("ep") % NY, own_expert, upper.astype(jnp.int32)])
     place = place.astype(jnp.int32)
-    partial, their_send_d, their_send, own, hidden, cot, keep = experts(
+    partial, their_send_d, their_send, own, keep = experts(
         place, rows_x, rows_c, (right, left), mine, theirs
     )
 
@@ -365,15 +406,15 @@
         keep = after(keep, to_mirror)
     if X_LAST == 2:
         keep = after(keep, to_mirror, to_mirror_d)
-    own_keep, their_keep = kept(place, (right, left), hidden, cot, keep)
+    own_keep, their_keep = kept(place, (right, left), keep, own)
     got_keep = swap_x_pair(their_keep)
 
     groups = [[x * NY + k for x in pair for k in range(NY)] for pair in ((0, 3), (1, 2))]
     got = lax.all_to_all(
         partial.reshape(2 * NY, CAP, width), "ep", 0, 0, axis_index_groups=groups, tiled=True
     )
-    branch = dot(select, got.reshape(2 * NY * CAP, width), ((0,), (0,)))
-    input_grad = (block_cot.astype(F32) + branch).astype(BF)[None]
+    input_grad = unpack(got.reshape(2 * NY * CAP, width), select, block_cot)[None]
+
     def total(kept, near, far):
         return (kept.astype(F32) + near.astype(F32) + far.astype(F32)).astype(BF)[None]
 
@@ -391,6 +432,7 @@
 WEIGHT_SIDE = 0
 FAR = NY // 2
 ORDER = (5, 3, 6, 2, 7, 1, 0)
+UNPACK_STEPS = 4
 FIRST_COST = 100
 SECOND_COST = 100
 EXPERT_VMEM = 16

time: 128 us -> 128 us (level)
  matrix products: 2.86 us -> 0 us
  Pallas kernels: 12.2 us -> 14.6 us
    dot_general x1 -> x0, matrix products: 2.86 us -> none  [dot(): return lax.dot_general(a, b, (dims, ((), ())), preferred_element_type=F32)]
    pallas_call x0 -> x1, Pallas kernels: none -> 2.73 us  [unpack(): pl.pallas_call(unpack_kernel, out_shape=jax.ShapeDtypeStruct(block_cot.sh...]
where the time goes in v5:
time: 128 us; the launch traced here: 127 us
  starting transfers between devices  72.7 us (57%)
  waiting for transfers between devices  34.1 us (27%)
  Pallas kernels  14.6 us (11%)
  local copies, waits for them, and re-layouts  3.27 us (3%)
    ppermute x8, starting transfers between devices, shift_y(): lax.ppermute(v, 'ep', [(i, i // NY * NY + (i + step) % NY) for i in range...  30.5 us
    ppermute x2, starting transfers between devices, mirror(): return lax.ppermute(v, 'pp', [(i, n - 1 - i) for i in range(n)])  20.3 us
    ppermute x2, waiting for transfers between devices, mirror(): return lax.ppermute(v, 'pp', [(i, n - 1 - i) for i in range(n)])  17.8 us
    ppermute x8, waiting for transfers between devices, shift_y(): lax.ppermute(v, 'ep', [(i, i // NY * NY + (i + step) % NY) for i in range...  14.8 us
    ppermute x4, starting transfers between devices, swap_x_pair(): return lax.ppermute(v, 'ep', [(i, i ^ NY) for i in range(NX * NY)])  10.3 us
    all_to_all x1, starting transfers between devices, shards(): lax.all_to_all(partial.reshape(2 * NY, CAP, width), 'ep', 0, 0, axis_inde...  6.29 us
    ppermute x1, starting transfers between devices, swap_x_outer(): lax.ppermute(v, 'ep', [(i, (NX - 1 - i // NY) * NY + i % NY) for i in ran...  5.35 us
    pallas_call x1, Pallas kernels, experts(): pl.pallas_call(near_kernel, out_shape=near, in_specs=[smem] + [vmem] * 4,...  3.94 us
  transfers between devices with their start and end apart: 16, of which 6 were waited for; matrix products, arithmetic and copies ran while one was open for 1% of the time, Pallas kernels for 5%

profile of v5, /device:TPU:1, one launch (start us, length us, event | category | flops | bytes accessed | tf_op | source)
XLA Modules:
  0.0 127.0 jit_solution(8554531729074230773)
XLA Ops:
  0.6 0.0 copy-start.10
  0.6 0.0 copy-start.11
  0.7 0.0 copy-start.12
  0.7 2.6 %shard_map.102 = (bf16[32,3584]{1,0:T(8,128)(2,1)}, bf16[32,3584]{1,0:T(8,128)(2,1)}, bf16[256,128]{1,0:T(8,128)(2,1)}) custom-call(s32[1]{0:T(128)} %bitcast.1.expert_ref, s32[1,128]{1,0:T(1,128)} %slot_hbm.1, s32[1,128]{1,0:T(1,128)} %gate_hbm.1, bf16[128,3584]{1,0:T(8,128)(2,1)} %bitcast.58, bf16[128,3584]{1,0:T(8,128)(2,1)} %bitcast.38), custom_call_target="tpu_custom_call" | custom-call | tf_op jit(solution)/shard_map/pallas_call | solution.py:92
  3.3 0.0 copy-start.13
  3.3 5.4 %collective-permute-start = (bf16[32,3584]{1,0:T(8,128)(2,1)}, bf16[32,3584]{1,0:T(8,128)(2,1)S(1)}, u32[]{:S(2)}, u32[]{:S(2)}) collective-permute-start(bf16[32,3584]{1,0:T(8,128)(2,1)} %get-tuple-element.20), channel_id=1, source_target_pairs={{0,24},{1,25},{2,26},{3,27},{4,28},{5,29},{6,30},{7,31},{8,16},{9,... | collective-permute-start | bytes 688136 | tf_op jit(solution)/shard_map/ppermute | solution.py:17
  8.7 0.0 copy-done.10
  8.7 0.0 copy-done.11
  8.7 0.0 copy-done.12
  8.7 0.1 pad_maximum_fusion.mine_ref
  8.8 1.9 %collective-permute-start.4 = (bf16[192,3584]{1,0:T(8,128)(2,1)S(1)}, bf16[192,3584]{1,0:T(8,128)(2,1)S(1)}, u32[]{:S(2)}, u32[]{:S(2)}) collective-permute-start(bf16[192,3584]{1,0:T(8,128)(2,1)S(1)} %pad_maximum_fusion.mine_ref), channel_id=1, source_target_pairs={{0,8},{1,9},{2,10},{3,11},{4,12},{5,13},{6,14},{7,15},{8,0},{9,1},... | collective-permute-start | bytes 4128776 | tf_op jit(solution)/shard_map/ppermute | solution.py:21
  10.8 0.0 copy-done.13
  10.8 0.1 pad_add_fusion.place_ref
  10.9 1.4 %collective-permute-done = bf16[32,3584]{1,0:T(8,128)(2,1)S(1)} collective-permute-done((bf16[32,3584]{1,0:T(8,128)(2,1)}, bf16[32,3584]{1,0:T(8,128)(2,1)S(1)}, u32[]{:S(2)}, u32[]{:S(2)}) %collective-permute-start) | collective-permute-done | bytes 229408 | tf_op jit(solution)/shard_map/ppermute | solution.py:17
  12.3 6.9 %collective-permute-start.6 = (bf16[64,3584]{1,0:T(8,128)(2,1)S(1)}, bf16[64,3584]{1,0:T(8,128)(2,1)S(1)}, u32[]{:S(2)}, u32[]{:S(2)}) collective-permute-start(bf16[64,3584]{1,0:T(8,128)(2,1)S(1)} %constant_dynamic-update-slice_fusion), channel_id=1, source_target_pairs={{0,7},{1,0},{2,1},{3,2},{4,3},{5,4},{6,5},{7,6},{8,15},{9,8},{10,9... | collective-permute-start | bytes 1376264 | tf_op jit(solution)/shard_map/ppermute | solution.py:25
  19.2 1.9 %collective-permute-start.1 = (bf16[64,3584]{1,0:T(8,128)(2,1)S(1)}, bf16[64,3584]{1,0:T(8,128)(2,1)S(1)}, u32[]{:S(2)}, u32[]{:S(2)}) collective-permute-start(bf16[64,3584]{1,0:T(8,128)(2,1)S(1)} %constant_dynamic-update-slice_fusion), channel_id=1, source_target_pairs={{0,1},{1,2},{2,3},{3,4},{4,5},{5,6},{6,7},{7,0},{8,9},{9,10},{10,1... | collective-permute-start | bytes 1376264 | tf_op jit(solution)/shard_map/ppermute | solution.py:25
  21.2 5.7 %collective-permute-done.6 = bf16[64,3584]{1,0:T(8,128)(2,1)S(1)} collective-permute-done((bf16[64,3584]{1,0:T(8,128)(2,1)S(1)}, bf16[64,3584]{1,0:T(8,128)(2,1)S(1)}, u32[]{:S(2)}, u32[]{:S(2)}) %collective-permute-start.6) | collective-permute-done | bytes 458784 | tf_op jit(solution)/shard_map/ppermute | solution.py:25
  26.9 5.3 %collective-permute-start.7 = (bf16[64,3584]{1,0:T(8,128)(2,1)S(1)}, bf16[64,3584]{1,0:T(8,128)(2,1)S(1)}, u32[]{:S(2)}, u32[]{:S(2)}) collective-permute-start(bf16[64,3584]{1,0:T(8,128)(2,1)S(1)} %collective-permute-done.6), channel_id=1, source_target_pairs={{0,7},{1,0},{2,1},{3,2},{4,3},{5,4},{6,5},{7,6},{8,15},{9,8},{10,9... | collective-permute-start | bytes 1376264 | tf_op jit(solution)/shard_map/ppermute | solution.py:25
  32.2 0.0 collective-permute-done.1
  32.2 1.9 %collective-permute-start.2 = (bf16[64,3584]{1,0:T(8,128)(2,1)S(1)}, bf16[64,3584]{1,0:T(8,128)(2,1)S(1)}, u32[]{:S(2)}, u32[]{:S(2)}) collective-permute-start(bf16[64,3584]{1,0:T(8,128)(2,1)S(1)} %collective-permute-done.1), channel_id=1, source_target_pairs={{0,1},{1,2},{2,3},{3,4},{4,5},{5,6},{6,7},{7,0},{8,9},{9,10},{10,1... | collective-permute-start | bytes 1376264 | tf_op jit(solution)/shard_map/ppermute | solution.py:25
  34.2 4.7 %collective-permute-done.7 = bf16[64,3584]{1,0:T(8,128)(2,1)S(1)} collective-permute-done((bf16[64,3584]{1,0:T(8,128)(2,1)S(1)}, bf16[64,3584]{1,0:T(8,128)(2,1)S(1)}, u32[]{:S(2)}, u32[]{:S(2)}) %collective-permute-start.7) | collective-permute-done | bytes 458784 | tf_op jit(solution)/shard_map/ppermute | solution.py:25
  38.9 5.3 %collective-permute-start.8 = (bf16[64,3584]{1,0:T(8,128)(2,1)S(1)}, bf16[64,3584]{1,0:T(8,128)(2,1)S(1)}, u32[]{:S(2)}, u32[]{:S(2)}) collective-permute-start(bf16[64,3584]{1,0:T(8,128)(2,1)S(1)} %collective-permute-done.7), channel_id=1, source_target_pairs={{0,7},{1,0},{2,1},{3,2},{4,3},{5,4},{6,5},{7,6},{8,15},{9,8},{10,9... | collective-permute-start | bytes 1376264 | tf_op jit(solution)/shard_map/ppermute | solution.py:25
  44.2 0.0 collective-permute-done.2
  44.2 1.9 %collective-permute-start.3 = (bf16[64,3584]{1,0:T(8,128)(2,1)S(1)}, bf16[64,3584]{1,0:T(8,128)(2,1)S(1)}, u32[]{:S(2)}, u32[]{:S(2)}) collective-permute-start(bf16[64,3584]{1,0:T(8,128)(2,1)S(1)} %collective-permute-done.2), channel_id=1, source_target_pairs={{0,1},{1,2},{2,3},{3,4},{4,5},{5,6},{6,7},{7,0},{8,9},{9,10},{10,1... | collective-permute-start | bytes 1376264 | tf_op jit(solution)/shard_map/ppermute | solution.py:25
  46.2 3.8 %collective-permute-done.8 = bf16[64,3584]{1,0:T(8,128)(2,1)S(1)} collective-permute-done((bf16[64,3584]{1,0:T(8,128)(2,1)S(1)}, bf16[64,3584]{1,0:T(8,128)(2,1)S(1)}, u32[]{:S(2)}, u32[]{:S(2)}) %collective-permute-start.8) | collective-permute-done | bytes 458784 | tf_op jit(solution)/shard_map/ppermute | solution.py:25
  50.0 5.3 %collective-permute-start.9 = (bf16[32,3584]{1,0:T(8,128)(2,1)S(1)}, bf16[32,3584]{1,0:T(8,128)(2,1)S(1)}, u32[]{:S(2)}, u32[]{:S(2)}) collective-permute-start(bf16[32,3584]{1,0:T(8,128)(2,1)S(1)} %slice.96), channel_id=1, source_target_pairs={{0,7},{1,0},{2,1},{3,2},{4,3},{5,4},{6,5},{7,6},{8,15},{9,8},{10,9... | collective-permute-start | bytes 688136 | tf_op jit(solution)/shard_map/ppermute | solution.py:25
  55.3 0.0 collective-permute-done.3
  55.5 0.0 collective-permute-done.4.theirs_ref
  55.5 1.9 %collective-permute-start.5 = (bf16[32,3584]{1,0:T(8,128)(2,1)S(1)}, bf16[32,3584]{1,0:T(8,128)(2,1)S(1)}, u32[]{:S(2)}, u32[]{:S(2)}) collective-permute-start(bf16[32,3584]{1,0:T(8,128)(2,1)S(1)} %slice.72), channel_id=1, source_target_pairs={{0,1},{1,2},{2,3},{3,4},{4,5},{5,6},{6,7},{7,0},{8,9},{9,10},{10,1... | collective-permute-start | bytes 688136 | tf_op jit(solution)/shard_map/ppermute | solution.py:25
  57.7 3.9 %shard_map.103 = (bf16[256,3584]{1,0:T(8,128)(2,1)}, bf16[384,1792]{1,0:T(8,128)(2,1)S(1)}, bf16[384,1792]{1,0:T(8,128)(2,1)S(1)}) custom-call(s32[3]{0:T(128)S(1)} %pad_add_fusion.place_ref, bf16[224,3584]{1,0:T(8,128)(2,1)S(1)} %get-tuple-element.51.x_ref, bf16[224,3584]{1,0:T(8,128)(2,1)S(1)} %get-tuple-element.52.c_ref, ...), custom_call_target="tpu_custom_call" | custom-call | flops 4000000000 | bytes 16777216 | tf_op jit(solution)/shard_map/pallas_call | solution.py:275
  61.7 1.1 copy-done.6
  62.8 0.0 collective-permute-done.9.left_ref.left_any
  62.8 0.7 collective-permute-done.5.right_ref.right_any
  63.5 3.2 %shard_map.104 = (bf16[256,3584]{1,0:T(8,128)(2,1)}, bf16[64,1792]{1,0:T(8,128)(2,1)S(1)}, bf16[128,1792]{1,0:T(8,128)(2,1)S(1)}, bf16[224,1792]{1,0:T(8,128)(2,1)S(1)}) custom-call(s32[3]{0:T(128)S(1)} %pad_add_fusion.place_ref, bf16[32,3584]{1,0:T(8,128)(2,1)S(1)} %collective-permute-done.5.right_ref.right_any, ...), custom_call_target="tpu_custom_call", output_to_operand_aliasing={{0}: (6, {})} | custom-call | flops 2000000000 | bytes 8388608 | tf_op jit(solution)/shard_map/pallas_call | solution.py:284
  66.7 0.0 copy-done.2
  66.7 0.0 copy-start.4
  66.7 0.7 copy-done.4
  67.4 0.9 copy-done.8
  68.2 3.7 %collective-permute-start.10 = (bf16[128,1792]{1,0:T(8,128)(2,1)S(1)}, bf16[128,1792]{1,0:T(8,128)(2,1)S(1)}, u32[]{:S(2)}, u32[]{:S(2)}) collective-permute-start(bf16[128,1792]{1,0:T(8,128)(2,1)S(1)} %get-tuple-element.29), channel_id=1, source_target_pairs={{0,8},{1,9},{2,10},{3,11},{4,12},{5,13},{6,14},{7,15},{8,0},{9,1},... | collective-permute-start | bytes 1376264 | tf_op jit(solution)/shard_map/ppermute | solution.py:21
  72.0 0.0 copy-start.5
  72.0 0.0 copy-start.9
  72.0 6.3 %all-to-all-start = ((bf16[16,16,3584]{2,1,0:T(8,128)(2,1)}), bf16[16,16,3584]{2,1,0:T(8,128)(2,1)}, u32[]{:S(2)}, u32[]{:S(2)}) async-start(bf16[16,16,3584]{2,1,0:T(8,128)(2,1)} %bitcast.29), calls=%async_computation | async-start | bytes 3670016 | tf_op jit(solution)/shard_map/all_to_all | solution.py:413
  78.3 0.0 copy-done.5
  78.3 2.8 %collective-permute-start.13 = (bf16[64,1792]{1,0:T(8,128)(2,1)S(1)}, bf16[64,1792]{1,0:T(8,128)(2,1)S(1)}, u32[]{:S(2)}, u32[]{:S(2)}) collective-permute-start(bf16[64,1792]{1,0:T(8,128)(2,1)S(1)} %copy-done.5), channel_id=1, source_target_pairs={{0,8},{1,9},{2,10},{3,11},{4,12},{5,13},{6,14},{7,15},{8,0},{9,1},... | collective-permute-start | bytes 688136 | tf_op jit(solution)/shard_map/ppermute | solution.py:21
  81.1 0.0 collective-permute-done.10.b_ref
  81.1 0.0 copy-done.9
  81.1 0.0 copy-start.3
  81.1 0.0 copy-start.7
  81.1 0.1 shard_map.106
  81.2 18.2 %collective-permute-start.12 = (bf16[128,1792]{1,0:T(8,128)(2,1)S(1)}, bf16[128,1792]{1,0:T(8,128)(2,1)S(1)}, u32[]{:S(2)}, u32[]{:S(2)}) collective-permute-start(bf16[128,1792]{1,0:T(8,128)(2,1)S(1)} %shard_map.106), channel_id=1, source_target_pairs={{0,480},{32,448},{64,416},{96,384},{128,352},{160,320},{192,288},{... | collective-permute-start | bytes 1376264 | tf_op jit(solution)/shard_map/ppermute | solution.py:32
  99.4 0.0 copy-done.3
  99.4 0.0 copy-done.7
  99.5 1.9 %shard_map.107 = (bf16[192,1792]{1,0:T(8,128)(2,1)S(1)}, bf16[192,1792]{1,0:T(8,128)(2,1)S(1)}) custom-call(s32[3]{0:T(128)S(1)} %pad_add_fusion.place_ref, bf16[32,3584]{1,0:T(8,128)(2,1)S(1)} %copy-done.3, bf16[32,3584]{1,0:T(8,128)(2,1)S(1)} %collective-permute-done.9.left_ref.left_any, bf16[384,1792]{1,0:T(8,128)(2,1)S(1)} %copy-done.7, ...), custom_call_target="tpu_custom_call" | custom-call | flops 1000000000 | bytes 8388608 | tf_op jit(solution)/shard_map/pallas_call | solution.py:251
  101.4 1.9 %collective-permute-start.11 = (bf16[192,1792]{1,0:T(8,128)(2,1)S(1)}, bf16[192,1792]{1,0:T(8,128)(2,1)S(1)}, u32[]{:S(2)}, u32[]{:S(2)}) collective-permute-start(bf16[192,1792]{1,0:T(8,128)(2,1)S(1)} %get-tuple-element.32), channel_id=1, source_target_pairs={{0,8},{1,9},{2,10},{3,11},{4,12},{5,13},{6,14},{7,15},{8,0},{9,1},... | collective-permute-start | bytes 2064392 | tf_op jit(solution)/shard_map/ppermute | solution.py:21
  103.3 0.0 collective-permute-done.13.b_ref
  103.3 0.1 shard_map.108
  103.4 0.0 copy-start
  103.4 2.1 %collective-permute-start.14 = (bf16[64,1792]{1,0:T(8,128)(2,1)S(1)}, bf16[64,1792]{1,0:T(8,128)(2,1)S(1)}, u32[]{:S(2)}, u32[]{:S(2)}) collective-permute-start(bf16[64,1792]{1,0:T(8,128)(2,1)S(1)} %shard_map.108), channel_id=1, source_target_pairs={{0,480},{32,448},{64,416},{96,384},{128,352},{160,320},{192,288},{... | collective-permute-start | bytes 688136 | tf_op jit(solution)/shard_map/ppermute | solution.py:32
  105.5 17.8 %collective-permute-done.14 = bf16[64,1792]{1,0:T(8,128)(2,1)S(1)} collective-permute-done((bf16[64,1792]{1,0:T(8,128)(2,1)S(1)}, bf16[64,1792]{1,0:T(8,128)(2,1)S(1)}, u32[]{:S(2)}, u32[]{:S(2)}) %collective-permute-start.14) | collective-permute-done | bytes 229408 | tf_op jit(solution)/shard_map/ppermute | solution.py:32
  123.2 0.0 collective-permute-done.12
  123.2 0.0 collective-permute-done.11
  123.2 1.0 fusion.1
  124.3 0.0 all-to-all-done
  124.3 2.7 %shard_map.105 = bf16[128,3584]{1,0:T(8,128)(2,1)} custom-call(bf16[256,3584]{1,0:T(8,128)(2,1)} %bitcast.30.got_any, bf16[256,128]{1,0:T(8,128)(2,1)S(1)} %copy-done.1, bf16[128,3584]{1,0:T(8,128)(2,1)S(1)} %bitcast.39), custom_call_target="tpu_custom_call" | custom-call | flops 1000000000 | bytes 4194304 | tf_op jit(solution)/shard_map/pallas_call | solution.py:323
  (30 shorter events, 0.5 us)
Async XLA Ops:
  0.6 8.1 %copy-start.10 = (bf16[1,64,3584]{2,1,0:T(8,128)(2,1)S(1)}, bf16[1,64,3584]{2,1,0:T(8,128)(2,1)}, u32[]{:S(2)}) copy-start(bf16[1,64,3584]{2,1,0:T(8,128)(2,1)} %param.13) | copy-start | bytes 1376260
  0.6 8.1 %copy-start.11 = (bf16[1,64,3584]{2,1,0:T(8,128)(2,1)S(1)}, bf16[1,64,3584]{2,1,0:T(8,128)(2,1)}, u32[]{:S(2)}) copy-start(bf16[1,64,3584]{2,1,0:T(8,128)(2,1)} %param.12) | copy-start | bytes 1376260
  0.7 8.1 %copy-start.12 = (bf16[1,64,3584]{2,1,0:T(8,128)(2,1)S(1)}, bf16[1,64,3584]{2,1,0:T(8,128)(2,1)}, u32[]{:S(2)}) copy-start(bf16[1,64,3584]{2,1,0:T(8,128)(2,1)} %param.11) | copy-start | bytes 1376260
  3.3 7.4 %copy-start.13 = (bf16[32,3584]{1,0:T(8,128)(2,1)S(1)}, bf16[32,3584]{1,0:T(8,128)(2,1)}, u32[]{:S(2)}) copy-start(bf16[32,3584]{1,0:T(8,128)(2,1)} %get-tuple-element.19) | copy-start | bytes 688132
  3.3 9.0 %collective-permute-start = (bf16[32,3584]{1,0:T(8,128)(2,1)}, bf16[32,3584]{1,0:T(8,128)(2,1)S(1)}, u32[]{:S(2)}, u32[]{:S(2)}) collective-permute-start(bf16[32,3584]{1,0:T(8,128)(2,1)} %get-tuple-element.20), channel_id=1, source_target_pairs={{0,24},{1,25},{2,26},{3,27},{4,28},{5,29},{6,30},{7,31},{8,16},{9,... | collective-permute-start | bytes 688136 | tf_op jit(solution)/shard_map/ppermute | solution.py:17
  8.8 46.7 %collective-permute-start.4 = (bf16[192,3584]{1,0:T(8,128)(2,1)S(1)}, bf16[192,3584]{1,0:T(8,128)(2,1)S(1)}, u32[]{:S(2)}, u32[]{:S(2)}) collective-permute-start(bf16[192,3584]{1,0:T(8,128)(2,1)S(1)} %pad_maximum_fusion.mine_ref), channel_id=1, source_target_pairs={{0,8},{1,9},{2,10},{3,11},{4,12},{5,13},{6,14},{7,15},{8,0},{9,1},... | collective-permute-start | bytes 4128776 | tf_op jit(solution)/shard_map/ppermute | solution.py:21
  12.3 14.5 %collective-permute-start.6 = (bf16[64,3584]{1,0:T(8,128)(2,1)S(1)}, bf16[64,3584]{1,0:T(8,128)(2,1)S(1)}, u32[]{:S(2)}, u32[]{:S(2)}) collective-permute-start(bf16[64,3584]{1,0:T(8,128)(2,1)S(1)} %constant_dynamic-update-slice_fusion), channel_id=1, source_target_pairs={{0,7},{1,0},{2,1},{3,2},{4,3},{5,4},{6,5},{7,6},{8,15},{9,8},{10,9... | collective-permute-start | bytes 1376264 | tf_op jit(solution)/shard_map/ppermute | solution.py:25
  19.2 13.0 %collective-permute-start.1 = (bf16[64,3584]{1,0:T(8,128)(2,1)S(1)}, bf16[64,3584]{1,0:T(8,128)(2,1)S(1)}, u32[]{:S(2)}, u32[]{:S(2)}) collective-permute-start(bf16[64,3584]{1,0:T(8,128)(2,1)S(1)} %constant_dynamic-update-slice_fusion), channel_id=1, source_target_pairs={{0,1},{1,2},{2,3},{3,4},{4,5},{5,6},{6,7},{7,0},{8,9},{9,10},{10,1... | collective-permute-start | bytes 1376264 | tf_op jit(solution)/shard_map/ppermute | solution.py:25
  26.9 12.0 %collective-permute-start.7 = (bf16[64,3584]{1,0:T(8,128)(2,1)S(1)}, bf16[64,3584]{1,0:T(8,128)(2,1)S(1)}, u32[]{:S(2)}, u32[]{:S(2)}) collective-permute-start(bf16[64,3584]{1,0:T(8,128)(2,1)S(1)} %collective-permute-done.6), channel_id=1, source_target_pairs={{0,7},{1,0},{2,1},{3,2},{4,3},{5,4},{6,5},{7,6},{8,15},{9,8},{10,9... | collective-permute-start | bytes 1376264 | tf_op jit(solution)/shard_map/ppermute | solution.py:25
  32.2 12.0 %collective-permute-start.2 = (bf16[64,3584]{1,0:T(8,128)(2,1)S(1)}, bf16[64,3584]{1,0:T(8,128)(2,1)S(1)}, u32[]{:S(2)}, u32[]{:S(2)}) collective-permute-start(bf16[64,3584]{1,0:T(8,128)(2,1)S(1)} %collective-permute-done.1), channel_id=1, source_target_pairs={{0,1},{1,2},{2,3},{3,4},{4,5},{5,6},{6,7},{7,0},{8,9},{9,10},{10,1... | collective-permute-start | bytes 1376264 | tf_op jit(solution)/shard_map/ppermute | solution.py:25
  38.9 11.1 %collective-permute-start.8 = (bf16[64,3584]{1,0:T(8,128)(2,1)S(1)}, bf16[64,3584]{1,0:T(8,128)(2,1)S(1)}, u32[]{:S(2)}, u32[]{:S(2)}) collective-permute-start(bf16[64,3584]{1,0:T(8,128)(2,1)S(1)} %collective-permute-done.7), channel_id=1, source_target_pairs={{0,7},{1,0},{2,1},{3,2},{4,3},{5,4},{6,5},{7,6},{8,15},{9,8},{10,9... | collective-permute-start | bytes 1376264 | tf_op jit(solution)/shard_map/ppermute | solution.py:25
  44.2 11.1 %collective-permute-start.3 = (bf16[64,3584]{1,0:T(8,128)(2,1)S(1)}, bf16[64,3584]{1,0:T(8,128)(2,1)S(1)}, u32[]{:S(2)}, u32[]{:S(2)}) collective-permute-start(bf16[64,3584]{1,0:T(8,128)(2,1)S(1)} %collective-permute-done.2), channel_id=1, source_target_pairs={{0,1},{1,2},{2,3},{3,4},{4,5},{5,6},{6,7},{7,0},{8,9},{9,10},{10,1... | collective-permute-start | bytes 1376264 | tf_op jit(solution)/shard_map/ppermute | solution.py:25
  50.0 12.8 %collective-permute-start.9 = (bf16[32,3584]{1,0:T(8,128)(2,1)S(1)}, bf16[32,3584]{1,0:T(8,128)(2,1)S(1)}, u32[]{:S(2)}, u32[]{:S(2)}) collective-permute-start(bf16[32,3584]{1,0:T(8,128)(2,1)S(1)} %slice.96), channel_id=1, source_target_pairs={{0,7},{1,0},{2,1},{3,2},{4,3},{5,4},{6,5},{7,6},{8,15},{9,8},{10,9... | collective-permute-start | bytes 688136 | tf_op jit(solution)/shard_map/ppermute | solution.py:25
  55.5 8.0 %collective-permute-start.5 = (bf16[32,3584]{1,0:T(8,128)(2,1)S(1)}, bf16[32,3584]{1,0:T(8,128)(2,1)S(1)}, u32[]{:S(2)}, u32[]{:S(2)}) collective-permute-start(bf16[32,3584]{1,0:T(8,128)(2,1)S(1)} %slice.72), channel_id=1, source_target_pairs={{0,1},{1,2},{2,3},{3,4},{4,5},{5,6},{6,7},{7,0},{8,9},{9,10},{10,1... | collective-permute-start | bytes 688136 | tf_op jit(solution)/shard_map/ppermute | solution.py:25
  61.7 1.1 copy-start.6
  63.5 3.2 %copy-start.2 = (bf16[32,3584]{1,0:T(8,128)(2,1)}, bf16[32,3584]{1,0:T(8,128)(2,1)S(1)}, u32[]{:S(2)}) copy-start(bf16[32,3584]{1,0:T(8,128)(2,1)S(1)} %collective-permute-done.5.right_ref.right_any) | copy-start | bytes 688132
  66.7 0.7 copy-start.4
  67.4 0.9 copy-start.8
  68.2 12.8 %collective-permute-start.10 = (bf16[128,1792]{1,0:T(8,128)(2,1)S(1)}, bf16[128,1792]{1,0:T(8,128)(2,1)S(1)}, u32[]{:S(2)}, u32[]{:S(2)}) collective-permute-start(bf16[128,1792]{1,0:T(8,128)(2,1)S(1)} %get-tuple-element.29), channel_id=1, source_target_pairs={{0,8},{1,9},{2,10},{3,11},{4,12},{5,13},{6,14},{7,15},{8,0},{9,1},... | collective-permute-start | bytes 1376264 | tf_op jit(solution)/shard_map/ppermute | solution.py:21
  72.0 6.3 %copy-start.5 = (bf16[64,1792]{1,0:T(8,128)(2,1)S(1)}, bf16[64,1792]{1,0:T(8,128)(2,1)}, u32[]{:S(2)}) copy-start(bf16[64,1792]{1,0:T(8,128)(2,1)} %copy-done.4) | copy-start | bytes 688132
  72.0 9.1 %copy-start.9 = (bf16[224,1792]{1,0:T(8,128)(2,1)S(1)}, bf16[224,1792]{1,0:T(8,128)(2,1)}, u32[]{:S(2)}) copy-start(bf16[224,1792]{1,0:T(8,128)(2,1)} %copy-done.8) | copy-start | bytes 2408452
  72.0 52.3 %all-to-all-start = ((bf16[16,16,3584]{2,1,0:T(8,128)(2,1)}), bf16[16,16,3584]{2,1,0:T(8,128)(2,1)}, u32[]{:S(2)}, u32[]{:S(2)}) async-start(bf16[16,16,3584]{2,1,0:T(8,128)(2,1)} %bitcast.29), calls=%async_computation | async-start | bytes 3670016 | tf_op jit(solution)/shard_map/all_to_all | solution.py:413
  78.3 25.0 %collective-permute-start.13 = (bf16[64,1792]{1,0:T(8,128)(2,1)S(1)}, bf16[64,1792]{1,0:T(8,128)(2,1)S(1)}, u32[]{:S(2)}, u32[]{:S(2)}) collective-permute-start(bf16[64,1792]{1,0:T(8,128)(2,1)S(1)} %copy-done.5), channel_id=1, source_target_pairs={{0,8},{1,9},{2,10},{3,11},{4,12},{5,13},{6,14},{7,15},{8,0},{9,1},... | collective-permute-start | bytes 688136 | tf_op jit(solution)/shard_map/ppermute | solution.py:21
  81.1 18.4 %copy-start.3 = (bf16[32,3584]{1,0:T(8,128)(2,1)S(1)}, bf16[32,3584]{1,0:T(8,128)(2,1)}, u32[]{:S(2)}) copy-start(bf16[32,3584]{1,0:T(8,128)(2,1)} %copy-done.2) | copy-start | bytes 688132
  81.1 18.4 %copy-start.7 = (bf16[384,1792]{1,0:T(8,128)(2,1)S(1)}, bf16[384,1792]{1,0:T(8,128)(2,1)}, u32[]{:S(2)}) copy-start(bf16[384,1792]{1,0:T(8,128)(2,1)} %copy-done.6) | copy-start | bytes 4128772
  81.2 42.0 %collective-permute-start.12 = (bf16[128,1792]{1,0:T(8,128)(2,1)S(1)}, bf16[128,1792]{1,0:T(8,128)(2,1)S(1)}, u32[]{:S(2)}, u32[]{:S(2)}) collective-permute-start(bf16[128,1792]{1,0:T(8,128)(2,1)S(1)} %shard_map.106), channel_id=1, source_target_pairs={{0,480},{32,448},{64,416},{96,384},{128,352},{160,320},{192,288},{... | collective-permute-start | bytes 1376264 | tf_op jit(solution)/shard_map/ppermute | solution.py:32
  101.4 21.9 %collective-permute-start.11 = (bf16[192,1792]{1,0:T(8,128)(2,1)S(1)}, bf16[192,1792]{1,0:T(8,128)(2,1)S(1)}, u32[]{:S(2)}, u32[]{:S(2)}) collective-permute-start(bf16[192,1792]{1,0:T(8,128)(2,1)S(1)} %get-tuple-element.32), channel_id=1, source_target_pairs={{0,8},{1,9},{2,10},{3,11},{4,12},{5,13},{6,14},{7,15},{8,0},{9,1},... | collective-permute-start | bytes 2064392 | tf_op jit(solution)/shard_map/ppermute | solution.py:21
  103.4 20.9 %copy-start = (bf16[1,128,3584]{2,1,0:T(8,128)(2,1)S(1)}, bf16[1,128,3584]{2,1,0:T(8,128)(2,1)}, u32[]{:S(2)}) copy-start(bf16[1,128,3584]{2,1,0:T(8,128)(2,1)} %param.8) | copy-start | bytes 2752516
  103.4 20.9 %copy-start.1 = (bf16[256,128]{1,0:T(8,128)(2,1)S(1)}, bf16[256,128]{1,0:T(8,128)(2,1)}, u32[]{:S(2)}) copy-start(bf16[256,128]{1,0:T(8,128)(2,1)} %get-tuple-element.26.select_ref) | copy-start | bytes 196612
  103.4 19.8 %collective-permute-start.14 = (bf16[64,1792]{1,0:T(8,128)(2,1)S(1)}, bf16[64,1792]{1,0:T(8,128)(2,1)S(1)}, u32[]{:S(2)}, u32[]{:S(2)}) collective-permute-start(bf16[64,1792]{1,0:T(8,128)(2,1)S(1)} %shard_map.108), channel_id=1, source_target_pairs={{0,480},{32,448},{64,416},{96,384},{128,352},{160,320},{192,288},{... | collective-permute-start | bytes 688136 | tf_op jit(solution)/shard_map/ppermute | solution.py:32

commit v6 on v5

--- a/solution.py
+++ b/solution.py
@@ -204,9 +204,10 @@
         gu = (gu + send_ref[: 4 * h, cols].astype(F32)).astype(BF)
         down = dot(hidden_t, pair(right_ref, left_ref, CAP, at_cols), ((1,), (0,)))
         down = (down + send_ref[4 * h :, cols].astype(F32)).astype(BF)
-        first_ref[:, cols] = down[h:]
         second_ref[:h, cols] = gu[h : 2 * h]
-        second_ref[h:, cols] = gu[3 * h :]
+        second_ref[h:, cols] = gu[3 * h : 3 * h + h // 2]
+        first_ref[: h // 2, cols] = gu[3 * h + h // 2 :]
+        first_ref[h // 2 :, cols] = down[h:]
         own_ref[:h, cols] = gu[:h]
         own_ref[h : 2 * h, cols] = gu[2 * h : 3 * h]
         own_ref[2 * h : 3 * h, cols] = down[:h]
@@ -283,7 +284,7 @@
     rows = near[0].shape[0] // NY
     outs = pl.pallas_call(
         far_kernel,
-        out_shape=near[:1] + arrays((h, half), (2 * h, half), (3 * h + rows, half)),
+        out_shape=near[:1] + arrays((3 * h // 2, half), (3 * h // 2, half), (3 * h + rows, half)),
         in_specs=[smem] + [vmem] * 4 + [anywhere] * 2,
         out_specs=(anywhere,) + (vmem,) * 3,
         scratch_shapes=[pltpu.VMEM(send.shape, BF), pltpu.VMEM((rows, width), BF), pltpu.SemaphoreType.DMA((5,))],
@@ -398,7 +399,7 @@
 
     got_send_d = swap_x_pair(their_send_d)
     got_send = swap_x_pair(their_send)
-    to_mirror_d = add(own, got_send_d, 2, FIRST_COST)
+    to_mirror_d = add(own, got_send_d, 1, FIRST_COST)
     from_mirror_d = mirror(to_mirror_d)
     to_mirror = add(own, got_send, 0, SECOND_COST)
     from_mirror = mirror(to_mirror)
@@ -418,11 +419,12 @@
     def total(kept, near, far):
         return (kept.astype(F32) + near.astype(F32) + far.astype(F32)).astype(BF)[None]
 
+    far_up = jnp.concatenate([from_mirror[h:], from_mirror_d[: h // 2]], axis=0)
     return (
         input_grad,
         total(own_keep[:h], got_keep[:h], from_mirror[:h]),
-        total(own_keep[h : 2 * h], got_keep[h : 2 * h], from_mirror[h:]),
-        total(own_keep[2 * h :], got_keep[2 * h :], from_mirror_d),
+        total(own_keep[h : 2 * h], got_keep[h : 2 * h], far_up),
+        total(own_keep[2 * h :], got_keep[2 * h :], from_mirror_d[h // 2 :]),
     )
 
 

time: 128 us -> 127 us (level)
  waiting for transfers between devices: 34.1 us -> 32.4 us
  starting transfers between devices: 72.7 us -> 74.3 us
    ppermute x2, waiting for transfers between devices: 17.8 us -> 16.1 us  [mirror(): return lax.ppermute(v, 'pp', [(i, n - 1 - i) for i in range(n)])]
    ppermute x2, starting transfers between devices: 20.3 us -> 21.6 us  [mirror(): return lax.ppermute(v, 'pp', [(i, n - 1 - i) for i in range(n)])]
  transfers between devices with their start and end apart: 16 -> 16, of which waited for: 6 -> 7; matrix products, arithmetic and copies ran while one was open for 1% -> 1% of each run, Pallas kernels for 5% -> 5%
where the time goes in v6:
time: 127 us; the launch traced here: 126 us
  starting transfers between devices  74.3 us (59%)
  waiting for transfers between devices  32.4 us (26%)
  Pallas kernels  14.6 us (11%)
  local copies, waits for them, and re-layouts  2.6 us (2%)
    ppermute x8, starting transfers between devices, shift_y(): lax.ppermute(v, 'ep', [(i, i // NY * NY + (i + step) % NY) for i in range...  30.5 us
    ppermute x2, starting transfers between devices, mirror(): return lax.ppermute(v, 'pp', [(i, n - 1 - i) for i in range(n)])  21.6 us
    ppermute x2, waiting for transfers between devices, mirror(): return lax.ppermute(v, 'pp', [(i, n - 1 - i) for i in range(n)])  16.1 us
    ppermute x8, waiting for transfers between devices, shift_y(): lax.ppermute(v, 'ep', [(i, i // NY * NY + (i + step) % NY) for i in range...  14.8 us
    ppermute x4, starting transfers between devices, swap_x_pair(): return lax.ppermute(v, 'ep', [(i, i ^ NY) for i in range(NX * NY)])  10.6 us
    all_to_all x1, starting transfers between devices, shards(): lax.all_to_all(partial.reshape(2 * NY, CAP, width), 'ep', 0, 0, axis_inde...  6.29 us
    ppermute x1, starting transfers between devices, swap_x_outer(): lax.ppermute(v, 'ep', [(i, (NX - 1 - i // NY) * NY + i % NY) for i in ran...  5.35 us
    pallas_call x1, Pallas kernels, experts(): pl.pallas_call(near_kernel, out_shape=near, in_specs=[smem] + [vmem] * 4,...  3.94 us
  transfers between devices with their start and end apart: 16, of which 7 were waited for; matrix products, arithmetic and copies ran while one was open for 1% of the time, Pallas kernels for 5%

profile of v6, /device:TPU:1, one launch (start us, length us, event | category | flops | bytes accessed | tf_op | source)
XLA Modules:
  0.0 126.3 jit_solution(3294516932991671751)
XLA Ops:
  0.6 0.0 copy-start.10
  0.6 0.0 copy-start.11
  0.7 0.0 copy-start.12
  0.7 2.6 %shard_map.102 = (bf16[32,3584]{1,0:T(8,128)(2,1)}, bf16[32,3584]{1,0:T(8,128)(2,1)}, bf16[256,128]{1,0:T(8,128)(2,1)}) custom-call(s32[1]{0:T(128)} %bitcast.1.expert_ref, s32[1,128]{1,0:T(1,128)} %slot_hbm.1, s32[1,128]{1,0:T(1,128)} %gate_hbm.1, bf16[128,3584]{1,0:T(8,128)(2,1)} %bitcast.58, bf16[128,3584]{1,0:T(8,128)(2,1)} %bitcast.38), custom_call_target="tpu_custom_call" | custom-call | tf_op jit(solution)/shard_map/pallas_call | solution.py:92
  3.3 0.0 copy-start.13
  3.3 5.4 %collective-permute-start = (bf16[32,3584]{1,0:T(8,128)(2,1)}, bf16[32,3584]{1,0:T(8,128)(2,1)S(1)}, u32[]{:S(2)}, u32[]{:S(2)}) collective-permute-start(bf16[32,3584]{1,0:T(8,128)(2,1)} %get-tuple-element.20), channel_id=1, source_target_pairs={{0,24},{1,25},{2,26},{3,27},{4,28},{5,29},{6,30},{7,31},{8,16},{9,... | collective-permute-start | bytes 688136 | tf_op jit(solution)/shard_map/ppermute | solution.py:17
  8.7 0.0 copy-done.10
  8.7 0.0 copy-done.11
  8.7 0.0 copy-done.12
  8.7 0.1 pad_maximum_fusion.mine_ref
  8.8 1.9 %collective-permute-start.4 = (bf16[192,3584]{1,0:T(8,128)(2,1)S(1)}, bf16[192,3584]{1,0:T(8,128)(2,1)S(1)}, u32[]{:S(2)}, u32[]{:S(2)}) collective-permute-start(bf16[192,3584]{1,0:T(8,128)(2,1)S(1)} %pad_maximum_fusion.mine_ref), channel_id=1, source_target_pairs={{0,8},{1,9},{2,10},{3,11},{4,12},{5,13},{6,14},{7,15},{8,0},{9,1},... | collective-permute-start | bytes 4128776 | tf_op jit(solution)/shard_map/ppermute | solution.py:21
  10.8 0.0 copy-done.13
  10.8 0.1 pad_add_fusion.place_ref
  10.9 1.4 %collective-permute-done = bf16[32,3584]{1,0:T(8,128)(2,1)S(1)} collective-permute-done((bf16[32,3584]{1,0:T(8,128)(2,1)}, bf16[32,3584]{1,0:T(8,128)(2,1)S(1)}, u32[]{:S(2)}, u32[]{:S(2)}) %collective-permute-start) | collective-permute-done | bytes 229408 | tf_op jit(solution)/shard_map/ppermute | solution.py:17
  12.3 6.9 %collective-permute-start.6 = (bf16[64,3584]{1,0:T(8,128)(2,1)S(1)}, bf16[64,3584]{1,0:T(8,128)(2,1)S(1)}, u32[]{:S(2)}, u32[]{:S(2)}) collective-permute-start(bf16[64,3584]{1,0:T(8,128)(2,1)S(1)} %constant_dynamic-update-slice_fusion), channel_id=1, source_target_pairs={{0,7},{1,0},{2,1},{3,2},{4,3},{5,4},{6,5},{7,6},{8,15},{9,8},{10,9... | collective-permute-start | bytes 1376264 | tf_op jit(solution)/shard_map/ppermute | solution.py:25
  19.2 1.9 %collective-permute-start.1 = (bf16[64,3584]{1,0:T(8,128)(2,1)S(1)}, bf16[64,3584]{1,0:T(8,128)(2,1)S(1)}, u32[]{:S(2)}, u32[]{:S(2)}) collective-permute-start(bf16[64,3584]{1,0:T(8,128)(2,1)S(1)} %constant_dynamic-update-slice_fusion), channel_id=1, source_target_pairs={{0,1},{1,2},{2,3},{3,4},{4,5},{5,6},{6,7},{7,0},{8,9},{9,10},{10,1... | collective-permute-start | bytes 1376264 | tf_op jit(solution)/shard_map/ppermute | solution.py:25
  21.2 5.7 %collective-permute-done.6 = bf16[64,3584]{1,0:T(8,128)(2,1)S(1)} collective-permute-done((bf16[64,3584]{1,0:T(8,128)(2,1)S(1)}, bf16[64,3584]{1,0:T(8,128)(2,1)S(1)}, u32[]{:S(2)}, u32[]{:S(2)}) %collective-permute-start.6) | collective-permute-done | bytes 458784 | tf_op jit(solution)/shard_map/ppermute | solution.py:25
  26.9 5.3 %collective-permute-start.7 = (bf16[64,3584]{1,0:T(8,128)(2,1)S(1)}, bf16[64,3584]{1,0:T(8,128)(2,1)S(1)}, u32[]{:S(2)}, u32[]{:S(2)}) collective-permute-start(bf16[64,3584]{1,0:T(8,128)(2,1)S(1)} %collective-permute-done.6), channel_id=1, source_target_pairs={{0,7},{1,0},{2,1},{3,2},{4,3},{5,4},{6,5},{7,6},{8,15},{9,8},{10,9... | collective-permute-start | bytes 1376264 | tf_op jit(solution)/shard_map/ppermute | solution.py:25
  32.2 0.0 collective-permute-done.1
  32.2 1.9 %collective-permute-start.2 = (bf16[64,3584]{1,0:T(8,128)(2,1)S(1)}, bf16[64,3584]{1,0:T(8,128)(2,1)S(1)}, u32[]{:S(2)}, u32[]{:S(2)}) collective-permute-start(bf16[64,3584]{1,0:T(8,128)(2,1)S(1)} %collective-permute-done.1), channel_id=1, source_target_pairs={{0,1},{1,2},{2,3},{3,4},{4,5},{5,6},{6,7},{7,0},{8,9},{9,10},{10,1... | collective-permute-start | bytes 1376264 | tf_op jit(solution)/shard_map/ppermute | solution.py:25
  34.2 4.7 %collective-permute-done.7 = bf16[64,3584]{1,0:T(8,128)(2,1)S(1)} collective-permute-done((bf16[64,3584]{1,0:T(8,128)(2,1)S(1)}, bf16[64,3584]{1,0:T(8,128)(2,1)S(1)}, u32[]{:S(2)}, u32[]{:S(2)}) %collective-permute-start.7) | collective-permute-done | bytes 458784 | tf_op jit(solution)/shard_map/ppermute | solution.py:25
  38.9 5.3 %collective-permute-start.8 = (bf16[64,3584]{1,0:T(8,128)(2,1)S(1)}, bf16[64,3584]{1,0:T(8,128)(2,1)S(1)}, u32[]{:S(2)}, u32[]{:S(2)}) collective-permute-start(bf16[64,3584]{1,0:T(8,128)(2,1)S(1)} %collective-permute-done.7), channel_id=1, source_target_pairs={{0,7},{1,0},{2,1},{3,2},{4,3},{5,4},{6,5},{7,6},{8,15},{9,8},{10,9... | collective-permute-start | bytes 1376264 | tf_op jit(solution)/shard_map/ppermute | solution.py:25
  44.2 0.0 collective-permute-done.2
  44.2 1.9 %collective-permute-start.3 = (bf16[64,3584]{1,0:T(8,128)(2,1)S(1)}, bf16[64,3584]{1,0:T(8,128)(2,1)S(1)}, u32[]{:S(2)}, u32[]{:S(2)}) collective-permute-start(bf16[64,3584]{1,0:T(8,128)(2,1)S(1)} %collective-permute-done.2), channel_id=1, source_target_pairs={{0,1},{1,2},{2,3},{3,4},{4,5},{5,6},{6,7},{7,0},{8,9},{9,10},{10,1... | collective-permute-start | bytes 1376264 | tf_op jit(solution)/shard_map/ppermute | solution.py:25
  46.2 3.8 %collective-permute-done.8 = bf16[64,3584]{1,0:T(8,128)(2,1)S(1)} collective-permute-done((bf16[64,3584]{1,0:T(8,128)(2,1)S(1)}, bf16[64,3584]{1,0:T(8,128)(2,1)S(1)}, u32[]{:S(2)}, u32[]{:S(2)}) %collective-permute-start.8) | collective-permute-done | bytes 458784 | tf_op jit(solution)/shard_map/ppermute | solution.py:25
  50.0 5.3 %collective-permute-start.9 = (bf16[32,3584]{1,0:T(8,128)(2,1)S(1)}, bf16[32,3584]{1,0:T(8,128)(2,1)S(1)}, u32[]{:S(2)}, u32[]{:S(2)}) collective-permute-start(bf16[32,3584]{1,0:T(8,128)(2,1)S(1)} %slice.104), channel_id=1, source_target_pairs={{0,7},{1,0},{2,1},{3,2},{4,3},{5,4},{6,5},{7,6},{8,15},{9,8},{10,9... | collective-permute-start | bytes 688136 | tf_op jit(solution)/shard_map/ppermute | solution.py:25
  55.3 0.0 collective-permute-done.3
  55.5 0.0 collective-permute-done.4.theirs_ref
  55.5 1.9 %collective-permute-start.5 = (bf16[32,3584]{1,0:T(8,128)(2,1)S(1)}, bf16[32,3584]{1,0:T(8,128)(2,1)S(1)}, u32[]{:S(2)}, u32[]{:S(2)}) collective-permute-start(bf16[32,3584]{1,0:T(8,128)(2,1)S(1)} %slice.78), channel_id=1, source_target_pairs={{0,1},{1,2},{2,3},{3,4},{4,5},{5,6},{6,7},{7,0},{8,9},{9,10},{10,1... | collective-permute-start | bytes 688136 | tf_op jit(solution)/shard_map/ppermute | solution.py:25
  57.7 3.9 %shard_map.103 = (bf16[256,3584]{1,0:T(8,128)(2,1)}, bf16[384,1792]{1,0:T(8,128)(2,1)S(1)}, bf16[384,1792]{1,0:T(8,128)(2,1)S(1)}) custom-call(s32[3]{0:T(128)S(1)} %pad_add_fusion.place_ref, bf16[224,3584]{1,0:T(8,128)(2,1)S(1)} %get-tuple-element.51.x_ref, bf16[224,3584]{1,0:T(8,128)(2,1)S(1)} %get-tuple-element.52.c_ref, ...), custom_call_target="tpu_custom_call" | custom-call | flops 4000000000 | bytes 16777216 | tf_op jit(solution)/shard_map/pallas_call | solution.py:276
  61.7 1.1 copy-done.6
  62.8 0.0 collective-permute-done.9.left_ref.left_any
  62.8 0.7 collective-permute-done.5.right_ref.right_any
  63.5 3.2 %shard_map.104 = (bf16[256,3584]{1,0:T(8,128)(2,1)}, bf16[96,1792]{1,0:T(8,128)(2,1)S(1)}, bf16[96,1792]{1,0:T(8,128)(2,1)S(1)}, bf16[224,1792]{1,0:T(8,128)(2,1)S(1)}) custom-call(s32[3]{0:T(128)S(1)} %pad_add_fusion.place_ref, bf16[32,3584]{1,0:T(8,128)(2,1)S(1)} %collective-permute-done.5.right_ref.right_any, ...), custom_call_target="tpu_custom_call", output_to_operand_aliasing={{0}: (6, {})} | custom-call | flops 2000000000 | bytes 8388608 | tf_op jit(solution)/shard_map/pallas_call | solution.py:285
  66.7 0.0 copy-done.2
  66.7 0.0 copy-done.4
  66.7 0.0 copy-start.8
  66.7 0.9 copy-done.8
  67.6 3.7 %collective-permute-start.10 = (bf16[96,1792]{1,0:T(8,128)(2,1)S(1)}, bf16[96,1792]{1,0:T(8,128)(2,1)S(1)}, u32[]{:S(2)}, u32[]{:S(2)}) collective-permute-start(bf16[96,1792]{1,0:T(8,128)(2,1)S(1)} %get-tuple-element.29), channel_id=1, source_target_pairs={{0,8},{1,9},{2,10},{3,11},{4,12},{5,13},{6,14},{7,15},{8,0},{9,1},... | collective-permute-start | bytes 1032200 | tf_op jit(solution)/shard_map/ppermute | solution.py:21
  71.3 0.0 copy-start.9
  71.3 6.3 %all-to-all-start = ((bf16[16,16,3584]{2,1,0:T(8,128)(2,1)}), bf16[16,16,3584]{2,1,0:T(8,128)(2,1)}, u32[]{:S(2)}, u32[]{:S(2)}) async-start(bf16[16,16,3584]{2,1,0:T(8,128)(2,1)} %bitcast.29), calls=%async_computation | async-start | bytes 3670016 | tf_op jit(solution)/shard_map/all_to_all | solution.py:414
  77.6 2.8 %collective-permute-start.13 = (bf16[96,1792]{1,0:T(8,128)(2,1)S(1)}, bf16[96,1792]{1,0:T(8,128)(2,1)S(1)}, u32[]{:S(2)}, u32[]{:S(2)}) collective-permute-start(bf16[96,1792]{1,0:T(8,128)(2,1)S(1)} %get-tuple-element.33), channel_id=1, source_target_pairs={{0,8},{1,9},{2,10},{3,11},{4,12},{5,13},{6,14},{7,15},{8,0},{9,1},... | collective-permute-start | bytes 1032200 | tf_op jit(solution)/shard_map/ppermute | solution.py:21
  80.4 0.0 collective-permute-done.10.b_ref
  80.4 0.0 copy-done.9
  80.4 0.0 copy-start.3
  80.4 0.0 copy-start.5
  80.4 0.0 copy-start.7
  80.4 0.1 shard_map.106
  80.5 17.3 %collective-permute-start.12 = (bf16[96,1792]{1,0:T(8,128)(2,1)S(1)}, bf16[96,1792]{1,0:T(8,128)(2,1)S(1)}, u32[]{:S(2)}, u32[]{:S(2)}) collective-permute-start(bf16[96,1792]{1,0:T(8,128)(2,1)S(1)} %shard_map.106), channel_id=1, source_target_pairs={{0,480},{32,448},{64,416},{96,384},{128,352},{160,320},{192,288},{... | collective-permute-start | bytes 1032200 | tf_op jit(solution)/shard_map/ppermute | solution.py:32
  97.8 0.0 copy-done.3
  97.8 0.0 copy-done.5
  97.8 1.9 %shard_map.107 = (bf16[192,1792]{1,0:T(8,128)(2,1)S(1)}, bf16[192,1792]{1,0:T(8,128)(2,1)S(1)}) custom-call(s32[3]{0:T(128)S(1)} %pad_add_fusion.place_ref, bf16[32,3584]{1,0:T(8,128)(2,1)S(1)} %copy-done.5, bf16[32,3584]{1,0:T(8,128)(2,1)S(1)} %copy-done.3, bf16[384,1792]{1,0:T(8,128)(2,1)S(1)} %copy-done.7, bf16[224,1792]{1,0:T(8,128)(2,1)S(1)} %copy-done.9), custom_call_target="tpu_custom_call" | custom-call | flops 1000000000 | bytes 8388608 | tf_op jit(solution)/shard_map/pallas_call | solution.py:252
  99.7 2.2 %collective-permute-start.11 = (bf16[192,1792]{1,0:T(8,128)(2,1)S(1)}, bf16[192,1792]{1,0:T(8,128)(2,1)S(1)}, u32[]{:S(2)}, u32[]{:S(2)}) collective-permute-start(bf16[192,1792]{1,0:T(8,128)(2,1)S(1)} %get-tuple-element.32), channel_id=1, source_target_pairs={{0,8},{1,9},{2,10},{3,11},{4,12},{5,13},{6,14},{7,15},{8,0},{9,1},... | collective-permute-start | bytes 2064392 | tf_op jit(solution)/shard_map/ppermute | solution.py:21
  102.0 0.0 collective-permute-done.13.b_ref
  102.0 0.1 shard_map.108
  102.1 0.0 copy-start
  102.1 4.3 %collective-permute-start.14 = (bf16[96,1792]{1,0:T(8,128)(2,1)S(1)}, bf16[96,1792]{1,0:T(8,128)(2,1)S(1)}, u32[]{:S(2)}, u32[]{:S(2)}) collective-permute-start(bf16[96,1792]{1,0:T(8,128)(2,1)S(1)} %shard_map.108), channel_id=1, source_target_pairs={{0,480},{32,448},{64,416},{96,384},{128,352},{160,320},{192,288},{... | collective-permute-start | bytes 1032200 | tf_op jit(solution)/shard_map/ppermute | solution.py:32
  106.4 11.6 %collective-permute-done.12 = bf16[96,1792]{1,0:T(8,128)(2,1)S(1)} collective-permute-done((bf16[96,1792]{1,0:T(8,128)(2,1)S(1)}, bf16[96,1792]{1,0:T(8,128)(2,1)S(1)}, u32[]{:S(2)}, u32[]{:S(2)}) %collective-permute-start.12) | collective-permute-done | bytes 344096 | tf_op jit(solution)/shard_map/ppermute | solution.py:32
  118.0 4.5 %collective-permute-done.14 = bf16[96,1792]{1,0:T(8,128)(2,1)S(1)} collective-permute-done((bf16[96,1792]{1,0:T(8,128)(2,1)S(1)}, bf16[96,1792]{1,0:T(8,128)(2,1)S(1)}, u32[]{:S(2)}, u32[]{:S(2)}) %collective-permute-start.14) | collective-permute-done | bytes 344096 | tf_op jit(solution)/shard_map/ppermute | solution.py:32
  122.5 0.0 collective-permute-done.11
  122.5 1.0 fusion.2
  123.6 0.0 all-to-all-done
  123.6 0.0 copy-done.1
  123.6 2.7 %shard_map.105 = bf16[128,3584]{1,0:T(8,128)(2,1)} custom-call(bf16[256,3584]{1,0:T(8,128)(2,1)} %bitcast.30.got_any, bf16[256,128]{1,0:T(8,128)(2,1)S(1)} %copy-done.1, bf16[128,3584]{1,0:T(8,128)(2,1)S(1)} %bitcast.39), custom_call_target="tpu_custom_call" | custom-call | flops 1000000000 | bytes 4194304 | tf_op jit(solution)/shard_map/pallas_call | solution.py:324
  (32 shorter events, 0.6 us)
Async XLA Ops:
  0.6 8.1 %copy-start.10 = (bf16[1,64,3584]{2,1,0:T(8,128)(2,1)S(1)}, bf16[1,64,3584]{2,1,0:T(8,128)(2,1)}, u32[]{:S(2)}) copy-start(bf16[1,64,3584]{2,1,0:T(8,128)(2,1)} %param.13) | copy-start | bytes 1376260
  0.6 8.1 %copy-start.11 = (bf16[1,64,3584]{2,1,0:T(8,128)(2,1)S(1)}, bf16[1,64,3584]{2,1,0:T(8,128)(2,1)}, u32[]{:S(2)}) copy-start(bf16[1,64,3584]{2,1,0:T(8,128)(2,1)} %param.12) | copy-start | bytes 1376260
  0.7 8.1 %copy-start.12 = (bf16[1,64,3584]{2,1,0:T(8,128)(2,1)S(1)}, bf16[1,64,3584]{2,1,0:T(8,128)(2,1)}, u32[]{:S(2)}) copy-start(bf16[1,64,3584]{2,1,0:T(8,128)(2,1)} %param.11) | copy-start | bytes 1376260
  3.3 7.4 %copy-start.13 = (bf16[32,3584]{1,0:T(8,128)(2,1)S(1)}, bf16[32,3584]{1,0:T(8,128)(2,1)}, u32[]{:S(2)}) copy-start(bf16[32,3584]{1,0:T(8,128)(2,1)} %get-tuple-element.19) | copy-start | bytes 688132
  3.3 9.0 %collective-permute-start = (bf16[32,3584]{1,0:T(8,128)(2,1)}, bf16[32,3584]{1,0:T(8,128)(2,1)S(1)}, u32[]{:S(2)}, u32[]{:S(2)}) collective-permute-start(bf16[32,3584]{1,0:T(8,128)(2,1)} %get-tuple-element.20), channel_id=1, source_target_pairs={{0,24},{1,25},{2,26},{3,27},{4,28},{5,29},{6,30},{7,31},{8,16},{9,... | collective-permute-start | bytes 688136 | tf_op jit(solution)/shard_map/ppermute | solution.py:17
  8.8 46.7 %collective-permute-start.4 = (bf16[192,3584]{1,0:T(8,128)(2,1)S(1)}, bf16[192,3584]{1,0:T(8,128)(2,1)S(1)}, u32[]{:S(2)}, u32[]{:S(2)}) collective-permute-start(bf16[192,3584]{1,0:T(8,128)(2,1)S(1)} %pad_maximum_fusion.mine_ref), channel_id=1, source_target_pairs={{0,8},{1,9},{2,10},{3,11},{4,12},{5,13},{6,14},{7,15},{8,0},{9,1},... | collective-permute-start | bytes 4128776 | tf_op jit(solution)/shard_map/ppermute | solution.py:21
  12.3 14.5 %collective-permute-start.6 = (bf16[64,3584]{1,0:T(8,128)(2,1)S(1)}, bf16[64,3584]{1,0:T(8,128)(2,1)S(1)}, u32[]{:S(2)}, u32[]{:S(2)}) collective-permute-start(bf16[64,3584]{1,0:T(8,128)(2,1)S(1)} %constant_dynamic-update-slice_fusion), channel_id=1, source_target_pairs={{0,7},{1,0},{2,1},{3,2},{4,3},{5,4},{6,5},{7,6},{8,15},{9,8},{10,9... | collective-permute-start | bytes 1376264 | tf_op jit(solution)/shard_map/ppermute | solution.py:25
  19.2 13.0 %collective-permute-start.1 = (bf16[64,3584]{1,0:T(8,128)(2,1)S(1)}, bf16[64,3584]{1,0:T(8,128)(2,1)S(1)}, u32[]{:S(2)}, u32[]{:S(2)}) collective-permute-start(bf16[64,3584]{1,0:T(8,128)(2,1)S(1)} %constant_dynamic-update-slice_fusion), channel_id=1, source_target_pairs={{0,1},{1,2},{2,3},{3,4},{4,5},{5,6},{6,7},{7,0},{8,9},{9,10},{10,1... | collective-permute-start | bytes 1376264 | tf_op jit(solution)/shard_map/ppermute | solution.py:25
  26.9 12.0 %collective-permute-start.7 = (bf16[64,3584]{1,0:T(8,128)(2,1)S(1)}, bf16[64,3584]{1,0:T(8,128)(2,1)S(1)}, u32[]{:S(2)}, u32[]{:S(2)}) collective-permute-start(bf16[64,3584]{1,0:T(8,128)(2,1)S(1)} %collective-permute-done.6), channel_id=1, source_target_pairs={{0,7},{1,0},{2,1},{3,2},{4,3},{5,4},{6,5},{7,6},{8,15},{9,8},{10,9... | collective-permute-start | bytes 1376264 | tf_op jit(solution)/shard_map/ppermute | solution.py:25
  32.2 12.0 %collective-permute-start.2 = (bf16[64,3584]{1,0:T(8,128)(2,1)S(1)}, bf16[64,3584]{1,0:T(8,128)(2,1)S(1)}, u32[]{:S(2)}, u32[]{:S(2)}) collective-permute-start(bf16[64,3584]{1,0:T(8,128)(2,1)S(1)} %collective-permute-done.1), channel_id=1, source_target_pairs={{0,1},{1,2},{2,3},{3,4},{4,5},{5,6},{6,7},{7,0},{8,9},{9,10},{10,1... | collective-permute-start | bytes 1376264 | tf_op jit(solution)/shard_map/ppermute | solution.py:25
  38.9 11.1 %collective-permute-start.8 = (bf16[64,3584]{1,0:T(8,128)(2,1)S(1)}, bf16[64,3584]{1,0:T(8,128)(2,1)S(1)}, u32[]{:S(2)}, u32[]{:S(2)}) collective-permute-start(bf16[64,3584]{1,0:T(8,128)(2,1)S(1)} %collective-permute-done.7), channel_id=1, source_target_pairs={{0,7},{1,0},{2,1},{3,2},{4,3},{5,4},{6,5},{7,6},{8,15},{9,8},{10,9... | collective-permute-start | bytes 1376264 | tf_op jit(solution)/shard_map/ppermute | solution.py:25
  44.2 11.1 %collective-permute-start.3 = (bf16[64,3584]{1,0:T(8,128)(2,1)S(1)}, bf16[64,3584]{1,0:T(8,128)(2,1)S(1)}, u32[]{:S(2)}, u32[]{:S(2)}) collective-permute-start(bf16[64,3584]{1,0:T(8,128)(2,1)S(1)} %collective-permute-done.2), channel_id=1, source_target_pairs={{0,1},{1,2},{2,3},{3,4},{4,5},{5,6},{6,7},{7,0},{8,9},{9,10},{10,1... | collective-permute-start | bytes 1376264 | tf_op jit(solution)/shard_map/ppermute | solution.py:25
  50.0 12.8 %collective-permute-start.9 = (bf16[32,3584]{1,0:T(8,128)(2,1)S(1)}, bf16[32,3584]{1,0:T(8,128)(2,1)S(1)}, u32[]{:S(2)}, u32[]{:S(2)}) collective-permute-start(bf16[32,3584]{1,0:T(8,128)(2,1)S(1)} %slice.104), channel_id=1, source_target_pairs={{0,7},{1,0},{2,1},{3,2},{4,3},{5,4},{6,5},{7,6},{8,15},{9,8},{10,9... | collective-permute-start | bytes 688136 | tf_op jit(solution)/shard_map/ppermute | solution.py:25
  55.5 8.0 %collective-permute-start.5 = (bf16[32,3584]{1,0:T(8,128)(2,1)S(1)}, bf16[32,3584]{1,0:T(8,128)(2,1)S(1)}, u32[]{:S(2)}, u32[]{:S(2)}) collective-permute-start(bf16[32,3584]{1,0:T(8,128)(2,1)S(1)} %slice.78), channel_id=1, source_target_pairs={{0,1},{1,2},{2,3},{3,4},{4,5},{5,6},{6,7},{7,0},{8,9},{9,10},{10,1... | collective-permute-start | bytes 688136 | tf_op jit(solution)/shard_map/ppermute | solution.py:25
  61.7 1.1 copy-start.6
  62.8 3.9 %copy-start.2 = (bf16[32,3584]{1,0:T(8,128)(2,1)}, bf16[32,3584]{1,0:T(8,128)(2,1)S(1)}, u32[]{:S(2)}) copy-start(bf16[32,3584]{1,0:T(8,128)(2,1)S(1)} %collective-permute-done.9.left_ref.left_any) | copy-start | bytes 688132
  63.5 3.2 %copy-start.4 = (bf16[32,3584]{1,0:T(8,128)(2,1)}, bf16[32,3584]{1,0:T(8,128)(2,1)S(1)}, u32[]{:S(2)}) copy-start(bf16[32,3584]{1,0:T(8,128)(2,1)S(1)} %collective-permute-done.5.right_ref.right_any) | copy-start | bytes 688132
  66.7 0.9 copy-start.8
  67.6 12.8 %collective-permute-start.10 = (bf16[96,1792]{1,0:T(8,128)(2,1)S(1)}, bf16[96,1792]{1,0:T(8,128)(2,1)S(1)}, u32[]{:S(2)}, u32[]{:S(2)}) collective-permute-start(bf16[96,1792]{1,0:T(8,128)(2,1)S(1)} %get-tuple-element.29), channel_id=1, source_target_pairs={{0,8},{1,9},{2,10},{3,11},{4,12},{5,13},{6,14},{7,15},{8,0},{9,1},... | collective-permute-start | bytes 1032200 | tf_op jit(solution)/shard_map/ppermute | solution.py:21
  71.3 9.1 %copy-start.9 = (bf16[224,1792]{1,0:T(8,128)(2,1)S(1)}, bf16[224,1792]{1,0:T(8,128)(2,1)}, u32[]{:S(2)}) copy-start(bf16[224,1792]{1,0:T(8,128)(2,1)} %copy-done.8) | copy-start | bytes 2408452
  71.3 52.3 %all-to-all-start = ((bf16[16,16,3584]{2,1,0:T(8,128)(2,1)}), bf16[16,16,3584]{2,1,0:T(8,128)(2,1)}, u32[]{:S(2)}, u32[]{:S(2)}) async-start(bf16[16,16,3584]{2,1,0:T(8,128)(2,1)} %bitcast.29), calls=%async_computation | async-start | bytes 3670016 | tf_op jit(solution)/shard_map/all_to_all | solution.py:414
  77.6 24.4 %collective-permute-start.13 = (bf16[96,1792]{1,0:T(8,128)(2,1)S(1)}, bf16[96,1792]{1,0:T(8,128)(2,1)S(1)}, u32[]{:S(2)}, u32[]{:S(2)}) collective-permute-start(bf16[96,1792]{1,0:T(8,128)(2,1)S(1)} %get-tuple-element.33), channel_id=1, source_target_pairs={{0,8},{1,9},{2,10},{3,11},{4,12},{5,13},{6,14},{7,15},{8,0},{9,1},... | collective-permute-start | bytes 1032200 | tf_op jit(solution)/shard_map/ppermute | solution.py:21
  80.4 17.4 %copy-start.3 = (bf16[32,3584]{1,0:T(8,128)(2,1)S(1)}, bf16[32,3584]{1,0:T(8,128)(2,1)}, u32[]{:S(2)}) copy-start(bf16[32,3584]{1,0:T(8,128)(2,1)} %copy-done.2) | copy-start | bytes 688132
  80.4 17.4 %copy-start.5 = (bf16[32,3584]{1,0:T(8,128)(2,1)S(1)}, bf16[32,3584]{1,0:T(8,128)(2,1)}, u32[]{:S(2)}) copy-start(bf16[32,3584]{1,0:T(8,128)(2,1)} %copy-done.4) | copy-start | bytes 688132
  80.4 17.4 %copy-start.7 = (bf16[384,1792]{1,0:T(8,128)(2,1)S(1)}, bf16[384,1792]{1,0:T(8,128)(2,1)}, u32[]{:S(2)}) copy-start(bf16[384,1792]{1,0:T(8,128)(2,1)} %copy-done.6) | copy-start | bytes 4128772
  80.5 37.5 %collective-permute-start.12 = (bf16[96,1792]{1,0:T(8,128)(2,1)S(1)}, bf16[96,1792]{1,0:T(8,128)(2,1)S(1)}, u32[]{:S(2)}, u32[]{:S(2)}) collective-permute-start(bf16[96,1792]{1,0:T(8,128)(2,1)S(1)} %shard_map.106), channel_id=1, source_target_pairs={{0,480},{32,448},{64,416},{96,384},{128,352},{160,320},{192,288},{... | collective-permute-start | bytes 1032200 | tf_op jit(solution)/shard_map/ppermute | solution.py:32
  99.7 22.8 %collective-permute-start.11 = (bf16[192,1792]{1,0:T(8,128)(2,1)S(1)}, bf16[192,1792]{1,0:T(8,128)(2,1)S(1)}, u32[]{:S(2)}, u32[]{:S(2)}) collective-permute-start(bf16[192,1792]{1,0:T(8,128)(2,1)S(1)} %get-tuple-element.32), channel_id=1, source_target_pairs={{0,8},{1,9},{2,10},{3,11},{4,12},{5,13},{6,14},{7,15},{8,0},{9,1},... | collective-permute-start | bytes 2064392 | tf_op jit(solution)/shard_map/ppermute | solution.py:21
  102.1 21.5 %copy-start = (bf16[1,128,3584]{2,1,0:T(8,128)(2,1)S(1)}, bf16[1,128,3584]{2,1,0:T(8,128)(2,1)}, u32[]{:S(2)}) copy-start(bf16[1,128,3584]{2,1,0:T(8,128)(2,1)} %param.8) | copy-start | bytes 2752516
  102.1 21.5 %copy-start.1 = (bf16[256,128]{1,0:T(8,128)(2,1)S(1)}, bf16[256,128]{1,0:T(8,128)(2,1)}, u32[]{:S(2)}) copy-start(bf16[256,128]{1,0:T(8,128)(2,1)} %get-tuple-element.26.select_ref) | copy-start | bytes 196612
  102.1 20.4 %collective-permute-start.14 = (bf16[96,1792]{1,0:T(8,128)(2,1)S(1)}, bf16[96,1792]{1,0:T(8,128)(2,1)S(1)}, u32[]{:S(2)}, u32[]{:S(2)}) collective-permute-start(bf16[96,1792]{1,0:T(8,128)(2,1)S(1)} %shard_map.108), channel_id=1, source_target_pairs={{0,480},{32,448},{64,416},{96,384},{128,352},{160,320},{192,288},{... | collective-permute-start | bytes 1032200 | tf_op jit(solution)/shard_map/ppermute | solution.py:32
